TPU v7x, 128 devices: a whole 4x4x4 slice. The times are simulated.
128 devices in a mesh: wide: 16 (over z, y_hi, core), narrow: 8 (over x, y_lo).
Axes of the slice: x: 4, y: 4 (y_hi: 2, y_lo: 2; y = y_hi * 2 + y_lo), z: 4, core: 2. Of those that a mesh axis runs over, the one named last changes fastest.
Arguments:
- layer_input: bfloat16 [8192, 2560], P('wide', 'narrow'), may hold values from -6 to 6
- gain_attn: float32 [2560], P('narrow'), may hold values from 0.1 to 1.9
- w_query: bfloat16 [2560, 2560], P('wide', 'narrow'), may hold values from -0.125 to 0.125
- w_key: bfloat16 [2560, 640], P('wide', 'narrow'), may hold values from -0.125 to 0.125
- w_value: bfloat16 [2560, 640], P('wide', 'narrow'), may hold values from -0.125 to 0.125
- w_out: bfloat16 [2560, 2560], P('narrow', 'wide'), may hold values from -1.5 to 1.5
- gain_mlp: float32 [2560], P('narrow'), may hold values from 0.1 to 1.9
- w_gate: bfloat16 [2560, 7168], P('wide', 'narrow'), may hold values from -0.125 to 0.125
- w_up: bfloat16 [2560, 7168], P('wide', 'narrow'), may hold values from -0.125 to 0.125
- w_down: bfloat16 [7168, 2560], P('narrow', 'wide'), may hold values from -0.0625 to 0.0625
- doc_lengths: int32 [8], replicated, may hold values from 1 to 7968, as said below
- cotangent: bfloat16 [8192, 2560], P('wide', 'narrow'), may hold values from -6 to 6
Outputs:
- layer_output: bfloat16 [8192, 2560], P('wide', 'narrow')
- grad_input: float32 [8192, 2560], P('wide', 'narrow')
- grad_gain_attn: float32 [2560], P('narrow')
- grad_query: float32 [2560, 2560], P('wide', 'narrow')
- grad_key: float32 [2560, 640], P('wide', 'narrow')
- grad_value: float32 [2560, 640], P('wide', 'narrow')
- grad_out: float32 [2560, 2560], P('narrow', 'wide')
- grad_gain_mlp: float32 [2560], P('narrow')
- grad_gate: float32 [2560, 7168], P('wide', 'narrow')
- grad_up: float32 [2560, 7168], P('wide', 'narrow')
- grad_down: float32 [7168, 2560], P('narrow', 'wide')
Inputs may be any that keep to these rules, and one draw needn't show every extreme that they name: `doc_lengths`: the 8 lengths sum to 8192. One document, at a place drawn from the seed, has exactly 7968 tokens; the others together have (7) * 32 tokens, each between 1 and 63, and one of them exactly 1.
All inputs are finite; a program needn't handle non-finite values.
Results may differ from a plain program's by a relative error of at most 0.019.
Values may be sent and summed in bfloat16 or wider, within the bound.
A program may use at most 192 MiB of HBM per device.

v0:
```python
import math

import jax
import jax.numpy as jnp
from jax import lax
from jax.sharding import Mesh
from jax.sharding import PartitionSpec as P

D = 2560
HEADS = 32
KV_HEADS = 8
HEAD = 80
WINDOW = 1024
NARROW = ("narrow_0", "narrow_1")


epsilon = 1e-05
rope_base = 1000000.0
rope_factor = 8.0
long_wave = 8192.0
short_wave = 2048.0
masked = -1e30


def in_order(pieces, dim):
    pieces = jnp.moveaxis(pieces, 0, dim)
    lengths = pieces.shape
    return pieces.reshape(*lengths[:dim], lengths[dim] * lengths[dim + 1], *lengths[dim + 2 :])


def from_everyone(x, axis):
    length = lax.axis_size(axis)
    return lax.all_to_all(jnp.broadcast_to(x[None], (length, *x.shape)), axis, 0, 0, tiled=True)


def gathered_copies(x, axis, dim):
    return in_order(from_everyone(x, axis), dim)


def summed_rows(x, axes, dim):
    for axis in axes:
        x = lax.psum_scatter(x, axis, scatter_dimension=dim, tiled=True)
    return x


def taken_together(x, axis):
    return from_everyone(x, axis).sum(axis=0)


def rows_first(arrays, axis, dims):
    turned = [jnp.moveaxis(a, dim, 0) for a, dim in zip(arrays, dims)]
    both = jnp.concatenate([t.reshape(len(t), -1) for t in turned], axis=1)
    result, at, finished = (lax.all_gather(both, axis, axis=0, tiled=True), 0, [])
    for t, dim in zip(turned, dims):
        section = result[:, at : at + t[0].size].reshape(-1, *t.shape[1:])
        finished.append(jnp.moveaxis(section, 0, dim))
        at += t[0].size
    return tuple(finished)


def from_behind(value, axis, steps):
    count = lax.axis_size(axis)
    initial, last = (max(0, -steps), min(count, count - steps))
    return lax.ppermute(value, axis, [(source, source + steps) for source in range(initial, last)])


def sent_together(arrays, axis, dim, along):
    ends, at = ([], 0)
    for a in arrays[:-1]:
        at += a.shape[along]
        ends.append(at)
    both = jnp.concatenate(arrays, axis=along)
    return tuple(
        jnp.split(lax.psum_scatter(both, axis, scatter_dimension=dim, tiled=True), ends, axis=along)
    )


def in_one(arrays, axis):
    ends = [0]
    for a in arrays:
        ends.append(ends[-1] + a.size)
    running = taken_together(jnp.concatenate([a.ravel() for a in arrays]), axis)
    return tuple((running[b:e].reshape(a.shape) for a, b, e in zip(arrays, ends, ends[1:])))


def documents(doc_lengths, places):
    ends_at = jnp.cumsum(doc_lengths)
    passed = places[:, None] >= ends_at[None, :]
    segment = jnp.sum(passed.astype(jnp.int32), axis=1)
    begins = jnp.sum(jnp.where(passed, doc_lengths[None, :], 0), axis=1)
    return (segment, places - begins)


def scaled_freqs():
    half_width = HEAD // 2
    freqs = rope_base ** (-2.0 * jnp.arange(half_width, dtype=jnp.float32) / HEAD)
    wavelen = 2.0 * math.pi / freqs
    smooth = (long_wave / wavelen - 1.0) / 3.0
    blended = (1.0 - smooth) * freqs / rope_factor + smooth * freqs
    return jnp.where(
        wavelen < short_wave, freqs, jnp.where(wavelen > long_wave, freqs / rope_factor, blended)
    )


def rope_tables(position):
    freqs = scaled_freqs()
    angles = position.astype(jnp.float32)[:, None] * freqs[None, :]
    return (jnp.cos(angles), jnp.sin(angles))


def rotate(stacked, cosine, sine_table):
    half_width = stacked.shape[-1] // 2
    front_half = stacked[..., :half_width]
    back_half = stacked[..., half_width:]
    cos_rows = cosine[:, None, :]
    sin_rows = sine_table[:, None, :]
    return jnp.concatenate(
        [
            front_half * cos_rows - back_half * sin_rows,
            back_half * cos_rows + front_half * sin_rows,
        ],
        axis=-1,
    )


def unrotate(stacked, cosine, sine_table):
    half_width = stacked.shape[-1] // 2
    front_half = stacked[..., :half_width]
    back_half = stacked[..., half_width:]
    cos_rows = cosine[:, None, :]
    sin_rows = sine_table[:, None, :]
    return jnp.concatenate(
        [
            front_half * cos_rows + back_half * sin_rows,
            back_half * cos_rows - front_half * sin_rows,
        ],
        axis=-1,
    )


def features(pieces):
    return gathered_copies(pieces, NARROW, 1)


def columns(partial_value):
    return summed_rows(partial_value, NARROW, 1)


def row_total(entries):
    return taken_together(entries, NARROW)


def norm_rows(stream, gain):
    inverse_rms = lax.rsqrt(row_total(jnp.sum(stream * stream, axis=1)) / D + epsilon)
    return (stream * inverse_rms[:, None] * gain[None, :], inverse_rms)


def norm_back(stream, inverse_rms, gain, upstream):
    weighted = upstream * gain[None, :]
    inner = row_total(jnp.sum(weighted * stream, axis=1))
    through = (
        inverse_rms[:, None] * weighted
        - stream * (inverse_rms * inverse_rms * inverse_rms * inner / D)[:, None]
    )
    return (through, jnp.sum(upstream * stream * inverse_rms[:, None], axis=0))


def scores_of(queries, keys_here, visible):
    raw_scores = jnp.einsum(
        "tkgd,skd->kgts", queries, keys_here, preferred_element_type=jnp.float32
    ) * (1.0 / math.sqrt(HEAD))
    return jnp.where(visible[None, None], raw_scores, masked)


def attend(queries, keys_here, values_here, visible):
    scores = scores_of(queries, keys_here, visible)
    largest = jnp.max(scores, axis=-1, keepdims=True)
    powers = jnp.exp(scores - largest)
    totals = jnp.sum(powers, axis=-1, keepdims=True)
    weights = (powers / totals).astype(jnp.bfloat16)
    mixed = jnp.einsum("kgts,skd->tkgd", weights, values_here, preferred_element_type=jnp.float32)
    return (mixed, largest + jnp.log(totals))


def attend_back(queries, keys_here, values_here, visible, log_totals, upstream):
    weights = jnp.exp(scores_of(queries, keys_here, visible) - log_totals)
    upstream_prob = jnp.einsum(
        "tkgd,skd->kgts", upstream, values_here, preferred_element_type=jnp.float32
    )
    grad_scores = (
        weights * (upstream_prob - jnp.sum(weights * upstream_prob, axis=-1, keepdims=True))
    ).astype(jnp.bfloat16)
    factor = 1.0 / math.sqrt(HEAD)
    grad_queries = (
        jnp.einsum("kgts,skd->tkgd", grad_scores, keys_here, preferred_element_type=jnp.float32)
        * factor
    )
    grad_keys = (
        jnp.einsum("kgts,tkgd->skd", grad_scores, queries, preferred_element_type=jnp.float32)
        * factor
    )
    grad_values = jnp.einsum(
        "kgts,tkgd->skd", weights.astype(jnp.bfloat16), upstream, preferred_element_type=jnp.float32
    )
    return (grad_queries, grad_keys, grad_values)


def body(
    layer_input,
    gain_attn,
    w_query,
    w_key,
    w_value,
    w_out,
    gain_mlp,
    w_gate,
    w_up,
    w_down,
    doc_lengths,
    cotangent,
):
    tok_rows = layer_input.shape[0]
    query_width = w_query.shape[1]
    kv_width = w_key.shape[1]
    ff_width = w_gate.shape[1]
    kv_local = kv_width // HEAD
    per_group = HEADS // KV_HEADS
    w_kv = jnp.concatenate([w_key, w_value], axis=1)
    w_gu = jnp.concatenate([w_gate, w_up], axis=1)
    full_query, full_kv, full_out, full_gu, full_down = rows_first(
        (w_query, w_kv, w_out, w_gu, w_down), "wide", (0, 0, 1, 0, 1)
    )
    query_index = lax.axis_index("wide") * tok_rows + jnp.arange(tok_rows, dtype=jnp.int32)
    query_seg, query_pos = documents(doc_lengths, query_index)
    cosine, sine_table = rope_tables(query_pos)
    stream = layer_input.astype(jnp.float32)
    normed_one, inverse_one = norm_rows(stream, gain_attn)
    normed_full = features(normed_one.astype(jnp.bfloat16))
    query_raw = jnp.dot(normed_full, full_query, preferred_element_type=jnp.float32)
    kv_raw = jnp.dot(normed_full, full_kv, preferred_element_type=jnp.float32)
    queries = rotate(query_raw.reshape(tok_rows, -1, HEAD), cosine, sine_table).astype(jnp.bfloat16)
    keys_mine = rotate(kv_raw[:, :kv_width].reshape(tok_rows, kv_local, HEAD), cosine, sine_table)
    kv_mine = jnp.concatenate(
        [keys_mine.reshape(tok_rows, kv_width), kv_raw[:, kv_width:]], axis=1
    ).astype(jnp.bfloat16)
    reach = WINDOW // tok_rows
    near_blocks = []
    for offset in range(reach, 0, -1):
        near_blocks.append(from_behind(kv_mine, "wide", offset))
    kv_seen = jnp.concatenate(near_blocks + [kv_mine], axis=0)
    blocks_seen = reach + 1
    key_start = (lax.axis_index("wide") - (blocks_seen - 1)) * tok_rows
    seen_rows = kv_seen.shape[0]
    key_index = key_start + jnp.arange(seen_rows, dtype=jnp.int32)
    key_seg = documents(doc_lengths, key_index)[0]
    visible = (
        (query_seg[:, None] == key_seg[None, :])
        & (key_index[None, :] <= query_index[:, None])
        & (query_index[:, None] - key_index[None, :] < WINDOW)
        & (key_index[None, :] >= 0)
    )
    keys_here = kv_seen[:, :kv_width].reshape(seen_rows, kv_local, HEAD)
    values_here = kv_seen[:, kv_width:].reshape(seen_rows, kv_local, HEAD)
    grouped = queries.reshape(tok_rows, kv_local, per_group, HEAD)
    mixed, log_totals = attend(grouped, keys_here, values_here, visible)
    attended = mixed.reshape(tok_rows, query_width).astype(jnp.bfloat16)
    midstream = stream + columns(jnp.dot(attended, full_out, preferred_element_type=jnp.float32))
    normed_two, inverse_two = norm_rows(midstream, gain_mlp)
    normed_wide = features(normed_two.astype(jnp.bfloat16))
    gate_up = jnp.dot(normed_wide, full_gu, preferred_element_type=jnp.float32)
    gate_val = gate_up[:, :ff_width]
    up_val = gate_up[:, ff_width:]
    sigmoid_gate = jax.nn.sigmoid(gate_val)
    activated = gate_val * sigmoid_gate
    hidden_act = (activated * up_val).astype(jnp.bfloat16)
    layer_output = (
        midstream + columns(jnp.dot(hidden_act, full_down, preferred_element_type=jnp.float32))
    ).astype(jnp.bfloat16)
    upstream_full = features(cotangent)
    grad_down_full = jnp.einsum(
        "tf,td->fd", hidden_act, upstream_full, preferred_element_type=jnp.float32
    )
    grad_hidden = jnp.einsum(
        "td,fd->tf", upstream_full, full_down, preferred_element_type=jnp.float32
    )
    grad_gate_pre = grad_hidden * up_val * sigmoid_gate * (1.0 + gate_val * (1.0 - sigmoid_gate))
    grad_up_pre = grad_hidden * activated
    grad_gu = jnp.concatenate([grad_gate_pre, grad_up_pre], axis=1).astype(jnp.bfloat16)
    grad_gu_full = jnp.einsum("td,tf->df", normed_wide, grad_gu, preferred_element_type=jnp.float32)
    grad_normed_two = columns(
        jnp.einsum("tf,df->td", grad_gu, full_gu, preferred_element_type=jnp.float32)
    )
    through_two, gain_two_part = norm_back(midstream, inverse_two, gain_mlp, grad_normed_two)
    grad_mid = cotangent.astype(jnp.float32) + through_two
    grad_mid_full = features(grad_mid.astype(jnp.bfloat16))
    grad_out_full = jnp.einsum(
        "tq,td->qd", attended, grad_mid_full, preferred_element_type=jnp.float32
    )
    grad_attended = jnp.einsum(
        "td,qd->tq", grad_mid_full, full_out, preferred_element_type=jnp.float32
    ).astype(jnp.bfloat16)
    grad_grouped, grad_keys, grad_values = attend_back(
        grouped,
        keys_here,
        values_here,
        visible,
        log_totals,
        grad_attended.reshape(tok_rows, kv_local, per_group, HEAD),
    )
    grad_seen = jnp.concatenate(
        [grad_keys.reshape(seen_rows, kv_width), grad_values.reshape(seen_rows, kv_width)], axis=1
    )
    grad_kv_mine = grad_seen[reach * tok_rows :]
    for offset in range(1, reach + 1):
        block_at = (reach - offset) * tok_rows
        grad_kv_mine = grad_kv_mine + from_behind(
            grad_seen[block_at : block_at + tok_rows].astype(jnp.bfloat16), "wide", -offset
        ).astype(jnp.float32)
    grad_query_raw = (
        unrotate(grad_grouped.reshape(tok_rows, -1, HEAD), cosine, sine_table)
        .reshape(tok_rows, query_width)
        .astype(jnp.bfloat16)
    )
    grad_key_raw = unrotate(
        grad_kv_mine[:, :kv_width].reshape(tok_rows, kv_local, HEAD), cosine, sine_table
    ).reshape(tok_rows, kv_width)
    grad_kv_raw = jnp.concatenate([grad_key_raw, grad_kv_mine[:, kv_width:]], axis=1).astype(
        jnp.bfloat16
    )
    grad_query_full = jnp.einsum(
        "td,tq->dq", normed_full, grad_query_raw, preferred_element_type=jnp.float32
    )
    grad_kv_full = jnp.einsum(
        "td,tk->dk", normed_full, grad_kv_raw, preferred_element_type=jnp.float32
    )
    grad_normed_one = columns(
        jnp.einsum("tq,dq->td", grad_query_raw, full_query, preferred_element_type=jnp.float32)
        + jnp.einsum("tk,dk->td", grad_kv_raw, full_kv, preferred_element_type=jnp.float32)
    )
    through_one, gain_one_part = norm_back(stream, inverse_one, gain_attn, grad_normed_one)
    grad_input = grad_mid + through_one
    grad_query, grad_kv, grad_out, grad_gu_rows, grad_down = (
        *tuple(
            (
                part.astype(jnp.float32)
                for part in sent_together(
                    (grad_query_full.astype(jnp.bfloat16), grad_kv_full.astype(jnp.bfloat16)),
                    "wide",
                    0,
                    1,
                )
            )
        ),
        lax.psum_scatter(
            grad_out_full.astype(jnp.bfloat16), "wide", scatter_dimension=1, tiled=True
        ).astype(jnp.float32),
        lax.psum_scatter(
            grad_gu_full.astype(jnp.bfloat16), "wide", scatter_dimension=0, tiled=True
        ).astype(jnp.float32),
        lax.psum_scatter(
            grad_down_full.astype(jnp.bfloat16), "wide", scatter_dimension=1, tiled=True
        ).astype(jnp.float32),
    )
    grad_gain_attn, grad_gain_mlp = in_one((gain_one_part, gain_two_part), "wide")
    return (
        layer_output,
        grad_input,
        grad_gain_attn,
        grad_query,
        grad_kv[:, :kv_width],
        grad_kv[:, kv_width:],
        grad_out,
        grad_gain_mlp,
        grad_gu_rows[:, :ff_width],
        grad_gu_rows[:, ff_width:],
        grad_down,
    )


def solution(mesh):
    torus = Mesh(mesh.devices.reshape(mesh.shape["wide"], 4, 2), ("wide", "narrow_0", "narrow_1"))
    return jax.shard_map(
        body,
        mesh=torus,
        in_specs=(
            P("wide", NARROW),
            P(NARROW),
            P("wide", NARROW),
            P("wide", NARROW),
            P("wide", NARROW),
            P(NARROW, "wide"),
            P(NARROW),
            P("wide", NARROW),
            P("wide", NARROW),
            P(NARROW, "wide"),
            P(),
            P("wide", NARROW),
        ),
        out_specs=(
            P("wide", NARROW),
            P("wide", NARROW),
            P(NARROW),
            P("wide", NARROW),
            P("wide", NARROW),
            P("wide", NARROW),
            P(NARROW, "wide"),
            P(NARROW),
            P("wide", NARROW),
            P("wide", NARROW),
            P(NARROW, "wide"),
        ),
        check_vma=False,
    )
```

profile of v0, /device:TPU:1, one launch (start us, length us, event | category | flops | bytes accessed | tf_op | source)
XLA Modules:
  0.0 1108.0 jit_solution(13786666360352068154)
XLA Ops:
  7.2 3.7 concatenate.45
  11.4 10.7 all_to_all.50
  25.3 3.6 all-to-all-start.1
  29.9 2.5 fusion.21
  32.4 33.7 %all-to-all-done.1 = bf16[8,512,320]{1,2,0:T(8,128)(2,1)S(1)} async-done(((bf16[8,512,320]{1,2,0:T(8,128)(2,1)}), bf16[8,512,320]{1,2,0:T(8,128)(2,1)S(1)}, u32[]{:S(2)}, u32[]{:S(2)}) %all-to-all-start.1) | async-done | bytes 2621472 | tf_op jit(solution)/shard_map/all_to_all | solution.py:33
  66.1 93.2 %all-gather.2.cloned.1.call-done = bf16[2560,3488]{1,0:T(8,128)(2,1)} async-done(((bf16[160,3488]{1,0:T(8,128)(2,1)}), bf16[2560,3488]{1,0:T(8,128)(2,1)}) %all-gather.2.cloned.1.call-update) | async-done | bytes 17858576 | tf_op jit(solution)/shard_map/all_gather | solution.py:53
  159.3 2.9 fusion.46
  162.7 2.3 collective-permute-start.1
  165.0 4.9 collective-permute-start
  169.9 3.0 slice_bitcast_fusion
  172.9 3.9 copy.91
  176.9 2.5 fusion.95
  181.4 2.4 fusion.94
  185.5 3.0 copy-done
  188.5 2.4 fusion.41
  191.6 6.0 fusion.34
  197.7 52.8 %reduce-scatter.23.cloned.1.call-done = f32[512,640]{1,0:T(8,128)} async-done(((f32[512,2560]{1,0:T(8,128)}), f32[512,640]{1,0:T(8,128)}) %reduce-scatter.23.cloned.1.call-update) | async-done | bytes 1310736 | tf_op jit(solution)/shard_map/reduce_scatter | solution.py:42
  250.5 2.8 copy.117
  253.3 25.6 %reduce-scatter.37.cloned.1.call-done = f32[320,512]{1,0:T(8,128)} async-done(((f32[640,512]{1,0:T(8,128)}), f32[320,512]{1,0:T(8,128)}) %reduce-scatter.37.cloned.1.call-update) | async-done | bytes 655376
  278.9 2.3 copy.118
  282.6 8.8 all_to_all.51
  295.5 32.8 %all_to_all.52 = bf16[8,512,320]{1,2,0:T(8,128)(2,1)} all-to-all(bf16[8,512,320]{1,2,0:T(8,128)(2,1)S(1)} %broadcast_in_dim.53), channel_id=1, replica_groups=mesh['wide'=16,'narrow_0'=4,'narrow_1'=2] {'narrow_0','narrow_1'}, dimensions={0} | all-to-all | bytes 5242880 | tf_op jit(solution)/shard_map/all_to_all | solution.py:33
  330.1 4.4 all-to-all-start.4
  334.8 11.9 %fusion.7 = f32[512,1792]{1,0:T(8,128)} fusion(bf16[512,2560]{0,1:T(8,128)(2,1)} %bitcast.153, bf16[2560,3488]{1,0:T(8,128)(2,1)} %all-gather.2.cloned.1.call-done), kind=kOutput, calls=%fused_computation.14 | convolution fusion | flops 4697620480 | bytes 15466496 | tf_op jit(solution)/shard_map/dot_general | solution.py:270
  346.7 23.0 %all-to-all-done.4 = bf16[8,512,320]{1,2,0:T(8,128)(2,1)} async-done(((bf16[8,512,320]{1,2,0:T(8,128)(2,1)}), bf16[8,512,320]{1,2,0:T(8,128)(2,1)}, u32[]{:S(2)}, u32[]{:S(2)}) %all-to-all-start.4) | async-done | bytes 2621472 | tf_op jit(solution)/shard_map/all_to_all | solution.py:33
  369.6 9.0 fusion.29
  379.9 12.8 %fusion.5 = f32[512,2560]{1,0:T(8,128)} fusion(bf16[2560,3488]{1,0:T(8,128)(2,1)} %all-gather.2.cloned.1.call-done, bf16[512,896]{1,0:T(8,128)(2,1)S(1)} %get-tuple-element.75, bf16[512,896]{1,0:T(8,128)(2,1)S(1)} %get-tuple-element.74), kind=kOutput, calls=%fused_computation.12 | convolution fusion | flops 4701290496 | bytes 16252928 | tf_op jit(solution)/shard_map/tf,df->td/dot_general | solution.py:291
  392.8 57.1 %reduce-scatter.27.cloned.1.call-done = f32[512,640]{1,0:T(8,128)} async-done(((f32[512,2560]{1,0:T(8,128)}), f32[512,640]{1,0:T(8,128)}) %reduce-scatter.27.cloned.1.call-update) | async-done | bytes 1310736 | tf_op jit(solution)/shard_map/reduce_scatter | solution.py:42
  449.9 2.8 copy.121
  452.7 8.2 fusion.18
  460.9 17.3 %reduce-scatter.41.cloned.1.call-done = f32[320,512]{1,0:T(8,128)} async-done(((f32[640,512]{1,0:T(8,128)}), f32[320,512]{1,0:T(8,128)}) %reduce-scatter.41.cloned.1.call-update) | async-done | bytes 655376
  478.2 2.3 copy.122
  482.5 4.0 all-to-all-start.5
  488.4 3.1 all-to-all-done.5
  491.6 2.3 fusion.89
  495.7 2.7 broadcast_in_dim.56
  498.4 4.4 all-to-all-start.6
  502.9 59.6 %all-to-all-done.6 = bf16[8,512,320]{1,2,0:T(8,128)(2,1)} async-done(((bf16[8,512,320]{1,2,0:T(8,128)(2,1)}), bf16[8,512,320]{1,2,0:T(8,128)(2,1)}, u32[]{:S(2)}, u32[]{:S(2)}) %all-to-all-start.6) | async-done | bytes 2621472 | tf_op jit(solution)/shard_map/all_to_all | solution.py:33
  562.5 4.7 fusion.38
  567.2 10.5 fusion
  579.8 6.8 fusion.12
  590.8 3.9 collective-permute-start.2
  597.4 2.9 collective-permute-done.2
  600.4 3.9 collective-permute-done.3
  604.8 2.9 fusion.44
  607.8 5.5 convolution_add_fusion
  613.4 7.1 convolution_convert_fusion.1
  620.5 2.8 copy.119
  623.6 10.7 convolution_convert_fusion
  634.4 4.7 convolution_convert_fusion.2
  642.5 2.6 copy.125
  645.2 23.8 %reduce-scatter.29.cloned.1.call-done = f32[512,640]{1,0:T(8,128)} async-done(((f32[512,2560]{1,0:T(8,128)}), f32[512,640]{1,0:T(8,128)}) %reduce-scatter.29.cloned.1.call-update) | async-done | bytes 1310736 | tf_op jit(solution)/shard_map/reduce_scatter | solution.py:42
  669.0 2.8 copy.123
  671.8 82.2 %reduce-scatter.35.cloned.1.call-done = bf16[896,160]{0,1:T(8,128)(2,1)} async-done(((bf16[896,2560]{0,1:T(8,128)(2,1)}), bf16[896,160]{0,1:T(8,128)(2,1)}) %reduce-scatter.35.cloned.1.call-update) | async-done | bytes 286736 | tf_op jit(solution)/shard_map/reduce_scatter | solution.py:360
  755.8 26.2 %reduce-scatter.39.cloned.1.call-done = f32[320,512]{1,0:T(8,128)} async-done(((f32[640,512]{1,0:T(8,128)}), f32[320,512]{1,0:T(8,128)}) %reduce-scatter.39.cloned.1.call-update) | async-done | bytes 655376
  782.1 2.3 copy.120
  784.4 109.0 %reduce-scatter.33.cloned.1.call-done = bf16[160,1792]{1,0:T(8,128)(2,1)} async-done(((bf16[2560,1792]{1,0:T(8,128)(2,1)}), bf16[160,1792]{1,0:T(8,128)(2,1)}) %reduce-scatter.33.cloned.1.call-update) | async-done | bytes 573456 | tf_op jit(solution)/shard_map/reduce_scatter | solution.py:357
  895.5 70.9 %reduce-scatter.31.cloned.1.call-done = bf16[320,160]{0,1:T(8,128)(2,1)} async-done(((bf16[320,2560]{0,1:T(8,128)(2,1)}), bf16[320,160]{0,1:T(8,128)(2,1)}) %reduce-scatter.31.cloned.1.call-update) | async-done | bytes 102416 | tf_op jit(solution)/shard_map/reduce_scatter | solution.py:354
  968.0 75.6 %reduce-scatter.45.cloned.1.call-done = bf16[160,480]{1,0:T(8,128)(2,1)} async-done(((bf16[2560,480]{1,0:T(8,128)(2,1)}), bf16[160,480]{1,0:T(8,128)(2,1)}) %reduce-scatter.45.cloned.1.call-update) | async-done | bytes 153616
  1048.1 24.1 %reduce-scatter.43.cloned.1.call-done = f32[320,512]{1,0:T(8,128)} async-done(((f32[640,512]{1,0:T(8,128)}), f32[320,512]{1,0:T(8,128)}) %reduce-scatter.43.cloned.1.call-update) | async-done | bytes 655376
  1074.6 4.0 all-to-all-start.7
  1078.6 5.0 all-to-all-done.7
  1084.2 9.0 all-to-all-start.8
  1093.3 2.6 fusion.54
  (176 shorter events, 55.8 us)
Async XLA Ops:
  7.2 3.8 copy-start.19
  7.2 16.1 %copy-start.24 = (f32[320]{0:T(512)S(1)}, f32[320]{0:T(512)}, u32[]{:S(2)}) copy-start(f32[320]{0:T(512)} %param.13) | copy-start | bytes 3844
  7.2 152.1 %all-gather.2.cloned.1.call-start = ((), (), s32[]{:S(2)}) async-start(), calls=%async_computation.21 | async-start | bytes 19496960 | tf_op jit(solution)/shard_map/all_gather | solution.py:53
  11.2 14.2 %copy-start.1 = (bf16[512,320]{1,0:T(8,128)(2,1)}, bf16[512,320]{1,0:T(8,128)(2,1)S(1)}, u32[]{:S(2)}) copy-start(bf16[512,320]{1,0:T(8,128)(2,1)S(1)} %copy.88) | copy-start | bytes 983044
  22.1 0.6 copy-start.26
  22.7 0.6 copy-start.21
  23.6 5.4 copy-start.28
  25.3 40.8 %all-to-all-start.1 = ((bf16[8,512,320]{1,2,0:T(8,128)(2,1)}), bf16[8,512,320]{1,2,0:T(8,128)(2,1)S(1)}, u32[]{:S(2)}, u32[]{:S(2)}) async-start(bf16[8,512,320]{1,2,0:T(8,128)(2,1)} %broadcast_in_dim.47), calls=%async_computation.1 | async-start | bytes 5242880 | tf_op jit(solution)/shard_map/all_to_all | solution.py:33
  29.0 221.6 %reduce-scatter.23.cloned.1.call-start = ((), (), s32[]{:S(2)}) async-start(), calls=%async_computation.22 | async-start | bytes 6553600 | tf_op jit(solution)/shard_map/reduce_scatter | solution.py:42
  29.8 149.6 %copy-start.10 = (f32[512,40]{0,1:T(8,128)}, f32[512,40]{0,1:T(8,128)S(1)}, u32[]{:S(2)}) copy-start(f32[512,40]{0,1:T(8,128)S(1)} %get-tuple-element.96) | copy-start | bytes 245764
  162.7 16.8 %collective-permute-start.1 = (bf16[512,160]{0,1:T(8,128)(2,1)S(1)}, bf16[512,160]{0,1:T(8,128)(2,1)S(1)}, u32[]{:S(2)}, u32[]{:S(2)}) collective-permute-start(bf16[512,160]{0,1:T(8,128)(2,1)S(1)} %pad_maximum_fusion.8), channel_id=1, source_target_pairs={{0,8},{8,16},{16,24},{24,32},{32,40},{40,48},{48,56},{56,64},{64,7... | collective-permute-start | bytes 491528 | tf_op jit(solution)/shard_map/ppermute | solution.py:64
  165.0 15.3 %collective-permute-start = (bf16[512,160]{0,1:T(8,128)(2,1)S(1)}, bf16[512,160]{0,1:T(8,128)(2,1)}, u32[]{:S(2)}, u32[]{:S(2)}) collective-permute-start(bf16[512,160]{0,1:T(8,128)(2,1)S(1)} %pad_maximum_fusion.8), channel_id=1, source_target_pairs={{0,16},{8,24},{16,32},{24,40},{32,48},{40,56},{48,64},{56,72},{64,... | collective-permute-start | bytes 491528 | tf_op jit(solution)/shard_map/ppermute | solution.py:64
  176.9 4.5 copy-start.9
  179.5 4.2 copy-start.15
  179.5 4.2 copy-start.17
  179.6 0.7 copy-start.20
  181.3 4.2 copy-start.5
  183.8 4.7 copy-start
  190.9 0.7 copy-start.14
  197.7 93.8 %copy-start.23 = (f32[320]{0:T(512)S(1)}, f32[320]{0:T(512)}, u32[]{:S(2)}) copy-start(f32[320]{0:T(512)} %param.18) | copy-start | bytes 3844
  197.7 81.2 %reduce-scatter.37.cloned.1.call-start = ((), (), s32[]{:S(2)}) async-start(), calls=%async_computation.29 | async-start | bytes 1966080
  294.2 34.1 %copy-start.8 = (bf16[512,320]{0,1:T(8,128)(2,1)S(1)}, bf16[512,320]{0,1:T(8,128)(2,1)}, u32[]{:S(2)}) copy-start(bf16[512,320]{0,1:T(8,128)(2,1)} %param.23) | copy-start | bytes 983044
  330.1 39.6 %all-to-all-start.4 = ((bf16[8,512,320]{1,2,0:T(8,128)(2,1)}), bf16[8,512,320]{1,2,0:T(8,128)(2,1)}, u32[]{:S(2)}, u32[]{:S(2)}) async-start(bf16[8,512,320]{1,2,0:T(8,128)(2,1)} %broadcast_in_dim.54), calls=%async_computation.6 | async-start | bytes 5242880 | tf_op jit(solution)/shard_map/all_to_all | solution.py:33
  334.5 115.4 %reduce-scatter.27.cloned.1.call-start = ((), (), s32[]{:S(2)}) async-start(), calls=%async_computation.24 | async-start | bytes 6553600 | tf_op jit(solution)/shard_map/reduce_scatter | solution.py:42
  378.6 0.9 copy-start.29
  378.6 1.3 copy-start.30
  392.8 85.5 %reduce-scatter.41.cloned.1.call-start = ((), (), s32[]{:S(2)}) async-start(), calls=%async_computation.31 | async-start | bytes 1966080
  452.7 167.9 %reduce-scatter.25.cloned.1.call-start = ((), (), s32[]{:S(2)}) async-start(), calls=%async_computation.23 | async-start | bytes 6553600 | tf_op jit(solution)/shard_map/reduce_scatter | solution.py:42
  482.5 9.0 all-to-all-start.5
  498.4 64.0 %all-to-all-start.6 = ((bf16[8,512,320]{1,2,0:T(8,128)(2,1)}), bf16[8,512,320]{1,2,0:T(8,128)(2,1)}, u32[]{:S(2)}, u32[]{:S(2)}) async-start(bf16[8,512,320]{1,2,0:T(8,128)(2,1)} %broadcast_in_dim.56), calls=%async_computation.9 | async-start | bytes 5242880 | tf_op jit(solution)/shard_map/all_to_all | solution.py:33
  502.8 166.2 %reduce-scatter.29.cloned.1.call-start = ((), (), s32[]{:S(2)}) async-start(), calls=%async_computation.25 | async-start | bytes 6553600 | tf_op jit(solution)/shard_map/reduce_scatter | solution.py:42
  562.5 4.7 copy-start.6
  567.1 10.5 slice-start
  567.1 11.2 %slice-start.1 = ((s8[12582912]{0:T(1024)(128)(4,1)}), s8[4194304]{0:T(1024)(128)(4,1)S(1)}, s32[]{:S(2)}) async-start(s8[12582912]{0:T(1024)(128)(4,1)} %bitcast.143), calls=%async_computation.35 | async-start | bytes 8388608
  567.2 12.6 %slice-start.2 = ((s8[12582912]{0:T(1024)(128)(4,1)}), s8[4194304]{0:T(1024)(128)(4,1)S(1)}, s32[]{:S(2)}) async-start(s8[12582912]{0:T(1024)(128)(4,1)} %bitcast.143), calls=%async_computation.36 | async-start | bytes 8388608
  579.8 6.9 copy-start.16
  579.8 6.9 copy-start.18
  590.8 6.5 copy-start.11
  590.8 9.6 collective-permute-start.2
  594.8 9.6 collective-permute-start.3
  597.4 10.4 copy-start.7
  604.8 2.9 copy-start.12
  613.3 140.7 %reduce-scatter.35.cloned.1.call-start = ((), (), s32[]{:S(2)}) async-start(), calls=%async_computation.28 | async-start | bytes 4874240 | tf_op jit(solution)/shard_map/reduce_scatter | solution.py:360
  620.5 161.6 %reduce-scatter.39.cloned.1.call-start = ((), (), s32[]{:S(2)}) async-start(), calls=%async_computation.30 | async-start | bytes 1966080
  623.3 270.0 %reduce-scatter.33.cloned.1.call-start = ((), (), s32[]{:S(2)}) async-start(), calls=%async_computation.27 | async-start | bytes 9748480 | tf_op jit(solution)/shard_map/reduce_scatter | solution.py:357
  634.4 332.0 %reduce-scatter.31.cloned.1.call-start = ((), (), s32[]{:S(2)}) async-start(), calls=%async_computation.26 | async-start | bytes 2088960 | tf_op jit(solution)/shard_map/reduce_scatter | solution.py:354
  639.2 404.5 %reduce-scatter.45.cloned.1.call-start = ((), (), s32[]{:S(2)}) async-start(), calls=%async_computation.33 | async-start | bytes 2785280
  639.2 2.1 copy-start.13
  645.1 427.0 %reduce-scatter.43.cloned.1.call-start = ((), (), s32[]{:S(2)}) async-start(), calls=%async_computation.32 | async-start | bytes 1966080
  782.1 291.5 %copy-start.2 = (bf16[512,320]{1,0:T(8,128)(2,1)S(1)}, bf16[512,320]{1,0:T(8,128)(2,1)}, u32[]{:S(2)}) copy-start(bf16[512,320]{1,0:T(8,128)(2,1)} %copy-done.1) | copy-start | bytes 983044
  782.1 291.5 %copy-start.22 = (f32[512]{0:T(512)S(1)}, f32[512]{0:T(512)}, u32[]{:S(2)}) copy-start(f32[512]{0:T(512)} %copy-done.21) | copy-start | bytes 6148
  782.1 291.5 %copy-start.25 = (f32[320]{0:T(512)S(1)}, f32[320]{0:T(512)}, u32[]{:S(2)}) copy-start(f32[320]{0:T(512)} %param.13) | copy-start | bytes 3844
  784.3 308.9 %copy-start.27 = (f32[512]{0:T(512)S(1)}, f32[512]{0:T(512)}, u32[]{:S(2)}) copy-start(f32[512]{0:T(512)} %copy-done.26) | copy-start | bytes 6148
  784.3 308.9 %copy-start.3 = (f32[512,320]{1,0:T(8,128)S(1)}, f32[512,320]{1,0:T(8,128)}, u32[]{:S(2)}) copy-start(f32[512,320]{1,0:T(8,128)} %copy.122) | copy-start | bytes 1966084
  784.4 308.9 %copy-start.4 = (bf16[512,320]{1,0:T(8,128)(2,1)S(1)}, bf16[512,320]{1,0:T(8,128)(2,1)}, u32[]{:S(2)}) copy-start(bf16[512,320]{1,0:T(8,128)(2,1)} %copy.96) | copy-start | bytes 983044
  1074.6 9.0 all-to-all-start.7
  1084.2 16.3 %all-to-all-start.8 = ((f32[16,1,640]{2,1,0:T(1,128)}), f32[16,1,640]{2,1,0:T(1,128)S(1)}, u32[]{:S(2)}, u32[]{:S(2)}) async-start(f32[16,1,640]{2,1,0:T(1,128)} %broadcast_in_dim.58), calls=%async_computation.12 | async-start | bytes 81920 | tf_op jit(solution)/shard_map/all_to_all | solution.py:33
Sparse Core Ops, SparseCore 0:
  11.1 148.2 all-gather.1
  197.8 52.6 reduce-scatter.22
  253.5 25.4 reduce-scatter.36
  392.9 56.9 reduce-scatter.26
  452.8 25.3 reduce-scatter.40
  480.5 83.6 reduce-scatter.24
  613.4 55.5 reduce-scatter.28
  673.1 80.8 reduce-scatter.34
  756.4 25.6 reduce-scatter.38
  786.9 106.3 reduce-scatter.32
  897.9 68.4 reduce-scatter.30
  970.8 72.7 reduce-scatter.44
  1046.1 25.9 reduce-scatter.42
where the time goes:
time: 1110 us
  waiting for transfers between devices  790 us (71%)
  matrix products  113 us (10%)
  local copies, waits for them, and re-layouts  68.3 us (6%)
  blocking collectives  52.3 us (5%)
  starting transfers between devices  42.8 us (4%)
  other arithmetic  27.2 us (2%)
  between operations  14.9 us (1%)
    unnamed x18, waiting for transfers between devices  169 us
    reduce_scatter x4, waiting for transfers between devices, summed_rows(): x = lax.psum_scatter(x, axis, scatter_dimension=dim, tiled=True)  134 us
    all_to_all x6, waiting for transfers between devices, from_everyone(): lax.all_to_all(jnp.broadcast_to(x[None], (length, *x.shape)), axis, 0, 0,...  125 us
    reduce_scatter x1, waiting for transfers between devices, body(): lax.psum_scatter(grad_gu_full.astype(jnp.bfloat16), 'wide', scatter_dimen...  109 us
    all_gather x1, waiting for transfers between devices, rows_first(): lax.all_gather(both, axis, axis=0, tiled=True)  93.2 us
    reduce_scatter x1, waiting for transfers between devices, body(): lax.psum_scatter(grad_down_full.astype(jnp.bfloat16), 'wide', scatter_dim...  82.2 us
    reduce_scatter x1, waiting for transfers between devices, body(): lax.psum_scatter(grad_out_full.astype(jnp.bfloat16), 'wide', scatter_dime...  70.9 us
    all_to_all x3, blocking collectives, from_everyone(): lax.all_to_all(jnp.broadcast_to(x[None], (length, *x.shape)), axis, 0, 0,...  52.3 us
  transfers between devices with their start and end apart: 23, of which 20 were waited for; matrix products, arithmetic and copies ran while one was open for 12% of the time, Pallas kernels for 0%

commit v1 on v0

v1 whole, which is shorter than its diff:
```python
import functools
import math

import jax
import jax.numpy as jnp
from jax import lax
from jax.experimental import pallas as pl
from jax.experimental.pallas import tpu as pltpu
from jax.sharding import PartitionSpec as P

D = 2560
HEADS = 32
KV_HEADS = 8
HEAD = 80
WINDOW = 1024
TOK = 512
OWN = 64
ROWS = 160
PANEL = 896

epsilon = 1e-05
rope_base = 1000000.0
rope_factor = 8.0
long_wave = 8192.0
short_wave = 2048.0
masked = -1e30

MESH = pl.DeviceIdType.MESH
BF = jnp.bfloat16
F32 = jnp.float32


class Place:
    def __init__(self):
        self.w = lax.axis_index("wide")
        self.n = lax.axis_index("narrow")
        self.z, self.h, self.c = self.w // 4, (self.w // 2) % 2, self.w % 2
        self.x, self.l = self.n // 2, self.n % 2

    def wide(self, dz, dh, dc):
        return ((self.z + dz) % 4) * 4 + ((self.h + dh) % 2) * 2 + (self.c + dc) % 2

    def narrow(self, dx, dl):
        return ((self.x + dx) % 4) * 2 + (self.l + dl) % 2

    def narrow_peers(self):
        return [(self.w, self.narrow(k // 2, k % 2)) for k in (2, 6, 1, 3, 7, 4, 5)]

    def wide_peers(self):
        return [(self.wide(*d), self.n) for d in ((0, 1, 0), (1, 0, 0), (3, 0, 0), (2, 0, 0), (0, 0, 1))]


class Net:
    def __init__(self, place, send_sems, recv_sems, local_sems):
        self.at = place
        self.sems = (send_sems, recv_sems, local_sems)
        self.sent, self.kept = [], []

    def barrier(self, givers, takers):
        bar = pltpu.get_barrier_semaphore()
        for device in givers:
            pl.semaphore_signal(bar, inc=1, device_id=device, device_id_type=MESH)
        pl.semaphore_wait(bar, takers)

    def send(self, src, dst, device):
        i = len(self.sent)
        copy = pltpu.make_async_remote_copy(
            src_ref=src,
            dst_ref=dst,
            send_sem=self.sems[0].at[i],
            recv_sem=self.sems[1].at[i],
            device_id=device,
            device_id_type=MESH,
        )
        copy.start()
        self.sent.append(copy)
        return copy

    def keep(self, src, dst):
        copy = pltpu.make_async_copy(src, dst, self.sems[2].at[len(self.kept)])
        copy.start()
        self.kept.append(copy)
        return copy

    def run(self, tasks):
        tasks = list(tasks)
        while tasks:
            left = []
            for task in tasks:
                try:
                    next(task)
                    left.append(task)
                except StopIteration:
                    pass
            tasks = left
        for copy in self.sent:
            copy.wait_send()
        for copy in self.kept:
            copy.wait()


def narrow_gather(net, src, dst):
    me = net.at.n
    copies = [net.send(src, dst.at[me], peer) for peer in net.at.narrow_peers()]
    net.keep(src, dst.at[me])
    yield
    yield
    yield
    for copy in copies:
        copy.wait_recv()


def narrow_swap(net, src, dst):
    me = net.at.n
    copies = [net.send(src.at[peer[1]], dst.at[me], peer) for peer in net.at.narrow_peers()]
    net.keep(src.at[me], dst.at[me])
    yield
    yield
    yield
    for copy in copies:
        copy.wait_recv()


def narrow_sum(net, src, slots, out):
    me = net.at.n
    copies = [
        net.send(src.at[peer[1]], slots.at[k], peer) for k, peer in enumerate(net.at.narrow_peers())
    ]
    yield
    yield
    yield
    for copy in copies:
        copy.wait_recv()

    @pl.loop(0, OWN // 16)
    def _(i):
        rows = pl.ds(pl.multiple_of(i * 16, 16), 16)
        total = src[me, rows, :].astype(F32)
        for k in range(7):
            total += slots[k, rows, :].astype(F32)
        out[rows, :] = total


def wide_gather(net, src, dst):
    at = net.at
    me, far = at.w, at.wide(0, 1, 0)
    net.keep(src, dst.at[me])
    from_far = net.send(src, dst.at[me], (far, at.n))
    turns = [(d, 0, net.send(src, dst.at[me], (at.wide(d, 0, 0), at.n))) for d in (1, 3, 2)]
    other = (at.wide(0, 0, 1), at.n)
    over = [net.send(src, dst.at[me], other)]
    yield
    from_far.wait_recv()
    turns += [(d, 1, net.send(dst.at[far], dst.at[far], (at.wide(d, 0, 0), at.n))) for d in (1, 3, 2)]
    over.append(net.send(dst.at[far], dst.at[far], other))
    yield
    for d, e, copy in turns:
        copy.wait_recv()
        block = at.wide(-d, e, 0)
        over.append(net.send(dst.at[block], dst.at[block], other))
    yield
    for copy in over:
        copy.wait_recv()


def wide_sum(net, src, half, turned, last, out):
    at = net.at
    other = (at.wide(0, 0, 1), at.n)
    over = [
        net.send(src.at[at.wide(d, e, 1)], half.at[d, e], other) for d in (1, 3, 2, 0) for e in (0, 1)
    ]
    yield
    turns = []
    k = 0
    for d in (1, 3, 2, 0):
        for e in (0, 1):
            over[k].wait_recv()
            k += 1
            block = at.wide(d, e, 0)

            @pl.loop(0, src.shape[1] // 32)
            def _(i):
                rows = pl.ds(pl.multiple_of(i * 32, 32), 32)
                src[block, rows, :] = (
                    src[block, rows, :].astype(F32) + half[d, e, rows, :].astype(F32)
                ).astype(BF)

            if d:
                turns.append(
                    (e, net.send(src.at[block], turned.at[d - 1, e], (at.wide(d, 0, 0), at.n)))
                )
    yield
    mine, far = at.w, at.wide(0, 1, 0)
    for _, copy in turns:
        copy.wait_recv()

    @pl.loop(0, src.shape[1] // 32)
    def _(i):
        rows = pl.ds(pl.multiple_of(i * 32, 32), 32)
        total = src[far, rows, :].astype(F32)
        for d in range(3):
            total += turned[d, 1, rows, :].astype(F32)
        src[far, rows, :] = total.astype(BF)

    final = net.send(src.at[far], last, (far, at.n))
    yield
    final.wait_recv()

    @pl.loop(0, src.shape[1] // 32)
    def _(i):
        rows = pl.ds(pl.multiple_of(i * 32, 32), 32)
        total = src[mine, rows, :].astype(F32) + last[rows, :].astype(F32)
        for d in range(3):
            total += turned[d, 0, rows, :].astype(F32)
        out[rows, :] = total


def wide_sum_scratch(columns):
    return [
        pltpu.VMEM((16, ROWS, columns), BF),
        pltpu.VMEM((4, 2, ROWS, columns), BF),
        pltpu.VMEM((3, 2, ROWS, columns), BF),
        pltpu.VMEM((ROWS, columns), BF),
    ]


def vmem():
    return pl.BlockSpec(memory_space=pltpu.VMEM)


def hbm():
    return pl.BlockSpec(memory_space=pl.ANY)


def exchange(name, number, body, ins, outs, scratch=(), sends=96, keeps=32):
    def kernel(*refs):
        a, b = len(ins), len(ins) + len(outs)
        net = Net(Place(), *refs[-3:])
        body(net, refs[:a], refs[a:b], refs[b:-3])

    return pl.pallas_call(
        kernel,
        out_shape=[jax.ShapeDtypeStruct(shape, dtype) for shape, dtype, _ in outs],
        in_specs=[spec for _, spec in ins],
        out_specs=[spec for _, _, spec in outs],
        scratch_shapes=[
            *scratch,
            pltpu.SemaphoreType.DMA((sends,)),
            pltpu.SemaphoreType.DMA((sends,)),
            pltpu.SemaphoreType.DMA((keeps,)),
        ],
        compiler_params=pltpu.CompilerParams(
            collective_id=number, has_side_effects=True, vmem_limit_bytes=56 * 2**20
        ),
        name=name,
    )(*[array for array, _ in ins])


def documents(doc_lengths, places):
    ends_at = jnp.cumsum(doc_lengths)
    passed = places[:, None] >= ends_at[None, :]
    segment = jnp.sum(passed.astype(jnp.int32), axis=1)
    begins = jnp.sum(jnp.where(passed, doc_lengths[None, :], 0), axis=1)
    return (segment, places - begins)


def scaled_freqs():
    half_width = HEAD // 2
    freqs = rope_base ** (-2.0 * jnp.arange(half_width, dtype=jnp.float32) / HEAD)
    wavelen = 2.0 * math.pi / freqs
    smooth = (long_wave / wavelen - 1.0) / 3.0
    blended = (1.0 - smooth) * freqs / rope_factor + smooth * freqs
    return jnp.where(
        wavelen < short_wave, freqs, jnp.where(wavelen > long_wave, freqs / rope_factor, blended)
    )


def rope_tables(position):
    freqs = scaled_freqs()
    angles = position.astype(jnp.float32)[:, None] * freqs[None, :]
    return (jnp.cos(angles), jnp.sin(angles))


def rotate(stacked, cosine, sine_table):
    half_width = stacked.shape[-1] // 2
    front_half = stacked[..., :half_width]
    back_half = stacked[..., half_width:]
    cos_rows = cosine[:, None, :]
    sin_rows = sine_table[:, None, :]
    return jnp.concatenate(
        [
            front_half * cos_rows - back_half * sin_rows,
            back_half * cos_rows + front_half * sin_rows,
        ],
        axis=-1,
    )


def unrotate(stacked, cosine, sine_table):
    return rotate(stacked, cosine, -sine_table)


def norm_rows(stream, gain):
    inverse_rms = lax.rsqrt(jnp.mean(stream * stream, axis=1, keepdims=True) + epsilon)
    return stream * inverse_rms * gain[None, :], inverse_rms


def norm_back(stream, inverse_rms, gain, upstream):
    weighted = upstream * gain[None, :]
    inner = jnp.sum(weighted * stream, axis=1, keepdims=True)
    through = inverse_rms * weighted - stream * (
        inverse_rms * inverse_rms * inverse_rms * inner / D
    )
    return (through, jnp.sum(upstream * stream * inverse_rms, axis=0))


def scores_of(queries, keys_here, visible):
    raw_scores = jnp.einsum(
        "tkgd,skd->kgts", queries, keys_here, preferred_element_type=jnp.float32
    ) * (1.0 / math.sqrt(HEAD))
    return jnp.where(visible[None, None], raw_scores, masked)


def attend(queries, keys_here, values_here, visible):
    scores = scores_of(queries, keys_here, visible)
    largest = jnp.max(scores, axis=-1, keepdims=True)
    powers = jnp.exp(scores - largest)
    totals = jnp.sum(powers, axis=-1, keepdims=True)
    weights = (powers / totals).astype(jnp.bfloat16)
    mixed = jnp.einsum("kgts,skd->tkgd", weights, values_here, preferred_element_type=jnp.float32)
    return (mixed, largest + jnp.log(totals))


def attend_back(queries, keys_here, values_here, visible, log_totals, upstream):
    weights = jnp.exp(scores_of(queries, keys_here, visible) - log_totals)
    upstream_prob = jnp.einsum(
        "tkgd,skd->kgts", upstream, values_here, preferred_element_type=jnp.float32
    )
    grad_scores = (
        weights * (upstream_prob - jnp.sum(weights * upstream_prob, axis=-1, keepdims=True))
    ).astype(jnp.bfloat16)
    factor = 1.0 / math.sqrt(HEAD)
    grad_queries = (
        jnp.einsum("kgts,skd->tkgd", grad_scores, keys_here, preferred_element_type=jnp.float32)
        * factor
    )
    grad_keys = (
        jnp.einsum("kgts,tkgd->skd", grad_scores, queries, preferred_element_type=jnp.float32)
        * factor
    )
    grad_values = jnp.einsum(
        "kgts,tkgd->skd", weights.astype(jnp.bfloat16), upstream, preferred_element_type=jnp.float32
    )
    return (grad_queries, grad_keys, grad_values)


def packed(block):
    return jnp.concatenate([block[: TOK // 2], block[TOK // 2 :]], axis=1)


def unpacked(pieces):
    return (
        pieces.reshape(8, TOK // 2, 2, D // 8).transpose(2, 1, 0, 3).reshape(TOK, D)
    )


def dot(a, b):
    return jnp.dot(a, b, preferred_element_type=F32)


def dot_t(a, b):
    return lax.dot_general(a, b, (((1,), (1,)), ((), ())), preferred_element_type=F32)


def t_dot(a, b):
    return lax.dot_general(a, b, (((0,), (0,)), ((), ())), preferred_element_type=F32)


def body(
    layer_input,
    gain_attn,
    w_query,
    w_key,
    w_value,
    w_out,
    gain_mlp,
    w_gate,
    w_up,
    w_down,
    doc_lengths,
    cotangent,
):
    q_width, kv_width, ff_width = 320, 80, 896
    per_group = HEADS // KV_HEADS
    me_n = lax.axis_index("narrow")
    me_w = lax.axis_index("wide")
    shard_a = jnp.concatenate(
        [w_query, w_key, w_value, jnp.zeros((ROWS, 32), BF), w_out.T, jnp.zeros((ROWS, 64), BF)],
        axis=1,
    )
    shard_d = w_down.T
    gains = jnp.zeros((8, 384), F32).at[0, :320].set(gain_attn).at[1, :320].set(gain_mlp)
    full = ((16, ROWS, PANEL), BF, hbm())

    def k1(net, ins, outs, scratch):
        at = net.at
        net.barrier(at.narrow_peers() + at.wide_peers(), 12)
        net.run(
            [
                narrow_gather(net, ins[2], outs[2]),
                narrow_gather(net, ins[0], outs[0]),
                wide_gather(net, ins[3], outs[3]),
                narrow_gather(net, ins[1], outs[1]),
                wide_gather(net, ins[4], outs[4]),
            ]
        )

    piece = ((8, TOK // 2, 640), BF, hbm())
    x_pieces, cot_pieces, gain_pieces, full_a, full_g = exchange(
        "gather_input",
        1,
        k1,
        [
            (packed(layer_input), hbm()),
            (packed(cotangent), hbm()),
            (gains, hbm()),
            (shard_a, hbm()),
            (w_gate, hbm()),
        ],
        [piece, piece, ((8, 8, 384), F32, hbm()), full, full],
    )
    full_a = full_a.reshape(D, PANEL)
    full_g = full_g.reshape(D, PANEL)
    gain_one = gain_pieces[:, 0, :320].reshape(D)
    gain_two = gain_pieces[:, 1, :320].reshape(D)
    w_qkv = full_a[:, :480]
    w_outt = full_a[:, 512:832]

    query_index = me_w * TOK + jnp.arange(TOK, dtype=jnp.int32)
    query_seg, query_pos = documents(doc_lengths, query_index)
    cosine, sine_table = rope_tables(query_pos)
    x_full = unpacked(x_pieces)
    cot_full = unpacked(cot_pieces)
    x_mine = lax.dynamic_slice_in_dim(x_full, me_n * OWN, OWN, 0).astype(F32)
    cot_mine = lax.dynamic_slice_in_dim(cot_full, me_n * OWN, OWN, 0).astype(F32)
    normed_one = norm_rows(x_full.astype(F32), gain_one)[0].astype(BF)
    qkv_raw = dot(normed_one, w_qkv)
    queries = rotate(qkv_raw[:, :q_width].reshape(TOK, -1, HEAD), cosine, sine_table).astype(BF)
    keys_mine = rotate(
        qkv_raw[:, q_width : q_width + kv_width].reshape(TOK, 1, HEAD), cosine, sine_table
    )
    kv_mine = jnp.concatenate(
        [
            keys_mine.reshape(TOK, HEAD),
            jnp.zeros((TOK, 48), F32),
            qkv_raw[:, q_width + kv_width :],
            jnp.zeros((TOK, 48), F32),
        ],
        axis=1,
    ).astype(BF)

    def k2(net, ins, outs, scratch):
        at = net.at
        net.barrier([((at.w + 15) % 16, at.n), ((at.w + 14) % 16, at.n)], 2)
        net.keep(ins[0], outs[0].at[2])
        copies = [
            net.send(ins[0], outs[0].at[1], ((at.w + 1) % 16, at.n)),
            net.send(ins[0], outs[0].at[0], ((at.w + 2) % 16, at.n)),
        ]
        for copy in copies:
            copy.wait_recv()
        net.run([])

    (kv_seen,) = exchange(
        "keys_values", 2, k2, [(kv_mine, hbm())], [((3, TOK, 256), BF, hbm())]
    )
    kv_seen = kv_seen.reshape(3 * TOK, 256)
    key_start = (me_w - 2) * TOK
    key_index = key_start + jnp.arange(3 * TOK, dtype=jnp.int32)
    key_seg = documents(doc_lengths, key_index)[0]
    visible = (
        (query_seg[:, None] == key_seg[None, :])
        & (key_index[None, :] <= query_index[:, None])
        & (query_index[:, None] - key_index[None, :] < WINDOW)
        & (key_index[None, :] >= 0)
    )
    keys_here = kv_seen[:, :HEAD].reshape(3 * TOK, 1, HEAD)
    values_here = kv_seen[:, 128 : 128 + HEAD].reshape(3 * TOK, 1, HEAD)
    grouped = queries.reshape(TOK, 1, per_group, HEAD)
    mixed, log_totals = attend(grouped, keys_here, values_here, visible)
    attended = mixed.reshape(TOK, q_width).astype(BF)
    out_part = dot_t(attended, w_outt).astype(BF).reshape(8, OWN, D)

    def k3(net, ins, outs, scratch):
        at = net.at
        net.barrier(at.narrow_peers() + at.wide_peers(), 12)
        net.run(
            [narrow_sum(net, ins[0], scratch[0], outs[0]), wide_gather(net, ins[1], outs[1])]
        )

    mine = ((OWN, D), F32, vmem())
    slots = pltpu.VMEM((7, OWN, D), BF)
    out_sum, full_u = exchange(
        "sum_out", 3, k3, [(out_part, vmem()), (w_up, hbm())], [mine, full], [slots]
    )
    full_u = full_u.reshape(D, PANEL)
    mid_mine = x_mine + out_sum
    normed_mine, inverse_two = norm_rows(mid_mine, gain_two)

    def k4(net, ins, outs, scratch):
        at = net.at
        net.barrier(at.narrow_peers() + at.wide_peers(), 12)
        net.run([narrow_gather(net, ins[0], outs[0]), wide_gather(net, ins[1], outs[1])])

    tokens = ((8, OWN, D), BF, hbm())
    normed_two, full_d = exchange(
        "gather_normed", 4, k4, [(normed_mine.astype(BF), hbm()), (shard_d, hbm())], [tokens, full]
    )
    normed_two = normed_two.reshape(TOK, D)
    full_d = full_d.reshape(D, PANEL)
    gate_val = dot(normed_two, full_g)
    up_val = dot(normed_two, full_u)
    sigmoid_gate = jax.nn.sigmoid(gate_val)
    activated = gate_val * sigmoid_gate
    hidden_act = (activated * up_val).astype(BF)
    down_part = dot_t(hidden_act, full_d).astype(BF).reshape(8, OWN, D)
    grad_hidden = dot(cot_full, full_d)
    grad_gate_pre = (
        grad_hidden * up_val * sigmoid_gate * (1.0 + gate_val * (1.0 - sigmoid_gate))
    ).astype(BF)
    grad_up_pre = (grad_hidden * activated).astype(BF)
    gn2_part = (
        (dot_t(grad_gate_pre, full_g) + dot_t(grad_up_pre, full_u)).astype(BF).reshape(8, OWN, D)
    )
    grad_d = t_dot(cot_full, hidden_act).astype(BF).reshape(16, ROWS, PANEL)
    grad_g = t_dot(normed_two, grad_gate_pre).astype(BF).reshape(16, ROWS, PANEL)
    grad_u = t_dot(normed_two, grad_up_pre).astype(BF).reshape(16, ROWS, PANEL)

    def k5(net, ins, outs, scratch):
        at = net.at
        net.barrier(at.narrow_peers() + at.wide_peers(), 12)
        loads = [net.keep(ins[2], scratch[2]), net.keep(ins[3], scratch[6])]
        for copy in loads:
            copy.wait()
        net.kept.clear()
        net.run(
            [
                narrow_sum(net, ins[0], scratch[0], outs[0]),
                wide_sum(net, *scratch[2:6], outs[2]),
                narrow_sum(net, ins[1], scratch[1], outs[1]),
                wide_sum(net, *scratch[6:10], outs[3]),
            ]
        )

    def summed(columns):
        return ((ROWS, columns), F32, vmem())

    gn2_sum, down_sum, grad_d_mine, grad_g_mine = exchange(
        "sum_mlp",
        5,
        k5,
        [(gn2_part, vmem()), (down_part, vmem()), (grad_d, hbm()), (grad_g, hbm())],
        [mine, mine, summed(PANEL), summed(PANEL)],
        [slots, slots, *wide_sum_scratch(PANEL), *wide_sum_scratch(PANEL)],
    )
    output_mine = (mid_mine + down_sum).astype(BF)
    through_two, gain_two_part = norm_back(mid_mine, inverse_two, gain_two, gn2_sum)
    grad_mid_mine = cot_mine + through_two

    def by_feature(rows):
        return rows.reshape(OWN, 8, 320).transpose(1, 0, 2)

    def k6(net, ins, outs, scratch):
        at = net.at
        net.barrier(at.narrow_peers() + at.wide_peers(), 12)
        net.keep(ins[2], scratch[0]).wait()
        net.kept.clear()
        net.run(
            [
                narrow_gather(net, ins[0], outs[0]),
                narrow_swap(net, ins[1], outs[1]),
                wide_sum(net, *scratch, outs[2]),
            ]
        )

    grad_mid_full, output_rows, grad_u_mine = exchange(
        "gather_grad_mid",
        6,
        k6,
        [
            (grad_mid_mine.astype(BF), hbm()),
            (by_feature(output_mine), hbm()),
            (grad_u, hbm()),
        ],
        [tokens, ((8, OWN, 320), BF, hbm()), summed(PANEL)],
        wide_sum_scratch(PANEL),
    )
    layer_output = output_rows.reshape(TOK, 320)
    grad_mid_full = grad_mid_full.reshape(TOK, D)
    grad_out = t_dot(grad_mid_full, attended).astype(BF)
    grad_out = jnp.pad(grad_out, ((0, 0), (0, 64))).reshape(16, ROWS, 384)
    grad_attended = dot(grad_mid_full, w_outt).astype(BF)
    grad_grouped, grad_keys, grad_values = attend_back(
        grouped,
        keys_here,
        values_here,
        visible,
        log_totals,
        grad_attended.reshape(TOK, 1, per_group, HEAD),
    )
    pad = jnp.zeros((3 * TOK, 48), F32)
    grad_seen = jnp.concatenate(
        [grad_keys.reshape(3 * TOK, HEAD), pad, grad_values.reshape(3 * TOK, HEAD), pad], axis=1
    ).reshape(3, TOK, 256)

    def k7(net, ins, outs, scratch):
        at = net.at
        net.barrier([((at.w + 1) % 16, at.n), ((at.w + 2) % 16, at.n)], 2)
        copies = [
            net.send(ins[0].at[1], outs[0].at[1], ((at.w + 15) % 16, at.n)),
            net.send(ins[0].at[0], outs[0].at[0], ((at.w + 14) % 16, at.n)),
        ]
        for copy in copies:
            copy.wait_recv()
        net.run([])

    (grad_later,) = exchange(
        "grad_keys_values", 7, k7, [(grad_seen[:2].astype(BF), hbm())], [((2, TOK, 256), BF, hbm())]
    )
    grad_kv_mine = (
        grad_seen[2]
        + jnp.where(me_w < 15, grad_later[1], 0).astype(F32)
        + jnp.where(me_w < 14, grad_later[0], 0).astype(F32)
    )
    grad_query_raw = unrotate(grad_grouped.reshape(TOK, 4, HEAD), cosine, sine_table).reshape(
        TOK, q_width
    )
    grad_key_raw = unrotate(
        grad_kv_mine[:, :HEAD].reshape(TOK, 1, HEAD), cosine, sine_table
    ).reshape(TOK, kv_width)
    grad_qkv = jnp.concatenate(
        [grad_query_raw, grad_key_raw, grad_kv_mine[:, 128 : 128 + HEAD]], axis=1
    ).astype(BF)
    gn1_part = dot_t(grad_qkv, w_qkv).astype(BF).reshape(8, OWN, D)
    grad_qkv_full = jnp.pad(t_dot(normed_one, grad_qkv).astype(BF), ((0, 0), (0, 32))).reshape(
        16, ROWS, 512
    )

    def k8(net, ins, outs, scratch):
        at = net.at
        net.barrier(at.narrow_peers() + at.wide_peers(), 12)
        loads = [net.keep(ins[1], scratch[1]), net.keep(ins[2], scratch[5])]
        for copy in loads:
            copy.wait()
        net.kept.clear()
        net.run(
            [
                narrow_sum(net, ins[0], scratch[0], outs[0]),
                wide_sum(net, *scratch[1:5], outs[1]),
                wide_sum(net, *scratch[5:9], outs[2]),
            ]
        )

    gn1_sum, grad_out_mine, grad_qkv_mine = exchange(
        "sum_attn",
        8,
        k8,
        [(gn1_part, vmem()), (grad_out, hbm()), (grad_qkv_full, hbm())],
        [mine, summed(384), summed(512)],
        [slots, *wide_sum_scratch(384), *wide_sum_scratch(512)],
    )
    inverse_one = lax.rsqrt(jnp.mean(x_mine * x_mine, axis=1, keepdims=True) + epsilon)
    through_one, gain_one_part = norm_back(x_mine, inverse_one, gain_one, gn1_sum)
    grad_input_mine = (grad_mid_mine + through_one).astype(BF)
    gain_parts = jnp.stack([gain_one_part.reshape(8, 320), gain_two_part.reshape(8, 320)], axis=1)
    gain_parts = jnp.pad(gain_parts, ((0, 0), (0, 6), (0, 64)))

    def k9(net, ins, outs, scratch):
        at = net.at
        everyone = [((at.w + k) % 16, at.n) for k in range(1, 16)]
        net.barrier(at.narrow_peers() + everyone, 22)
        me = at.n
        copies = [net.send(ins[1].at[p[1]], scratch[0].at[me], p) for p in at.narrow_peers()]
        task = narrow_swap(net, ins[0], outs[0])
        next(task)
        scratch[0][me] = ins[1][me]
        for copy in copies:
            copy.wait_recv()
        total = scratch[0][0]
        for k in range(1, 8):
            total += scratch[0][k]
        scratch[1][0] = total
        copies = [net.send(scratch[1].at[0], scratch[1].at[k + 1], p) for k, p in enumerate(everyone)]
        for copy in copies:
            copy.wait_recv()
        total = scratch[1][0]
        for k in range(1, 16):
            total += scratch[1][k]
        outs[1][...] = total
        net.run([task])

    grad_rows, gain_sums = exchange(
        "swap_grad_input",
        9,
        k9,
        [(by_feature(grad_input_mine), hbm()), (gain_parts, vmem())],
        [((8, OWN, 320), BF, hbm()), ((8, 384), F32, vmem())],
        [pltpu.VMEM((8, 8, 384), F32), pltpu.VMEM((16, 8, 384), F32)],
    )
    return (
        layer_output,
        grad_rows.reshape(TOK, 320).astype(F32),
        gain_sums[0, :320],
        grad_qkv_mine[:, :320],
        grad_qkv_mine[:, 320:400],
        grad_qkv_mine[:, 400:480],
        grad_out_mine[:, :320].T,
        gain_sums[1, :320],
        grad_g_mine,
        grad_u_mine,
        grad_d_mine.T,
    )


def solution(mesh):
    rows, columns = P("wide", "narrow"), P("narrow", "wide")
    return jax.shard_map(
        body,
        mesh=mesh,
        in_specs=(
            rows,
            P("narrow"),
            rows,
            rows,
            rows,
            columns,
            P("narrow"),
            rows,
            rows,
            columns,
            P(),
            rows,
        ),
        out_specs=(
            rows,
            rows,
            P("narrow"),
            rows,
            rows,
            rows,
            columns,
            P("narrow"),
            rows,
            rows,
            columns,
        ),
        check_vma=False,
    )
```

time: 1110 us -> 637 us (0.57)
  waiting for transfers between devices: 790 us -> 0 us
  Pallas kernels: 0 us -> 450 us
  blocking collectives: 52.3 us -> 0 us
  starting transfers between devices: 42.8 us -> 0 us
  matrix products: 113 us -> 87.7 us
  between operations: 14.9 us -> 1.9 us
  local copies, waits for them, and re-layouts: 68.3 us -> 56.8 us
    pallas_call x0 -> x9, Pallas kernels: none -> 450 us  [exchange(): pl.pallas_call(kernel, out_shape=[jax.ShapeDtypeStruct(shape, dtype) for...]
    reduce_scatter x7 -> x0, waiting for transfers between devices: 396 us -> none  [the longest x4 134 us: summed_rows(): x = lax.psum_scatter(x, axis, scatter_dimension=dim, tiled=True)]
    unnamed x18 -> x0, waiting for transfers between devices: 169 us -> none
    all_to_all x6 -> x0, waiting for transfers between devices: 125 us -> none  [from_everyone(): lax.all_to_all(jnp.broadcast_to(x[None], (length, *x.shape)), axis, 0, 0,...]
    all_gather x1 -> x0, waiting for transfers between devices: 93.2 us -> none  [rows_first(): lax.all_gather(both, axis, axis=0, tiled=True)]
    all_to_all x3 -> x0, blocking collectives: 52.3 us -> none  [from_everyone(): lax.all_to_all(jnp.broadcast_to(x[None], (length, *x.shape)), axis, 0, 0,...]
    all_to_all x6 -> x0, starting transfers between devices: 29.4 us -> none  [from_everyone(): lax.all_to_all(jnp.broadcast_to(x[None], (length, *x.shape)), axis, 0, 0,...]
    dot_general x15, matrix products: 92.1 us -> 63.1 us  [the longest x5 22.7 us: dot(): return jnp.dot(a, b, preferred_element_type=F32)]
  transfers between devices with their start and end apart: 23 -> 0, of which waited for: 20 -> 0; matrix products, arithmetic and copies ran while one was open for 12% -> 0% of each run, Pallas kernels for 0% -> 0%
where the time goes in v1:
time: 637 us; the launch traced here: 630 us
  Pallas kernels  450 us (71%)
  matrix products  87.7 us (14%)
  local copies, waits for them, and re-layouts  56.8 us (9%)
  other arithmetic  32.9 us (5%)
    pallas_call x9, Pallas kernels, exchange(): pl.pallas_call(kernel, out_shape=[jax.ShapeDtypeStruct(shape, dtype) for...  450 us
    dot_general x5, matrix products, dot(): return jnp.dot(a, b, preferred_element_type=F32)  22.7 us
    unnamed x116, local copies, waits for them, and re-layouts  22.6 us
    dot_general x5, matrix products, dot_t(): lax.dot_general(a, b, (((1,), (1,)), ((), ())), preferred_element_type=F32)  21.2 us
    dot_general x5, matrix products, t_dot(): lax.dot_general(a, b, (((0,), (0,)), ((), ())), preferred_element_type=F32)  19.1 us

profile of v1, /device:TPU:1, one launch (start us, length us, event | category | flops | bytes accessed | tf_op | source)
XLA Modules:
  0.0 629.7 jit_solution(11818518909242594949)
XLA Ops:
  4.0 1.9 concatenate.45.refs_3_
  8.3 1.0 fusion.72
  9.6 1.0 pad_maximum_fusion.2
  10.7 2.5 fusion.13
  13.2 99.8 %gather_input.1 = (bf16[8,256,640]{2,1,0:T(8,128)(2,1)}, bf16[8,256,640]{2,1,0:T(8,128)(2,1)}, f32[8,8,384]{2,1,0:T(8,128)}, bf16[16,160,896]{2,1,0:T(8,128)(2,1)}, bf16[16,160,896]{2,1,0:T(8,128)(2,1)}) custom-call(bf16[256,640]{1,0:T(8,128)(2,1)} %get-tuple-element.160.refs_0_, bf16[256,640]{1,0:T(8,128)(2,1)} %get-tuple-element.161.refs_1_, ...), custom_call_target="tpu_custom_call" | custom-call | tf_op jit(solution)/shard_map/gather_input/pallas_call | solution.py:241
  113.0 3.0 copy.106
  116.0 2.7 copy.107
  119.2 1.2 slice_reduce_fusion
  121.8 3.1 copy.109
  125.5 2.7 copy.110
  128.7 1.4 copy-done.5
  130.6 4.3 fusion.20
  136.1 1.4 fusion.56
  137.7 1.8 pad_maximum_fusion.6.refs_0_
  139.5 16.8 %keys_values.1 = bf16[3,512,256]{2,1,0:T(8,128)(2,1)} custom-call(bf16[512,256]{1,0:T(8,128)(2,1)} %pad_maximum_fusion.6.refs_0_), custom_call_target="tpu_custom_call" | custom-call | tf_op jit(solution)/shard_map/keys_values/pallas_call | solution.py:241
  156.3 3.4 fusion.74
  159.7 1.7 fusion.3
  161.5 3.0 copy-done
  164.5 2.4 fusion.30
  167.0 4.6 convolution_convert_fusion.5
  171.6 50.9 %sum_out.1 = (f32[64,2560]{1,0:T(8,128)}, bf16[16,160,896]{2,1,0:T(8,128)(2,1)}) custom-call(bf16[8,64,2560]{2,1,0:T(8,128)(2,1)} %bitcast.195, bf16[160,896]{1,0:T(8,128)(2,1)} %refs_1_.1), custom_call_target="tpu_custom_call" | custom-call | tf_op jit(solution)/shard_map/sum_out/pallas_call | solution.py:241
  222.5 1.3 multiply_reduce_fusion.3
  225.3 67.3 %gather_normed.1 = (bf16[8,64,2560]{2,1,0:T(8,128)(2,1)}, bf16[16,160,896]{2,1,0:T(8,128)(2,1)}) custom-call(bf16[64,2560]{1,0:T(8,128)(2,1)} %multiply_convert_fusion.6.refs_0_, bf16[160,896]{1,0:T(8,128)(2,1)} %bitcast.207), custom_call_target="tpu_custom_call" | custom-call | tf_op jit(solution)/shard_map/gather_normed/pallas_call | solution.py:241
  292.6 5.3 fusion.75
  298.0 5.3 fusion.76
  303.4 3.5 multiply_convert_fusion.1
  306.9 4.2 convolution_convert_fusion.4
  311.1 2.9 fusion.77
  314.0 4.3 add_convert_fusion
  318.4 4.5 convolution_convert_fusion.2
  322.9 4.7 convolution_convert_fusion
  327.6 4.6 convolution_convert_fusion.1
  332.2 80.6 %sum_mlp.1 = (f32[64,2560]{1,0:T(8,128)}, f32[64,2560]{1,0:T(8,128)}, f32[160,896]{1,0:T(8,128)}, f32[160,896]{1,0:T(8,128)}) custom-call(bf16[8,64,2560]{2,1,0:T(8,128)(2,1)} %bitcast.194, bf16[8,64,2560]{2,1,0:T(8,128)(2,1)} %bitcast.192, bf16[16,160,896]{2,1,0:T(8,128)(2,1)} %bitcast.179, bf16[16,160,896]{2,1,0:T(8,128)(2,1)} %bitcast.180), custom_call_target="tpu_custom_call" | custom-call | tf_op jit(solution)/shard_map/sum_mlp/pallas_call | solution.py:241
  412.9 1.3 multiply_reduce_fusion.1
  414.9 2.3 add_convert_fusion.1
  418.3 54.1 %gather_grad_mid.1 = (bf16[8,64,2560]{2,1,0:T(8,128)(2,1)}, bf16[8,64,320]{2,1,0:T(8,128)(2,1)}, f32[160,896]{1,0:T(8,128)}) custom-call(bf16[64,2560]{1,0:T(8,128)(2,1)} %get-tuple-element.141.refs_0_, bf16[8,64,320]{2,1,0:T(8,128)(2,1)} %bitcast.202, bf16[16,160,896]{2,1,0:T(8,128)(2,1)} %bitcast.181), custom_call_target="tpu_custom_call" | custom-call | tf_op jit(solution)/shard_map/gather_grad_mid/pallas_call | solution.py:241
  472.4 1.9 copy.129
  474.3 4.3 fusion.27
  478.6 2.2 convolution_convert_fusion.7
  480.8 3.6 copy.149
  484.4 1.5 pad.20.clone
  485.9 6.7 %fusion.14 = f32[1536,80]{1,0:T(8,128)S(1)} fusion(bf16[512,4,80]{0,2,1:T(8,128)(2,1)} %bitcast.199, f32[1,4,512,1536]{2,3,1,0:T(8,128)} %copy-done, f32[4,512]{1,0:T(4,128)S(1)} %log_add_fusion), kind=kOutput, calls=%fused_computation.31 | convolution fusion | flops 509607936 | bytes 13410304 | tf_op jit(solution)/shard_map/kgts,tkgd->skd/dot_general | solution.py:351
  492.7 6.2 fusion
  499.7 5.2 fusion.8
  504.9 4.2 fusion.26
  509.5 1.8 fusion.18
  513.7 11.9 %grad_keys_values.1 = bf16[2,512,256]{2,1,0:T(8,128)(2,1)} custom-call(bf16[2,512,256]{2,1,0:T(8,128)(2,1)} %bitcast.198), custom_call_target="tpu_custom_call" | custom-call | tf_op jit(solution)/shard_map/grad_keys_values/pallas_call | solution.py:241
  525.6 1.1 fusion.40
  527.6 2.0 fusion.52
  530.5 5.1 convolution_convert_fusion.3
  535.6 3.0 convolution_convert_fusion.6
  538.7 2.9 copy.150
  541.6 1.9 pad.21.clone
  543.6 50.6 %sum_attn.1 = (f32[64,2560]{1,0:T(8,128)}, f32[160,384]{1,0:T(8,128)}, f32[160,512]{1,0:T(8,128)}) custom-call(bf16[8,64,2560]{2,1,0:T(8,128)(2,1)} %bitcast.193, bf16[16,160,384]{2,1,0:T(8,128)(2,1)} %bitcast.178, bf16[16,160,512]{2,1,0:T(8,128)(2,1)} %bitcast.174), custom_call_target="tpu_custom_call" | custom-call | tf_op jit(solution)/shard_map/sum_attn/pallas_call | solution.py:241
  594.2 1.7 slice_bitcast_fusion.7
  595.9 1.4 fusion.39
  597.4 1.5 fusion.37
  600.7 18.3 %swap_grad_input.1 = (bf16[8,64,320]{2,1,0:T(8,128)(2,1)}, f32[8,384]{1,0:T(8,128)}) custom-call(bf16[8,64,320]{2,1,0:T(8,128)(2,1)} %bitcast.201, f32[8,8,384]{2,1,0:T(8,128)} %select_maximum_fusion.refs_1_), custom_call_target="tpu_custom_call" | custom-call | tf_op jit(solution)/shard_map/swap_grad_input/pallas_call | solution.py:241
  619.0 1.4 slice_reduce_fusion.2
  620.4 1.8 fusion.71
  622.1 1.7 slice.167
  623.8 1.0 bitcast_convert_fusion
  624.8 1.1 copy.130
  626.7 1.9 copy.163
  (164 shorter events, 22.6 us)
Async XLA Ops:
  0.7 135.4 %copy-start.30 = (f32[40]{0:T(128)}, f32[40]{0:T(128)S(1)}, u32[]{:S(2)}) copy-start(f32[40]{0:T(128)S(1)} %compare_select_fusion.2) | copy-start | bytes 484
  4.0 9.2 %copy-start.26 = (f32[8,384]{1,0:T(8,128)}, f32[8,384]{1,0:T(8,128)S(1)}, u32[]{:S(2)}) copy-start(f32[8,384]{1,0:T(8,128)S(1)} %scatter.9.refs_2_) | copy-start | bytes 36868
  119.2 1.7 copy-start.7
  120.6 10.1 %copy-start.22 = (f32[2560]{0:T(1024)}, f32[2560]{0:T(1024)S(1)}, u32[]{:S(2)}) copy-start(f32[2560]{0:T(1024)S(1)} %mul.372) | copy-start | bytes 30724
  128.7 1.5 copy-start.5
  128.7 6.3 copy-start.32
  130.6 91.9 %copy-start.3 = (bf16[64,2560]{1,0:T(8,128)(2,1)}, bf16[64,2560]{1,0:T(8,128)(2,1)S(1)}, u32[]{:S(2)}) copy-start(bf16[64,2560]{1,0:T(8,128)(2,1)S(1)} %copy.144) | copy-start | bytes 983044
  135.0 21.3 %copy-start.13 = (pred[512,1536]{0,1:T(8,128)(4,1)S(1)}, pred[512,1536]{0,1:T(8,128)(4,1)}, u32[]{:S(2)}) copy-start(pred[512,1536]{0,1:T(8,128)(4,1)} %fusion.13) | copy-start | bytes 2359300
  136.0 23.7 %copy-start.14 = (bf16[512,4,40]{0,2,1:T(8,128)(2,1)}, bf16[512,4,40]{0,2,1:T(8,128)(2,1)S(1)}, u32[]{:S(2)}) copy-start(bf16[512,4,40]{0,2,1:T(8,128)(2,1)S(1)} %get-tuple-element.138) | copy-start | bytes 491524
  136.0 23.7 %copy-start.16 = (bf16[512,4,40]{0,2,1:T(8,128)(2,1)}, bf16[512,4,40]{0,2,1:T(8,128)(2,1)S(1)}, u32[]{:S(2)}) copy-start(bf16[512,4,40]{0,2,1:T(8,128)(2,1)S(1)} %get-tuple-element.139) | copy-start | bytes 491524
  159.7 4.8 copy-start
  159.7 4.8 copy-start.9
  171.6 121.0 %copy-start.8 = (bf16[320,8,2,256]{3,1,2,0:T(8,128)(2,1)S(1)}, bf16[320,8,2,256]{3,1,2,0:T(8,128)(2,1)}, u32[]{:S(2)}) copy-start(bf16[320,8,2,256]{3,1,2,0:T(8,128)(2,1)} %copy-done.7) | copy-start | bytes 7864324
  223.9 74.1 %copy-start.36 = (f32[64]{0:T(128)}, f32[64]{0:T(128)S(1)}, u32[]{:S(2)}) copy-start(f32[64]{0:T(128)S(1)} %get-tuple-element.144) | copy-start | bytes 772
  223.9 191.0 %copy-start.28 = (f32[64]{0:T(128)}, f32[64]{0:T(128)S(1)}, u32[]{:S(2)}) copy-start(f32[64]{0:T(128)S(1)} %add_rsqrt_fusion.1) | copy-start | bytes 772
  292.6 5.4 copy-start.38
  292.6 10.7 %slice-start.5 = ((s8[4587520]{0:T(1024)(128)(4,1)}), s8[4194304]{0:T(1024)(128)(4,1)S(1)}, s32[]{:S(2)}) async-start(s8[4587520]{0:T(1024)(128)(4,1)} %bitcast.222), calls=%async_computation.5 | async-start | bytes 8388608
  292.6 14.2 %slice-start.7 = ((s8[4587520]{0:T(1024)(128)(4,1)}), s8[4194304]{0:T(1024)(128)(4,1)S(1)}, s32[]{:S(2)}) async-start(s8[4587520]{0:T(1024)(128)(4,1)} %bitcast.227), calls=%async_computation.7 | async-start | bytes 8388608
  298.0 5.4 slice-start.6
  298.0 8.9 %slice-start.8 = ((s8[4587520]{0:T(1024)(128)(4,1)}), s8[393216]{0:T(1024)(128)(4,1)S(1)}, s32[]{:S(2)}) async-start(s8[4587520]{0:T(1024)(128)(4,1)} %bitcast.227), calls=%async_computation.8 | async-start | bytes 786432
  298.0 13.1 %slice-start.3 = ((s8[4587520]{0:T(1024)(128)(4,1)}), s8[4194304]{0:T(1024)(128)(4,1)S(1)}, s32[]{:S(2)}) async-start(s8[4587520]{0:T(1024)(128)(4,1)} %bitcast.219), calls=%async_computation.3 | async-start | bytes 8388608
  303.4 7.8 %slice-start.4 = ((s8[4587520]{0:T(1024)(128)(4,1)}), s8[393216]{0:T(1024)(128)(4,1)S(1)}, s32[]{:S(2)}) async-start(s8[4587520]{0:T(1024)(128)(4,1)} %bitcast.219), calls=%async_computation.4 | async-start | bytes 786432
  332.2 82.7 %copy-start.10 = (bf16[64,2560]{1,0:T(8,128)(2,1)S(1)}, bf16[64,2560]{1,0:T(8,128)(2,1)}, u32[]{:S(2)}) copy-start(bf16[64,2560]{1,0:T(8,128)(2,1)} %copy.143) | copy-start | bytes 983044
  414.2 58.2 %copy-start.34 = (f32[64]{0:T(128)}, f32[64]{0:T(128)S(1)}, u32[]{:S(2)}) copy-start(f32[64]{0:T(128)S(1)} %fusion.65) | copy-start | bytes 772
  474.3 4.3 copy-start.39
  485.9 6.7 %copy-start.12 = (bf16[512,320]{0,1:T(8,128)(2,1)S(1)}, bf16[512,320]{0,1:T(8,128)(2,1)}, u32[]{:S(2)}) copy-start(bf16[512,320]{0,1:T(8,128)(2,1)} %fusion.27) | copy-start | bytes 983044
  485.9 13.0 %slice-start = ((s8[12582912]{0:T(1024)(128)(4,1)}), s8[4194304]{0:T(1024)(128)(4,1)S(1)}, s32[]{:S(2)}) async-start(s8[12582912]{0:T(1024)(128)(4,1)} %bitcast.170), calls=%async_computation | async-start | bytes 8388608
  492.6 6.3 slice-start.1
  492.6 7.1 %slice-start.2 = ((s8[12582912]{0:T(1024)(128)(4,1)}), s8[4194304]{0:T(1024)(128)(4,1)S(1)}, s32[]{:S(2)}) async-start(s8[12582912]{0:T(1024)(128)(4,1)} %bitcast.170), calls=%async_computation.2 | async-start | bytes 8388608
  504.9 4.6 copy-start.1
  504.9 4.6 copy-start.15
  504.9 4.6 copy-start.17
  509.5 2.5 copy-start.20
  527.6 8.0 %copy-start.6 = (bf16[320,8,2,256]{3,1,2,0:T(8,128)(2,1)S(1)}, bf16[320,8,2,256]{3,1,2,0:T(8,128)(2,1)}, u32[]{:S(2)}) copy-start(bf16[320,8,2,256]{3,1,2,0:T(8,128)(2,1)} %copy-done.5) | copy-start | bytes 7864324
  529.6 6.0 copy-start.23
  529.6 6.0 copy-start.24
  529.6 6.0 copy-start.33
  530.5 5.1 copy-start.21
  530.5 5.1 copy-start.25
  543.5 52.3 %copy-start.4 = (bf16[64,2560]{1,0:T(8,128)(2,1)S(1)}, bf16[64,2560]{1,0:T(8,128)(2,1)}, u32[]{:S(2)}) copy-start(bf16[64,2560]{1,0:T(8,128)(2,1)} %copy-done.3) | copy-start | bytes 983044
  543.5 52.3 %copy-start.31 = (f32[64]{0:T(128)S(1)}, f32[64]{0:T(128)}, u32[]{:S(2)}) copy-start(f32[64]{0:T(128)} %add_rsqrt_fusion) | copy-start | bytes 772
  543.5 53.8 %copy-start.37 = (f32[64]{0:T(128)S(1)}, f32[64]{0:T(128)}, u32[]{:S(2)}) copy-start(f32[64]{0:T(128)} %copy-done.36) | copy-start | bytes 772
  543.5 53.9 %copy-start.2 = (f32[64,2560]{1,0:T(8,128)S(1)}, f32[64,2560]{1,0:T(8,128)}, u32[]{:S(2)}) copy-start(f32[64,2560]{1,0:T(8,128)} %get-tuple-element.65) | copy-start | bytes 1966084
  543.5 53.9 %copy-start.11 = (bf16[64,2560]{1,0:T(8,128)(2,1)S(1)}, bf16[64,2560]{1,0:T(8,128)(2,1)}, u32[]{:S(2)}) copy-start(bf16[64,2560]{1,0:T(8,128)(2,1)} %copy.143) | copy-start | bytes 983044
  543.6 53.9 %copy-start.29 = (f32[64]{0:T(128)S(1)}, f32[64]{0:T(128)}, u32[]{:S(2)}) copy-start(f32[64]{0:T(128)} %copy-done.28) | copy-start | bytes 772
  543.6 53.9 %copy-start.35 = (f32[64]{0:T(128)S(1)}, f32[64]{0:T(128)}, u32[]{:S(2)}) copy-start(f32[64]{0:T(128)} %copy-done.34) | copy-start | bytes 772
  594.2 5.8 copy-start.27
  595.9 30.1 %copy-start.19 = (f32[160,896]{1,0:T(8,128)S(1)}, f32[160,896]{1,0:T(8,128)}, u32[]{:S(2)}) copy-start(f32[160,896]{1,0:T(8,128)} %get-tuple-element.181) | copy-start | bytes 1720324
  598.9 29.7 %copy-start.18 = (f32[160,896]{1,0:T(8,128)S(1)}, f32[160,896]{1,0:T(8,128)}, u32[]{:S(2)}) copy-start(f32[160,896]{1,0:T(8,128)} %get-tuple-element.76) | copy-start | bytes 1720324

commit v2 on v1

--- a/solution.py
+++ b/solution.py
@@ -99,11 +99,33 @@
             copy.wait()
 
 
-def narrow_gather(net, src, dst):
+def narrow_gather(net, src, dst, cut):
+    at = net.at
+    me, near = at.n, at.narrow(0, 1)
+    net.keep(src, dst.at[me])
+    late = net.send(src.at[cut:], dst.at[me, cut:], (at.w, near))
+    turns = [(d, net.send(src, dst.at[me], (at.w, at.narrow(d, 0)))) for d in (1, 3, 2)]
+    early = net.send(src.at[:cut], dst.at[me, :cut], (at.w, near))
+    yield
+    late.wait_recv()
+    rest = [
+        net.send(dst.at[near, cut:], dst.at[near, cut:], (at.w, at.narrow(d, 0))) for d in (1, 3, 2)
+    ]
+    yield
+    for d, copy in turns:
+        copy.wait_recv()
+        block = at.narrow(-d, 0)
+        rest.append(net.send(dst.at[block, :cut], dst.at[block, :cut], (at.w, near)))
+    yield
+    early.wait_recv()
+    for copy in rest:
+        copy.wait_recv()
+
+
+def narrow_share(net, src, dst):
     me = net.at.n
     copies = [net.send(src, dst.at[me], peer) for peer in net.at.narrow_peers()]
     net.keep(src, dst.at[me])
-    yield
     yield
     yield
     for copy in copies:
@@ -121,98 +143,137 @@
         copy.wait_recv()
 
 
-def narrow_sum(net, src, slots, out):
-    me = net.at.n
-    copies = [
-        net.send(src.at[peer[1]], slots.at[k], peer) for k, peer in enumerate(net.at.narrow_peers())
+def add_rows(rows, step, dst, terms):
+    @pl.loop(0, rows // step)
+    def _(i):
+        part = pl.ds(pl.multiple_of(i * step, step), step)
+        total = terms[0][part, :].astype(F32)
+        for term in terms[1:]:
+            total += term[part, :].astype(F32)
+        dst[part, :] = total.astype(dst.dtype)
+
+
+def narrow_sum(net, src, slots, out, cut):
+    at = net.at
+    me, near = at.n, at.narrow(0, 1)
+    rows = src.shape[1]
+    over = {
+        d: net.send(
+            src.at[at.narrow(d, 1), :cut], slots.at[d - 1, :cut], (at.w, near)
+        )
+        for d in (1, 3, 2)
+    }
+    across = {
+        d: net.send(
+            src.at[at.narrow(d, 1), cut:], slots.at[d - 1, cut:], (at.w, at.narrow(d, 0))
+        )
+        for d in (1, 3, 2)
+    }
+    late = [
+        net.send(src.at[at.narrow(d, 0), cut:], slots.at[2 + d, cut:], (at.w, at.narrow(d, 0)))
+        for d in (1, 3, 2)
     ]
-    yield
-    yield
-    yield
-    for copy in copies:
+    final = [net.send(src.at[near, :cut], slots.at[6, :cut], (at.w, near))]
+    yield
+    early = []
+    for d in (1, 3, 2):
+        over[d].wait_recv()
+        block = at.narrow(d, 0)
+        term = src.at[block, :cut]
+        add_rows(cut, 16, term, [term, slots.at[d - 1, :cut]])
+        early.append(net.send(term, slots.at[2 + d, :cut], (at.w, at.narrow(d, 0))))
+    yield
+    for d in (1, 3, 2):
+        across[d].wait_recv()
+    term = src.at[near, cut:]
+    add_rows(rows - cut, 16, term, [term, *(slots.at[k, cut:] for k in range(3))])
+    final.append(net.send(term, slots.at[6, cut:], (at.w, near)))
+    yield
+    for copy in late + early + final:
         copy.wait_recv()
-
-    @pl.loop(0, OWN // 16)
-    def _(i):
-        rows = pl.ds(pl.multiple_of(i * 16, 16), 16)
-        total = src[me, rows, :].astype(F32)
-        for k in range(7):
-            total += slots[k, rows, :].astype(F32)
-        out[rows, :] = total
+    add_rows(rows, 16, out, [src.at[me], *(slots.at[k] for k in range(3, 7))])
 
 
 def wide_gather(net, src, dst):
     at = net.at
+    half = ROWS // 2
     me, far = at.w, at.wide(0, 1, 0)
+    up, down = (at.wide(1, 0, 0), at.n), (at.wide(3, 0, 0), at.n)
+    other = (at.wide(0, 0, 1), at.n)
     net.keep(src, dst.at[me])
     from_far = net.send(src, dst.at[me], (far, at.n))
-    turns = [(d, 0, net.send(src, dst.at[me], (at.wide(d, 0, 0), at.n))) for d in (1, 3, 2)]
-    other = (at.wide(0, 0, 1), at.n)
+    turns = [[net.send(src, dst.at[me], up), net.send(src, dst.at[me], down)]]
     over = [net.send(src, dst.at[me], other)]
     yield
     from_far.wait_recv()
-    turns += [(d, 1, net.send(dst.at[far], dst.at[far], (at.wide(d, 0, 0), at.n))) for d in (1, 3, 2)]
+    turns.append([net.send(dst.at[far], dst.at[far], up), net.send(dst.at[far], dst.at[far], down)])
     over.append(net.send(dst.at[far], dst.at[far], other))
     yield
-    for d, e, copy in turns:
+    further = []
+    for e in (0, 1):
+        for d, part, ahead, copy in ((3, slice(0, half), up, turns[e][0]), (1, slice(half, ROWS), down, turns[e][1])):
+            copy.wait_recv()
+            block = at.wide(d, e, 0)
+            further.append((e, part, net.send(dst.at[block, part], dst.at[block, part], ahead)))
+            over.append(net.send(dst.at[block], dst.at[block], other))
+        yield
+    for e, part, copy in further:
         copy.wait_recv()
-        block = at.wide(-d, e, 0)
-        over.append(net.send(dst.at[block], dst.at[block], other))
+        block = at.wide(2, e, 0)
+        over.append(net.send(dst.at[block, part], dst.at[block, part], other))
     yield
     for copy in over:
         copy.wait_recv()
 
 
-def wide_sum(net, src, half, turned, last, out):
+def wide_sum(net, src, core, turned, last, out):
     at = net.at
+    rows = src.shape[1]
+    half = rows // 2
+    up, down = (at.wide(1, 0, 0), at.n), (at.wide(3, 0, 0), at.n)
     other = (at.wide(0, 0, 1), at.n)
-    over = [
-        net.send(src.at[at.wide(d, e, 1)], half.at[d, e], other) for d in (1, 3, 2, 0) for e in (0, 1)
-    ]
+    order = [(d, e) for d in (2, 1, 3, 0) for e in (1, 0)]
+    over = {(d, e): net.send(src.at[at.wide(d, e, 1)], core.at[d, e], other) for d, e in order}
+    yield
+    further = []
+    for d, e in order:
+        over[d, e].wait_recv()
+        block = src.at[at.wide(d, e, 0)]
+        add_rows(rows, 32, block, [block, core.at[d, e]])
+        if d == 2:
+            further.append(
+                (
+                    e,
+                    net.send(block.at[:half], turned.at[2, e, :half], up),
+                    net.send(block.at[half:], turned.at[2, e, half:], down),
+                )
+            )
     yield
     turns = []
-    k = 0
-    for d in (1, 3, 2, 0):
-        for e in (0, 1):
-            over[k].wait_recv()
-            k += 1
-            block = at.wide(d, e, 0)
-
-            @pl.loop(0, src.shape[1] // 32)
-            def _(i):
-                rows = pl.ds(pl.multiple_of(i * 32, 32), 32)
-                src[block, rows, :] = (
-                    src[block, rows, :].astype(F32) + half[d, e, rows, :].astype(F32)
-                ).astype(BF)
-
-            if d:
-                turns.append(
-                    (e, net.send(src.at[block], turned.at[d - 1, e], (at.wide(d, 0, 0), at.n)))
-                )
-    yield
-    mine, far = at.w, at.wide(0, 1, 0)
-    for _, copy in turns:
-        copy.wait_recv()
-
-    @pl.loop(0, src.shape[1] // 32)
-    def _(i):
-        rows = pl.ds(pl.multiple_of(i * 32, 32), 32)
-        total = src[far, rows, :].astype(F32)
-        for d in range(3):
-            total += turned[d, 1, rows, :].astype(F32)
-        src[far, rows, :] = total.astype(BF)
-
-    final = net.send(src.at[far], last, (far, at.n))
-    yield
+    for e, first, second in further:
+        first.wait_recv()
+        block = src.at[at.wide(1, e, 0)]
+        part = block.at[:half]
+        add_rows(half, 16, part, [part, turned.at[2, e, :half]])
+        turns.append((e, net.send(block, turned.at[0, e], up)))
+        second.wait_recv()
+        block = src.at[at.wide(3, e, 0)]
+        part = block.at[half:]
+        add_rows(half, 16, part, [part, turned.at[2, e, half:]])
+        turns.append((e, net.send(block, turned.at[1, e], down)))
+        yield
+    for e, copy in turns:
+        if e:
+            copy.wait_recv()
+    block = src.at[at.wide(0, 1, 0)]
+    add_rows(rows, 32, block, [block, turned.at[0, 1], turned.at[1, 1]])
+    final = net.send(block, last, (at.wide(0, 1, 0), at.n))
+    yield
+    for e, copy in turns:
+        if not e:
+            copy.wait_recv()
     final.wait_recv()
-
-    @pl.loop(0, src.shape[1] // 32)
-    def _(i):
-        rows = pl.ds(pl.multiple_of(i * 32, 32), 32)
-        total = src[mine, rows, :].astype(F32) + last[rows, :].astype(F32)
-        for d in range(3):
-            total += turned[d, 0, rows, :].astype(F32)
-        out[rows, :] = total
+    add_rows(rows, 32, out, [src.at[at.w], last, turned.at[0, 0], turned.at[1, 0]])
 
 
 def wide_sum_scratch(columns):
@@ -407,11 +468,11 @@
         net.barrier(at.narrow_peers() + at.wide_peers(), 12)
         net.run(
             [
-                narrow_gather(net, ins[2], outs[2]),
-                narrow_gather(net, ins[0], outs[0]),
                 wide_gather(net, ins[3], outs[3]),
-                narrow_gather(net, ins[1], outs[1]),
+                narrow_share(net, ins[2], outs[2]),
+                narrow_gather(net, ins[0], outs[0], 128),
                 wide_gather(net, ins[4], outs[4]),
+                narrow_gather(net, ins[1], outs[1], 128),
             ]
         )
 
@@ -495,7 +556,7 @@
         at = net.at
         net.barrier(at.narrow_peers() + at.wide_peers(), 12)
         net.run(
-            [narrow_sum(net, ins[0], scratch[0], outs[0]), wide_gather(net, ins[1], outs[1])]
+            [wide_gather(net, ins[1], outs[1]), narrow_sum(net, ins[0], scratch[0], outs[0], 32)]
         )
 
     mine = ((OWN, D), F32, vmem())
@@ -510,7 +571,7 @@
     def k4(net, ins, outs, scratch):
         at = net.at
         net.barrier(at.narrow_peers() + at.wide_peers(), 12)
-        net.run([narrow_gather(net, ins[0], outs[0]), wide_gather(net, ins[1], outs[1])])
+        net.run([wide_gather(net, ins[1], outs[1]), narrow_gather(net, ins[0], outs[0], 32)])
 
     tokens = ((8, OWN, D), BF, hbm())
     normed_two, full_d = exchange(
@@ -545,10 +606,10 @@
         net.kept.clear()
         net.run(
             [
-                narrow_sum(net, ins[0], scratch[0], outs[0]),
                 wide_sum(net, *scratch[2:6], outs[2]),
-                narrow_sum(net, ins[1], scratch[1], outs[1]),
+                narrow_sum(net, ins[0], scratch[0], outs[0], 32),
                 wide_sum(net, *scratch[6:10], outs[3]),
+                narrow_sum(net, ins[1], scratch[1], outs[1], 32),
             ]
         )
 
@@ -577,9 +638,9 @@
         net.kept.clear()
         net.run(
             [
-                narrow_gather(net, ins[0], outs[0]),
+                wide_sum(net, *scratch, outs[2]),
+                narrow_gather(net, ins[0], outs[0], 32),
                 narrow_swap(net, ins[1], outs[1]),
-                wide_sum(net, *scratch, outs[2]),
             ]
         )
 
@@ -655,8 +716,8 @@
         net.kept.clear()
         net.run(
             [
-                narrow_sum(net, ins[0], scratch[0], outs[0]),
                 wide_sum(net, *scratch[1:5], outs[1]),
+                narrow_sum(net, ins[0], scratch[0], outs[0], 32),
                 wide_sum(net, *scratch[5:9], outs[2]),
             ]
         )

time: 637 us -> 518 us (0.81)
  Pallas kernels: 450 us -> 331 us
    pallas_call x9, Pallas kernels: 450 us -> 331 us  [exchange(): pl.pallas_call(kernel, out_shape=[jax.ShapeDtypeStruct(shape, dtype) for...]
where the time goes in v2:
time: 518 us; the launch traced here: 511 us
  Pallas kernels  331 us (64%)
  matrix products  87.7 us (17%)
  local copies, waits for them, and re-layouts  56.8 us (11%)
  other arithmetic  32.9 us (6%)
    pallas_call x9, Pallas kernels, exchange(): pl.pallas_call(kernel, out_shape=[jax.ShapeDtypeStruct(shape, dtype) for...  331 us
    dot_general x5, matrix products, dot(): return jnp.dot(a, b, preferred_element_type=F32)  22.7 us
    unnamed x116, local copies, waits for them, and re-layouts  22.6 us
    dot_general x5, matrix products, dot_t(): lax.dot_general(a, b, (((1,), (1,)), ((), ())), preferred_element_type=F32)  21.2 us
    dot_general x5, matrix products, t_dot(): lax.dot_general(a, b, (((0,), (0,)), ((), ())), preferred_element_type=F32)  19.1 us

profile of v2, /device:TPU:1, one launch (start us, length us, event | category | flops | bytes accessed | tf_op | source)
XLA Modules:
  0.0 510.8 jit_solution(11982340563483587586)
XLA Ops:
  4.0 1.9 concatenate.45.refs_3_
  8.3 1.0 fusion.72
  9.6 1.0 pad_maximum_fusion.2
  10.7 2.5 fusion.13
  13.2 61.0 %gather_input.1 = (bf16[8,256,640]{2,1,0:T(8,128)(2,1)}, bf16[8,256,640]{2,1,0:T(8,128)(2,1)}, f32[8,8,384]{2,1,0:T(8,128)}, bf16[16,160,896]{2,1,0:T(8,128)(2,1)}, bf16[16,160,896]{2,1,0:T(8,128)(2,1)}) custom-call(bf16[256,640]{1,0:T(8,128)(2,1)} %get-tuple-element.160.refs_0_, bf16[256,640]{1,0:T(8,128)(2,1)} %get-tuple-element.161.refs_1_, ...), custom_call_target="tpu_custom_call" | custom-call | tf_op jit(solution)/shard_map/gather_input/pallas_call | solution.py:302
  74.2 3.0 copy.106
  77.2 2.7 copy.107
  80.4 1.2 slice_reduce_fusion
  83.0 3.1 copy.109
  86.7 2.7 copy.110
  89.9 1.4 copy-done.5
  91.8 4.3 fusion.20
  97.3 1.4 fusion.56
  98.9 1.8 pad_maximum_fusion.6.refs_0_
  100.7 17.0 %keys_values.1 = bf16[3,512,256]{2,1,0:T(8,128)(2,1)} custom-call(bf16[512,256]{1,0:T(8,128)(2,1)} %pad_maximum_fusion.6.refs_0_), custom_call_target="tpu_custom_call" | custom-call | tf_op jit(solution)/shard_map/keys_values/pallas_call | solution.py:302
  117.7 3.4 fusion.74
  121.1 1.7 fusion.3
  122.9 3.0 copy-done
  125.9 2.4 fusion.30
  128.4 4.6 convolution_convert_fusion.5
  133.0 34.7 %sum_out.1 = (f32[64,2560]{1,0:T(8,128)}, bf16[16,160,896]{2,1,0:T(8,128)(2,1)}) custom-call(bf16[8,64,2560]{2,1,0:T(8,128)(2,1)} %bitcast.195, bf16[160,896]{1,0:T(8,128)(2,1)} %refs_1_.1), custom_call_target="tpu_custom_call" | custom-call | tf_op jit(solution)/shard_map/sum_out/pallas_call | solution.py:302
  167.7 1.3 multiply_reduce_fusion.3
  170.4 33.9 %gather_normed.1 = (bf16[8,64,2560]{2,1,0:T(8,128)(2,1)}, bf16[16,160,896]{2,1,0:T(8,128)(2,1)}) custom-call(bf16[64,2560]{1,0:T(8,128)(2,1)} %multiply_convert_fusion.6.refs_0_, bf16[160,896]{1,0:T(8,128)(2,1)} %bitcast.207), custom_call_target="tpu_custom_call" | custom-call | tf_op jit(solution)/shard_map/gather_normed/pallas_call | solution.py:302
  204.4 5.3 %fusion.75 = f32[512,896]{1,0:T(8,128)S(1)} fusion(bf16[512,2560]{0,1:T(8,128)(2,1)S(1)} %bitcast.186, bf16[2560,896]{1,0:T(8,128)(2,1)} %bitcast.226), kind=kOutput, calls=%fused_computation.155 | convolution fusion | flops 2348810240 | bytes 9043968 | tf_op jit(solution)/shard_map/dot_general | solution.py:429
  209.8 5.3 %fusion.76 = f32[512,896]{1,0:T(8,128)S(1)} fusion(bf16[512,2560]{1,0:T(8,128)(2,1)S(1)} %bitcast.230, bf16[2560,896]{1,0:T(8,128)(2,1)} %bitcast.218), kind=kOutput, calls=%fused_computation.156 | convolution fusion | flops 2348810240 | bytes 9043968 | tf_op jit(solution)/shard_map/dot_general | solution.py:429
  215.1 3.5 multiply_convert_fusion.1
  218.6 4.2 convolution_convert_fusion.4
  222.9 2.9 fusion.77
  225.8 4.3 add_convert_fusion
  230.1 4.5 convolution_convert_fusion.2
  234.6 4.7 convolution_convert_fusion
  239.4 4.6 convolution_convert_fusion.1
  244.0 70.3 %sum_mlp.1 = (f32[64,2560]{1,0:T(8,128)}, f32[64,2560]{1,0:T(8,128)}, f32[160,896]{1,0:T(8,128)}, f32[160,896]{1,0:T(8,128)}) custom-call(bf16[8,64,2560]{2,1,0:T(8,128)(2,1)} %bitcast.194, bf16[8,64,2560]{2,1,0:T(8,128)(2,1)} %bitcast.192, bf16[16,160,896]{2,1,0:T(8,128)(2,1)} %bitcast.179, bf16[16,160,896]{2,1,0:T(8,128)(2,1)} %bitcast.180), custom_call_target="tpu_custom_call" | custom-call | tf_op jit(solution)/shard_map/sum_mlp/pallas_call | solution.py:302
  314.3 1.3 multiply_reduce_fusion.1
  316.4 2.3 add_convert_fusion.1
  319.7 40.9 %gather_grad_mid.1 = (bf16[8,64,2560]{2,1,0:T(8,128)(2,1)}, bf16[8,64,320]{2,1,0:T(8,128)(2,1)}, f32[160,896]{1,0:T(8,128)}) custom-call(bf16[64,2560]{1,0:T(8,128)(2,1)} %get-tuple-element.141.refs_0_, bf16[8,64,320]{2,1,0:T(8,128)(2,1)} %bitcast.202, bf16[16,160,896]{2,1,0:T(8,128)(2,1)} %bitcast.181), custom_call_target="tpu_custom_call" | custom-call | tf_op jit(solution)/shard_map/gather_grad_mid/pallas_call | solution.py:302
  360.7 1.9 copy.129
  362.6 4.3 fusion.27
  366.9 2.2 convolution_convert_fusion.7
  369.1 3.6 copy.149
  372.7 1.5 pad.20.clone
  374.2 6.7 %fusion.14 = f32[1536,80]{1,0:T(8,128)S(1)} fusion(bf16[512,4,80]{0,2,1:T(8,128)(2,1)} %bitcast.199, f32[1,4,512,1536]{2,3,1,0:T(8,128)} %copy-done, f32[4,512]{1,0:T(4,128)S(1)} %log_add_fusion), kind=kOutput, calls=%fused_computation.31 | convolution fusion | flops 509607936 | bytes 13410304 | tf_op jit(solution)/shard_map/kgts,tkgd->skd/dot_general | solution.py:412
  380.9 6.2 %fusion = (f32[4,512]{1,0:T(4,128)S(1)}, f32[1536,512,4]{1,0,2:T(8,128)S(1)}) fusion(f32[1,4,512,1536]{2,3,1,0:T(8,128)} %copy-done, f32[4,512]{1,0:T(4,128)S(1)} %log_add_fusion, bf16[512,4,80]{0,2,1:T(8,128)(2,1)S(1)} %bitcast.200, bf16[1536,256]{1,0:T(8,128)(2,1)S(1)} %bitcast.190), kind=kOutput, calls=%fused_computation.3 | convolution fusion | flops 512751616 | bytes 25903104 | tf_op jit(solution)/shard_map/tkgd,skd->kgts/dot_general | solution.py:397
  388.0 5.2 %fusion.8 = bf16[4,512,1536]{1,2,0:T(8,128)(2,1)} fusion(f32[1536,512,4]{1,0,2:T(8,128)S(1)} %get-tuple-element.159, f32[1,4,512,1536]{2,3,1,0:T(8,128)S(1)} %bitcast.171, f32[4,512]{1,0:T(4,128)S(1)} %get-tuple-element.158, f32[4,512]{1,0:T(4,128)S(1)} %log_add_fusion), kind=kLoop, calls=%fused_computation.13 | loop fusion | flops 12582912 | bytes 31473664 | tf_op jit(solution)/shard_map/reshape.122
  393.1 4.2 fusion.26
  397.7 1.8 fusion.18
  402.0 12.7 %grad_keys_values.1 = bf16[2,512,256]{2,1,0:T(8,128)(2,1)} custom-call(bf16[2,512,256]{2,1,0:T(8,128)(2,1)} %bitcast.198), custom_call_target="tpu_custom_call" | custom-call | tf_op jit(solution)/shard_map/grad_keys_values/pallas_call | solution.py:302
  414.7 1.1 fusion.40
  416.6 2.0 fusion.52
  419.6 5.1 convolution_convert_fusion.3
  424.7 3.0 convolution_convert_fusion.6
  427.7 2.9 copy.150
  430.7 1.9 pad.21.clone
  432.6 38.5 %sum_attn.1 = (f32[64,2560]{1,0:T(8,128)}, f32[160,384]{1,0:T(8,128)}, f32[160,512]{1,0:T(8,128)}) custom-call(bf16[8,64,2560]{2,1,0:T(8,128)(2,1)} %bitcast.193, bf16[16,160,384]{2,1,0:T(8,128)(2,1)} %bitcast.178, bf16[16,160,512]{2,1,0:T(8,128)(2,1)} %bitcast.174), custom_call_target="tpu_custom_call" | custom-call | tf_op jit(solution)/shard_map/sum_attn/pallas_call | solution.py:302
  471.1 1.7 slice_bitcast_fusion.7
  472.8 1.4 fusion.39
  474.4 1.5 fusion.37
  477.7 22.4 %swap_grad_input.1 = (bf16[8,64,320]{2,1,0:T(8,128)(2,1)}, f32[8,384]{1,0:T(8,128)}) custom-call(bf16[8,64,320]{2,1,0:T(8,128)(2,1)} %bitcast.201, f32[8,8,384]{2,1,0:T(8,128)} %select_maximum_fusion.refs_1_), custom_call_target="tpu_custom_call" | custom-call | tf_op jit(solution)/shard_map/swap_grad_input/pallas_call | solution.py:302
  500.1 1.4 slice_reduce_fusion.2
  501.5 1.8 fusion.71
  503.2 1.7 slice.167
  504.9 1.0 bitcast_convert_fusion
  505.9 1.1 copy.130
  507.8 1.9 copy.163
  (164 shorter events, 22.6 us)
Async XLA Ops:
  0.7 96.6 %copy-start.30 = (f32[40]{0:T(128)}, f32[40]{0:T(128)S(1)}, u32[]{:S(2)}) copy-start(f32[40]{0:T(128)S(1)} %compare_select_fusion.2) | copy-start | bytes 484
  4.0 9.2 %copy-start.26 = (f32[8,384]{1,0:T(8,128)}, f32[8,384]{1,0:T(8,128)S(1)}, u32[]{:S(2)}) copy-start(f32[8,384]{1,0:T(8,128)S(1)} %scatter.9.refs_2_) | copy-start | bytes 36868
  80.4 1.7 copy-start.7
  81.8 10.1 %copy-start.22 = (f32[2560]{0:T(1024)}, f32[2560]{0:T(1024)S(1)}, u32[]{:S(2)}) copy-start(f32[2560]{0:T(1024)S(1)} %mul.372) | copy-start | bytes 30724
  89.9 1.5 copy-start.5
  89.9 6.3 %copy-start.32 = (f32[1,2,2,128]{3,1,2,0:T(2,128)}, f32[1,2,2,128]{3,1,2,0:T(2,128)S(1)}, u32[]{:S(2)}) copy-start(f32[1,2,2,128]{3,1,2,0:T(2,128)S(1)} %copy.153) | copy-start | bytes 6148
  91.8 75.9 %copy-start.3 = (bf16[64,2560]{1,0:T(8,128)(2,1)}, bf16[64,2560]{1,0:T(8,128)(2,1)S(1)}, u32[]{:S(2)}) copy-start(bf16[64,2560]{1,0:T(8,128)(2,1)S(1)} %copy.144) | copy-start | bytes 983044
  96.2 21.5 %copy-start.13 = (pred[512,1536]{0,1:T(8,128)(4,1)S(1)}, pred[512,1536]{0,1:T(8,128)(4,1)}, u32[]{:S(2)}) copy-start(pred[512,1536]{0,1:T(8,128)(4,1)} %fusion.13) | copy-start | bytes 2359300
  97.2 23.9 %copy-start.14 = (bf16[512,4,40]{0,2,1:T(8,128)(2,1)}, bf16[512,4,40]{0,2,1:T(8,128)(2,1)S(1)}, u32[]{:S(2)}) copy-start(bf16[512,4,40]{0,2,1:T(8,128)(2,1)S(1)} %get-tuple-element.138) | copy-start | bytes 491524
  97.2 23.9 %copy-start.16 = (bf16[512,4,40]{0,2,1:T(8,128)(2,1)}, bf16[512,4,40]{0,2,1:T(8,128)(2,1)S(1)}, u32[]{:S(2)}) copy-start(bf16[512,4,40]{0,2,1:T(8,128)(2,1)S(1)} %get-tuple-element.139) | copy-start | bytes 491524
  121.1 4.8 copy-start
  121.1 4.8 copy-start.9
  133.0 71.4 %copy-start.8 = (bf16[320,8,2,256]{3,1,2,0:T(8,128)(2,1)S(1)}, bf16[320,8,2,256]{3,1,2,0:T(8,128)(2,1)}, u32[]{:S(2)}) copy-start(bf16[320,8,2,256]{3,1,2,0:T(8,128)(2,1)} %copy-done.7) | copy-start | bytes 7864324
  169.0 40.7 %copy-start.36 = (f32[64]{0:T(128)}, f32[64]{0:T(128)S(1)}, u32[]{:S(2)}) copy-start(f32[64]{0:T(128)S(1)} %get-tuple-element.144) | copy-start | bytes 772
  169.1 147.3 %copy-start.28 = (f32[64]{0:T(128)}, f32[64]{0:T(128)S(1)}, u32[]{:S(2)}) copy-start(f32[64]{0:T(128)S(1)} %add_rsqrt_fusion.1) | copy-start | bytes 772
  204.4 5.4 %copy-start.38 = (bf16[8,64,2560]{2,1,0:T(8,128)(2,1)S(1)}, bf16[8,64,2560]{2,1,0:T(8,128)(2,1)}, u32[]{:S(2)}) copy-start(bf16[8,64,2560]{2,1,0:T(8,128)(2,1)} %get-tuple-element.62) | copy-start | bytes 7864324
  204.4 10.7 %slice-start.5 = ((s8[4587520]{0:T(1024)(128)(4,1)}), s8[4194304]{0:T(1024)(128)(4,1)S(1)}, s32[]{:S(2)}) async-start(s8[4587520]{0:T(1024)(128)(4,1)} %bitcast.222), calls=%async_computation.5 | async-start | bytes 8388608
  204.4 14.2 %slice-start.7 = ((s8[4587520]{0:T(1024)(128)(4,1)}), s8[4194304]{0:T(1024)(128)(4,1)S(1)}, s32[]{:S(2)}) async-start(s8[4587520]{0:T(1024)(128)(4,1)} %bitcast.227), calls=%async_computation.7 | async-start | bytes 8388608
  209.7 5.4 %slice-start.6 = ((s8[4587520]{0:T(1024)(128)(4,1)}), s8[393216]{0:T(1024)(128)(4,1)S(1)}, s32[]{:S(2)}) async-start(s8[4587520]{0:T(1024)(128)(4,1)} %bitcast.222), calls=%async_computation.6 | async-start | bytes 786432
  209.8 8.9 %slice-start.8 = ((s8[4587520]{0:T(1024)(128)(4,1)}), s8[393216]{0:T(1024)(128)(4,1)S(1)}, s32[]{:S(2)}) async-start(s8[4587520]{0:T(1024)(128)(4,1)} %bitcast.227), calls=%async_computation.8 | async-start | bytes 786432
  209.8 13.1 %slice-start.3 = ((s8[4587520]{0:T(1024)(128)(4,1)}), s8[4194304]{0:T(1024)(128)(4,1)S(1)}, s32[]{:S(2)}) async-start(s8[4587520]{0:T(1024)(128)(4,1)} %bitcast.219), calls=%async_computation.3 | async-start | bytes 8388608
  215.1 7.7 %slice-start.4 = ((s8[4587520]{0:T(1024)(128)(4,1)}), s8[393216]{0:T(1024)(128)(4,1)S(1)}, s32[]{:S(2)}) async-start(s8[4587520]{0:T(1024)(128)(4,1)} %bitcast.219), calls=%async_computation.4 | async-start | bytes 786432
  244.0 72.4 %copy-start.10 = (bf16[64,2560]{1,0:T(8,128)(2,1)S(1)}, bf16[64,2560]{1,0:T(8,128)(2,1)}, u32[]{:S(2)}) copy-start(bf16[64,2560]{1,0:T(8,128)(2,1)} %copy.143) | copy-start | bytes 983044
  315.7 45.0 %copy-start.34 = (f32[64]{0:T(128)}, f32[64]{0:T(128)S(1)}, u32[]{:S(2)}) copy-start(f32[64]{0:T(128)S(1)} %fusion.65) | copy-start | bytes 772
  362.6 4.3 copy-start.39
  374.2 6.7 %copy-start.12 = (bf16[512,320]{0,1:T(8,128)(2,1)S(1)}, bf16[512,320]{0,1:T(8,128)(2,1)}, u32[]{:S(2)}) copy-start(bf16[512,320]{0,1:T(8,128)(2,1)} %fusion.27) | copy-start | bytes 983044
  374.2 13.0 %slice-start = ((s8[12582912]{0:T(1024)(128)(4,1)}), s8[4194304]{0:T(1024)(128)(4,1)S(1)}, s32[]{:S(2)}) async-start(s8[12582912]{0:T(1024)(128)(4,1)} %bitcast.170), calls=%async_computation | async-start | bytes 8388608
  380.9 6.3 %slice-start.1 = ((s8[12582912]{0:T(1024)(128)(4,1)}), s8[4194304]{0:T(1024)(128)(4,1)S(1)}, s32[]{:S(2)}) async-start(s8[12582912]{0:T(1024)(128)(4,1)} %bitcast.170), calls=%async_computation.1 | async-start | bytes 8388608
  380.9 7.1 %slice-start.2 = ((s8[12582912]{0:T(1024)(128)(4,1)}), s8[4194304]{0:T(1024)(128)(4,1)S(1)}, s32[]{:S(2)}) async-start(s8[12582912]{0:T(1024)(128)(4,1)} %bitcast.170), calls=%async_computation.2 | async-start | bytes 8388608
  393.1 4.6 copy-start.1
  393.1 4.6 copy-start.15
  393.1 4.6 copy-start.17
  397.7 2.5 copy-start.20
  416.6 8.0 %copy-start.6 = (bf16[320,8,2,256]{3,1,2,0:T(8,128)(2,1)S(1)}, bf16[320,8,2,256]{3,1,2,0:T(8,128)(2,1)}, u32[]{:S(2)}) copy-start(bf16[320,8,2,256]{3,1,2,0:T(8,128)(2,1)} %copy-done.5) | copy-start | bytes 7864324
  418.7 6.0 %copy-start.23 = (f32[2560]{0:T(1024)S(1)}, f32[2560]{0:T(1024)}, u32[]{:S(2)}) copy-start(f32[2560]{0:T(1024)} %copy-done.22) | copy-start | bytes 30724
  418.7 6.0 %copy-start.24 = (bf16[512,80]{0,1:T(8,128)(2,1)S(1)}, bf16[512,80]{0,1:T(8,128)(2,1)}, u32[]{:S(2)}) copy-start(bf16[512,80]{0,1:T(8,128)(2,1)} %copy.125) | copy-start | bytes 245764
  418.7 6.0 %copy-start.33 = (f32[1,2,2,128]{3,1,2,0:T(2,128)S(1)}, f32[1,2,2,128]{3,1,2,0:T(2,128)}, u32[]{:S(2)}) copy-start(f32[1,2,2,128]{3,1,2,0:T(2,128)} %copy-done.32) | copy-start | bytes 6148
  419.5 5.1 %copy-start.21 = (bf16[512,4,80]{0,2,1:T(8,128)(2,1)S(1)}, bf16[512,4,80]{0,2,1:T(8,128)(2,1)}, u32[]{:S(2)}) copy-start(bf16[512,4,80]{0,2,1:T(8,128)(2,1)} %pad_maximum_fusion.5) | copy-start | bytes 983044
  419.5 5.1 %copy-start.25 = (bf16[512,80]{0,1:T(8,128)(2,1)S(1)}, bf16[512,80]{0,1:T(8,128)(2,1)}, u32[]{:S(2)}) copy-start(bf16[512,80]{0,1:T(8,128)(2,1)} %copy.124) | copy-start | bytes 245764
  432.6 40.2 %copy-start.4 = (bf16[64,2560]{1,0:T(8,128)(2,1)S(1)}, bf16[64,2560]{1,0:T(8,128)(2,1)}, u32[]{:S(2)}) copy-start(bf16[64,2560]{1,0:T(8,128)(2,1)} %copy-done.3) | copy-start | bytes 983044
  432.6 40.2 %copy-start.31 = (f32[64]{0:T(128)S(1)}, f32[64]{0:T(128)}, u32[]{:S(2)}) copy-start(f32[64]{0:T(128)} %add_rsqrt_fusion) | copy-start | bytes 772
  432.6 41.7 %copy-start.37 = (f32[64]{0:T(128)S(1)}, f32[64]{0:T(128)}, u32[]{:S(2)}) copy-start(f32[64]{0:T(128)} %copy-done.36) | copy-start | bytes 772
  432.6 41.8 %copy-start.2 = (f32[64,2560]{1,0:T(8,128)S(1)}, f32[64,2560]{1,0:T(8,128)}, u32[]{:S(2)}) copy-start(f32[64,2560]{1,0:T(8,128)} %get-tuple-element.65) | copy-start | bytes 1966084
  432.6 41.8 %copy-start.11 = (bf16[64,2560]{1,0:T(8,128)(2,1)S(1)}, bf16[64,2560]{1,0:T(8,128)(2,1)}, u32[]{:S(2)}) copy-start(bf16[64,2560]{1,0:T(8,128)(2,1)} %copy.143) | copy-start | bytes 983044
  432.6 41.8 %copy-start.29 = (f32[64]{0:T(128)S(1)}, f32[64]{0:T(128)}, u32[]{:S(2)}) copy-start(f32[64]{0:T(128)} %copy-done.28) | copy-start | bytes 772
  432.6 41.8 %copy-start.35 = (f32[64]{0:T(128)S(1)}, f32[64]{0:T(128)}, u32[]{:S(2)}) copy-start(f32[64]{0:T(128)} %copy-done.34) | copy-start | bytes 772
  471.1 5.8 %copy-start.27 = (f32[8,1,320]{2,1,0:T(1,128)S(1)}, f32[8,1,320]{2,1,0:T(1,128)}, u32[]{:S(2)}) copy-start(f32[8,1,320]{2,1,0:T(1,128)} %stack_reshape.7) | copy-start | bytes 30724
  472.8 34.2 %copy-start.19 = (f32[160,896]{1,0:T(8,128)S(1)}, f32[160,896]{1,0:T(8,128)}, u32[]{:S(2)}) copy-start(f32[160,896]{1,0:T(8,128)} %get-tuple-element.181) | copy-start | bytes 1720324
  475.9 33.9 %copy-start.18 = (f32[160,896]{1,0:T(8,128)S(1)}, f32[160,896]{1,0:T(8,128)}, u32[]{:S(2)}) copy-start(f32[160,896]{1,0:T(8,128)} %get-tuple-element.76) | copy-start | bytes 1720324

commit v3 on v2

v3 whole, which is shorter than its diff:
```python
import functools
import math

import jax
import jax.numpy as jnp
from jax import lax
from jax.experimental import pallas as pl
from jax.experimental.pallas import tpu as pltpu
from jax.sharding import PartitionSpec as P

D = 2560
HEADS = 32
KV_HEADS = 8
HEAD = 80
WINDOW = 1024
TOK = 512
OWN = 64
ROWS = 160
PANEL = 896
TILE = 128
REACH = WINDOW + TILE

epsilon = 1e-05
rope_base = 1000000.0
rope_factor = 8.0
long_wave = 8192.0
short_wave = 2048.0
masked = -1e30

MESH = pl.DeviceIdType.MESH
BF = jnp.bfloat16
F32 = jnp.float32


class Place:
    def __init__(self):
        self.w = lax.axis_index("wide")
        self.n = lax.axis_index("narrow")
        self.z, self.h, self.c = self.w // 4, (self.w // 2) % 2, self.w % 2
        self.x, self.l = self.n // 2, self.n % 2

    def wide(self, dz, dh, dc):
        return ((self.z + dz) % 4) * 4 + ((self.h + dh) % 2) * 2 + (self.c + dc) % 2

    def narrow(self, dx, dl):
        return ((self.x + dx) % 4) * 2 + (self.l + dl) % 2

    def narrow_peers(self):
        return [(self.w, self.narrow(k // 2, k % 2)) for k in (2, 6, 1, 3, 7, 4, 5)]

    def wide_peers(self):
        return [(self.wide(*d), self.n) for d in ((0, 1, 0), (1, 0, 0), (3, 0, 0), (2, 0, 0), (0, 0, 1))]


class Net:
    def __init__(self, place, send_sems, recv_sems, local_sems):
        self.at = place
        self.sems = (send_sems, recv_sems, local_sems)
        self.sent, self.kept, self.open = [], [], []

    def barrier(self, givers, takers):
        bar = pltpu.get_barrier_semaphore()
        for device in givers:
            pl.semaphore_signal(bar, inc=1, device_id=device, device_id_type=MESH)
        pl.semaphore_wait(bar, takers)

    def send(self, src, dst, device):
        i = len(self.sent)
        copy = pltpu.make_async_remote_copy(
            src_ref=src,
            dst_ref=dst,
            send_sem=self.sems[0].at[i],
            recv_sem=self.sems[1].at[i],
            device_id=device,
            device_id_type=MESH,
        )
        copy.start()
        self.sent.append(copy)
        return copy

    def keep(self, src, dst):
        copy = pltpu.make_async_copy(src, dst, self.sems[2].at[len(self.kept)])
        copy.start()
        self.kept.append(copy)
        self.open.append(copy)
        return copy

    def settle(self, *copies):
        for copy in copies:
            copy.wait()
            self.open = [c for c in self.open if c is not copy]

    def run(self, tasks):
        tasks = list(tasks)
        while tasks:
            left = []
            for task in tasks:
                try:
                    next(task)
                    left.append(task)
                except StopIteration:
                    pass
            tasks = left
        for copy in self.sent:
            copy.wait_send()
        for copy in self.open:
            copy.wait()


def block_of(ref, index, rows):
    return ref.at[pl.ds(pl.multiple_of(index * rows, 16), rows)]


def narrow_gather(net, src, dst, cut, stacked=False):
    at = net.at
    me, near = at.n, at.narrow(0, 1)
    rows = src.shape[0]

    def block(n):
        return dst.at[n] if stacked else block_of(dst, n, rows)

    kept = net.keep(src, block(me))
    late = net.send(src.at[cut:], block(me).at[cut:], (at.w, near))
    turns = [(d, net.send(src, block(me), (at.w, at.narrow(d, 0)))) for d in (1, 3, 2)]
    early = net.send(src.at[:cut], block(me).at[:cut], (at.w, near))
    yield
    late.wait_recv()
    rest = [
        net.send(block(near).at[cut:], block(near).at[cut:], (at.w, at.narrow(d, 0)))
        for d in (1, 3, 2)
    ]
    yield
    for d, copy in turns:
        copy.wait_recv()
        part = block(at.narrow(-d, 0)).at[:cut]
        rest.append(net.send(part, part, (at.w, near)))
    yield
    early.wait_recv()
    for copy in rest:
        copy.wait_recv()
    net.settle(kept)


def narrow_share(net, src, dst):
    me = net.at.n
    copies = [net.send(src, dst.at[me], peer) for peer in net.at.narrow_peers()]
    kept = net.keep(src, dst.at[me])
    yield
    yield
    for copy in copies:
        copy.wait_recv()
    net.settle(kept)


def narrow_swap(net, src, dst):
    me = net.at.n
    copies = [net.send(src.at[peer[1]], dst.at[me], peer) for peer in net.at.narrow_peers()]
    net.keep(src.at[me], dst.at[me])
    yield
    yield
    yield
    for copy in copies:
        copy.wait_recv()


def add_rows(rows, step, dst, terms):
    @pl.loop(0, rows // step)
    def _(i):
        part = pl.ds(pl.multiple_of(i * step, step), step)
        total = terms[0][part, :].astype(F32)
        for term in terms[1:]:
            total += term[part, :].astype(F32)
        dst[part, :] = total.astype(dst.dtype)


def narrow_sum(net, src, slots, out, cut):
    at = net.at
    me, near = at.n, at.narrow(0, 1)
    rows = out.shape[0]

    def block(n):
        return block_of(src, n, rows)

    over = {
        d: net.send(block(at.narrow(d, 1)).at[:cut], slots.at[d - 1, :cut], (at.w, near))
        for d in (1, 3, 2)
    }
    across = {
        d: net.send(block(at.narrow(d, 1)).at[cut:], slots.at[d - 1, cut:], (at.w, at.narrow(d, 0)))
        for d in (1, 3, 2)
    }
    late = [
        net.send(block(at.narrow(d, 0)).at[cut:], slots.at[2 + d, cut:], (at.w, at.narrow(d, 0)))
        for d in (1, 3, 2)
    ]
    final = [net.send(block(near).at[:cut], slots.at[6, :cut], (at.w, near))]
    yield
    early = []
    for d in (1, 3, 2):
        over[d].wait_recv()
        term = slots.at[d - 1, :cut]
        add_rows(cut, 16, term, [term, block(at.narrow(d, 0)).at[:cut]])
        early.append(net.send(term, slots.at[2 + d, :cut], (at.w, at.narrow(d, 0))))
    yield
    for d in (1, 3, 2):
        across[d].wait_recv()
    term = slots.at[0, cut:]
    add_rows(rows - cut, 16, term, [block(near).at[cut:], *(slots.at[k, cut:] for k in range(3))])
    final.append(net.send(term, slots.at[6, cut:], (at.w, near)))
    yield
    for copy in late + early + final:
        copy.wait_recv()
    add_rows(rows, 16, out, [block(me), *(slots.at[k] for k in range(3, 7))])


def wide_gather(net, src, dst):
    at = net.at
    half = ROWS // 2
    me, far = at.w, at.wide(0, 1, 0)
    up, down = (at.wide(1, 0, 0), at.n), (at.wide(3, 0, 0), at.n)
    other = (at.wide(0, 0, 1), at.n)

    def block(w):
        return block_of(dst, w, ROWS)

    kept = net.keep(src, block(me))
    from_far = net.send(src, block(me), (far, at.n))
    turns = [[net.send(src, block(me), up), net.send(src, block(me), down)]]
    over = [net.send(src, block(me), other)]
    yield
    from_far.wait_recv()
    turns.append([net.send(block(far), block(far), up), net.send(block(far), block(far), down)])
    over.append(net.send(block(far), block(far), other))
    yield
    further = []
    for e in (0, 1):
        for d, part, ahead, copy in (
            (3, slice(0, half), up, turns[e][0]),
            (1, slice(half, ROWS), down, turns[e][1]),
        ):
            copy.wait_recv()
            shard = block(at.wide(d, e, 0))
            further.append((e, part, net.send(shard.at[part], shard.at[part], ahead)))
            over.append(net.send(shard, shard, other))
        yield
    for e, part, copy in further:
        copy.wait_recv()
        shard = block(at.wide(2, e, 0)).at[part]
        over.append(net.send(shard, shard, other))
    yield
    for copy in over:
        copy.wait_recv()
    net.settle(kept)


def wide_sum(net, src, core, turned, last, out):
    at = net.at
    half = ROWS // 2
    up, down = (at.wide(1, 0, 0), at.n), (at.wide(3, 0, 0), at.n)
    other = (at.wide(0, 0, 1), at.n)
    order = [(d, e) for d in (2, 1, 3, 0) for e in (1, 0)]

    def block(w):
        return block_of(src, w, ROWS)

    over = {(d, e): net.send(block(at.wide(d, e, 1)), core.at[d, e], other) for d, e in order}
    yield
    further = []
    for d, e in order:
        over[d, e].wait_recv()
        part = core.at[d, e]
        add_rows(ROWS, 32, part, [part, block(at.wide(d, e, 0))])
        if d == 2:
            further.append(
                (
                    e,
                    net.send(part.at[:half], turned.at[2, e, :half], up),
                    net.send(part.at[half:], turned.at[2, e, half:], down),
                )
            )
    yield
    turns = []
    for e, first, second in further:
        first.wait_recv()
        part = core.at[1, e]
        add_rows(half, 16, part.at[:half], [part.at[:half], turned.at[2, e, :half]])
        turns.append((e, net.send(part, turned.at[0, e], up)))
        second.wait_recv()
        part = core.at[3, e]
        add_rows(half, 16, part.at[half:], [part.at[half:], turned.at[2, e, half:]])
        turns.append((e, net.send(part, turned.at[1, e], down)))
        yield
    for e, copy in turns:
        if e:
            copy.wait_recv()
    part = core.at[0, 1]
    add_rows(ROWS, 32, part, [part, turned.at[0, 1], turned.at[1, 1]])
    final = net.send(part, last, (at.wide(0, 1, 0), at.n))
    yield
    for e, copy in turns:
        if not e:
            copy.wait_recv()
    final.wait_recv()
    add_rows(ROWS, 32, out, [core.at[0, 0], last, turned.at[0, 0], turned.at[1, 0]])


def step(*tasks):
    for task in tasks:
        next(task, None)


def finish(*tasks):
    tasks = list(tasks)
    while tasks:
        tasks = [task for task in tasks if next(task, "end") != "end"]


def pieces_of(width, size, body):
    whole = width // size

    @pl.loop(0, whole)
    def _(i):
        body(pl.ds(pl.multiple_of(i * size, size), size))

    if width % size:
        body(pl.ds(whole * size, width % size))


def dot(a, b):
    return jnp.dot(a, b, preferred_element_type=F32)


def dot_t(a, b):
    return lax.dot_general(a, b, (((1,), (1,)), ((), ())), preferred_element_type=F32)


def t_dot(a, b):
    return lax.dot_general(a, b, (((0,), (0,)), ((), ())), preferred_element_type=F32)


def spread(dst, pieces):
    for j in range(8):
        for k in range(2):
            dst[pl.ds(k * 256, 256), pl.ds(j * 320, 320)] = pieces[j, :, pl.ds(k * 320, 320)]


def scores(keys, queries, low, first):
    raw = dot(keys, queries) * (1.0 / math.sqrt(HEAD))
    key = first + lax.broadcasted_iota(jnp.int32, raw.shape, 0)
    query = first + WINDOW + lax.broadcasted_iota(jnp.int32, raw.shape, 1) % TILE
    return jnp.where((key >= low) & (key <= query), raw, masked)


def attention(net, ins, outs, scratch):
    x_own, cot_own, gains_own, shard_a, shard_gu, shard_d, cosine, sine, low = ins
    normed, queries, kv, lse, attended, w_a, x_rows, mid, normed_mid, inverse, gains = outs[:11]
    cot_pieces, w_gu, w_d = outs[11:]
    x_pieces, gain_pieces, x, qkv, src, slots, total, values_t = scratch
    at = net.at
    later = [((at.w + k) % 16, at.n) for k in (1, 2)]
    earlier = [((at.w + 16 - k) % 16, at.n) for k in (1, 2)]
    net.barrier(at.narrow_peers() + at.wide_peers() + earlier, 14)
    panel = wide_gather(net, shard_a, w_a)
    stream = narrow_gather(net, x_own, x_pieces, 128, True)
    sizes = narrow_share(net, gains_own, gain_pieces)
    step(panel, stream, sizes)
    step(stream, panel, stream, panel, panel)
    finish(stream, sizes)
    cots = narrow_gather(net, cot_own, cot_pieces, 128, True)
    gate_up = wide_gather(net, shard_gu, w_gu)
    step(cots)
    spread(x, x_pieces)
    for j in range(8):
        gains[:, pl.ds(j * 320, 320)] = gain_pieces[j, :, :320]

    @pl.loop(0, TOK // 16)
    def _(i):
        rows = pl.ds(pl.multiple_of(i * 16, 16), 16)
        part = x[rows, :].astype(F32)
        inv = lax.rsqrt(jnp.mean(part * part, axis=1, keepdims=True) + epsilon)
        normed[rows, :] = (part * inv * gains[0:1, :]).astype(BF)

    own = x[pl.ds(pl.multiple_of(at.n * OWN, OWN), OWN), :].astype(F32)
    x_rows[...] = own
    finish(panel)
    step(gate_up)
    for k in range(2):
        part = pl.ds(k * 256, 256)
        qkv[part, :] = dot(normed[...], w_a[:, part]).T
    cos, sin = cosine[...], sine[...]
    zeros = jnp.zeros((48, TOK), F32)

    def turned(at_row):
        a, b = qkv[pl.ds(at_row, 40), :], qkv[pl.ds(at_row + 40, 40), :]
        return jnp.concatenate([a * cos - b * sin, b * cos + a * sin, zeros], axis=0)

    mine = pl.ds(2 * TOK, TOK)
    kv[mine, :128] = turned(320).T.astype(BF)
    kv[mine, 128:] = jnp.concatenate([qkv[pl.ds(400, 80), :], zeros], axis=0).T.astype(BF)
    arriving = [
        net.send(kv.at[mine], kv.at[pl.ds((2 - k) * TOK, TOK)], later[k - 1]) for k in (1, 2)
    ]
    for head in range(4):
        one = turned(head * HEAD).astype(BF)
        for tile in range(4):
            queries[tile, :, pl.ds(head * TILE, TILE)] = one[:, tile * TILE : (tile + 1) * TILE]
    step(cots, gate_up)
    for copy in arriving:
        copy.wait_recv()
    values_t[...] = kv[:, 128:].T

    @pl.loop(0, 4)
    def _(i):
        first = pl.multiple_of(i * TILE, TILE)
        seen = pl.ds(first, REACH)
        s = scores(kv[seen, :128], queries[i], low[i], first)
        largest = jnp.max(s, axis=0, keepdims=True)
        powers = jnp.exp(s - largest)
        totals = jnp.sum(powers, axis=0, keepdims=True)
        weights = (powers / totals).astype(BF)
        lse[i] = largest + jnp.log(totals)
        mixed = dot(values_t[:, seen], weights)
        attended[pl.ds(first, TILE), :] = (
            jnp.concatenate([mixed[:HEAD, h * TILE : (h + 1) * TILE] for h in range(4)], axis=0)
            .T.astype(BF)
        )

    @pl.loop(0, D // 256)
    def _(i):
        rows = pl.ds(pl.multiple_of(i * 256, 256), 256)
        src[:, rows] = dot_t(attended[...], w_a[rows, 512:832]).astype(BF)

    summed = narrow_sum(net, src, slots, total, 32)
    step(summed, cots, gate_up, gate_up, gate_up)
    down = wide_gather(net, shard_d, w_d)
    step(down)
    finish(summed)
    step(cots, down, gate_up)
    stream = x_rows[...] + total[...]
    mid[...] = stream
    inv = lax.rsqrt(jnp.mean(stream * stream, axis=1, keepdims=True) + epsilon)
    inverse[...] = jnp.broadcast_to(inv, inverse.shape)
    normed_mid[...] = (stream * inv * gains[1:2, :]).astype(BF)
    finish(cots, gate_up, down)
    net.run([])


def mlp(net, ins, outs, scratch):
    normed_own, d_hbm, gu_hbm, cot_hbm, mid, inverse, gains = ins
    grad_mid_full, grad_mid, down_part, grad_gu, grad_d, gain_part = outs
    w_gu, w_d, normed, cot_pieces, cot, gu, grad_hidden, hidden, grad_pre, src, slots, total = scratch[:12]
    core, turned, last, low = scratch[12:]
    at = net.at
    net.barrier(at.narrow_peers() + at.wide_peers(), 12)
    gather = narrow_gather(net, normed_own, normed, 32)
    step(gather)
    pieces = net.keep(cot_hbm, cot_pieces)
    weights = net.keep(gu_hbm, w_gu), net.keep(d_hbm, w_d)
    net.settle(pieces)
    spread(cot, cot_pieces)
    step(gather)
    net.settle(*weights)

    def back_down(columns):
        grad_hidden[:, columns] = dot(cot[...], w_d[:, columns])

    pieces_of(PANEL, 256, back_down)
    finish(gather)

    def gate_up(columns):
        gu[:, columns] = dot(normed[...], w_gu[:, columns])

    pieces_of(2 * PANEL, 256, gate_up)

    @pl.loop(0, TOK // 16)
    def _(i):
        rows = pl.ds(pl.multiple_of(i * 16, 16), 16)
        gate, up, grad = gu[rows, :PANEL], gu[rows, PANEL:], grad_hidden[rows, :]
        sigmoid = jax.nn.sigmoid(gate)
        active = gate * sigmoid
        hidden[rows, :] = (active * up).astype(BF)
        grad_pre[rows, :PANEL] = (grad * up * sigmoid * (1.0 + gate * (1.0 - sigmoid))).astype(BF)
        grad_pre[rows, PANEL:] = (grad * active).astype(BF)

    def back_normed(i):
        rows = pl.ds(pl.multiple_of(i * 256, 256), 256)
        src[:, rows] = dot_t(grad_pre[...], w_gu[rows, :]).astype(BF)

    pl.loop(0, D // 256)(back_normed)
    summed = narrow_sum(net, src, slots, total, 32)
    step(summed)

    def weight_grad(left, right, dst):
        def one(i):
            rows = pl.ds(pl.multiple_of(i * 256, 256), 256)
            dst[rows, :] = t_dot(left[:, rows], right[...]).astype(BF)

        pl.loop(0, D // 256)(one)

    weight_grad(normed, grad_pre, w_gu)
    sums = [wide_sum(net, w_gu, core, turned, last, grad_gu)]
    step(*sums)
    step(summed)

    def forward_down(i):
        rows = pl.ds(pl.multiple_of(i * 256, 256), 256)
        down_part[:, rows] = dot_t(hidden[...], w_d[rows, :]).astype(BF)

    pl.loop(0, D // 256)(forward_down)
    step(*sums)
    step(summed)
    weight_grad(cot, hidden, w_d)
    net.keep(w_d, grad_d)
    finish(summed)
    inv, scale = inverse[:, :1], gains[1:2, :]
    grad, stream = total[...], mid[...]
    weighted = grad * scale
    inner = jnp.sum(weighted * stream, axis=1, keepdims=True)
    through = inv * weighted - stream * (inv * inv * inv * inner / D)
    own = cot[pl.ds(pl.multiple_of(at.n * OWN, OWN), OWN), :].astype(F32) + through
    grad_mid[...] = own
    low[...] = own.astype(BF)
    gain_part[...] = jnp.broadcast_to(
        jnp.sum(grad * stream * inv, axis=0, keepdims=True), gain_part.shape
    )
    finish(narrow_gather(net, low, grad_mid_full, 32), *sums)
    net.run([])


def attention_back(net, ins, outs, scratch):
    grad_mid, grad_mid_own, attended, queries, kv, lse, low, w_a, normed = ins[:9]
    cosine, sine, down_part, d_hbm, mid, x_rows, gains, gain_two_part = ins[9:]
    output_rows, grad_rows, gain_sums, grad_out, grad_qkv, grad_d = outs
    w_d, upstream, keys_t, grad_kv, grad_q, src, slots_one, slots_two, total_one, total_two = scratch[:10]
    later_kv, turned_back, qkv_rows, w_out, w_qkv, rows_one, rows_two, parts, narrow_parts, wide_parts = scratch[10:20]
    sum_d, sum_out, sum_qkv = scratch[20:23], scratch[23:26], scratch[26:29]
    at = net.at
    everyone = [((at.w + k) % 16, at.n) for k in range(1, 16)]
    net.barrier(at.narrow_peers() + everyone, 22)
    loaded = net.keep(d_hbm, w_d)
    downs = narrow_sum(net, down_part, slots_one, total_one, 32)
    step(downs)
    for columns in (pl.ds(0, 256), pl.ds(256, 64)):
        qkv_rows[:, columns] = dot(
            grad_mid[...], w_a[:, pl.ds(512 + columns.start, columns.size)]
        )
    grads_t = qkv_rows[...].T
    zeros = jnp.zeros((48, TOK), F32)
    for head in range(4):
        one = jnp.concatenate([grads_t[head * HEAD : (head + 1) * HEAD], zeros], axis=0).astype(BF)
        for tile in range(4):
            upstream[tile, :, pl.ds(head * TILE, TILE)] = one[:, tile * TILE : (tile + 1) * TILE]
    keys_t[...] = kv[:, :128].T
    net.settle(loaded)
    wide_d = wide_sum(net, w_d, *sum_d, grad_d)
    step(wide_d, downs)
    fill = jnp.zeros((256, 64), F32)

    @pl.loop(0, D // 256)
    def _(i):
        rows = pl.ds(pl.multiple_of(i * 256, 256), 256)
        w_out[rows, :] = jnp.concatenate(
            [t_dot(grad_mid[:, rows], attended[...]), fill], axis=1
        ).astype(BF)

    wide_out = wide_sum(net, w_out, *sum_out, grad_out)
    step(wide_d, wide_out, downs)
    grad_kv[...] = jnp.zeros(grad_kv.shape, F32)
    factor = 1.0 / math.sqrt(HEAD)

    def one_tile(i):
        first = pl.multiple_of(i * TILE, TILE)
        seen = pl.ds(first, REACH)
        s = scores(kv[seen, :128], queries[i], low[i], first)
        weights = jnp.exp(s - lse[i])
        grad_weights = dot(kv[seen, 128:], upstream[i])
        inner = jnp.sum(weights * grad_weights, axis=0, keepdims=True)
        grad_scores = (weights * (grad_weights - inner)).astype(BF)
        grad_kv[seen, 128:] += dot_t(weights.astype(BF), upstream[i])
        grad_kv[seen, :128] += dot_t(grad_scores, queries[i]) * factor
        back = dot(keys_t[:, seen], grad_scores) * factor
        for head in range(4):
            grad_q[pl.ds(head * HEAD, HEAD), pl.ds(first, TILE)] = back[
                :HEAD, head * TILE : (head + 1) * TILE
            ]

    pl.loop(0, 2)(one_tile)
    step(wide_d, wide_out)
    pl.loop(2, 4)(one_tile)
    later_kv[...] = grad_kv[pl.ds(0, 2 * TOK), :].astype(BF)
    arriving = [
        net.send(
            later_kv.at[pl.ds((2 - k) * TOK, TOK)],
            turned_back.at[2 - k],
            ((at.w + 16 - k) % 16, at.n),
        )
        for k in (1, 2)
    ]
    step(wide_d, wide_out, downs)
    cos, sin = cosine[...], sine[...]

    def unturned(part):
        a, b = part[:40], part[40:80]
        return [a * cos + b * sin, b * cos - a * sin]

    rotated = []
    for head in range(4):
        rotated += unturned(grad_q[pl.ds(head * HEAD, HEAD), :])
    rows_one_of = narrow_swap(net, rows_one, output_rows)
    finish(downs)
    by_feature(rows_one, (mid[...] + total_one[...]).astype(BF))
    step(rows_one_of)
    for copy in arriving:
        copy.wait_recv()
    whole = (
        grad_kv[pl.ds(2 * TOK, TOK), :]
        + turned_back[0].astype(F32)
        + turned_back[1].astype(F32)
    )
    rotated += unturned(whole[:, :128].T)
    rotated += [whole[:, 128:].T[:HEAD], jnp.zeros((32, TOK), F32)]
    grads = jnp.concatenate(rotated, axis=0).T.astype(BF)
    grads_ref = scratch[29]
    grads_ref[...] = grads

    @pl.loop(0, D // 256)
    def _(i):
        rows = pl.ds(pl.multiple_of(i * 256, 256), 256)
        src[:, rows] = dot_t(grads_ref[...], w_a[rows, :512]).astype(BF)

    summed = narrow_sum(net, src, slots_two, total_two, 32)
    step(summed)

    @pl.loop(0, D // 256)
    def _(i):
        rows = pl.ds(pl.multiple_of(i * 256, 256), 256)
        w_qkv[rows, :] = t_dot(normed[:, rows], grads_ref[...]).astype(BF)

    wide_qkv = wide_sum(net, w_qkv, *sum_qkv, grad_qkv)
    step(wide_qkv, wide_d, wide_out, summed, wide_qkv, summed)
    finish(summed)
    step(wide_qkv, wide_d, wide_out)
    stream, grad = x_rows[...], total_two[...]
    inv = lax.rsqrt(jnp.mean(stream * stream, axis=1, keepdims=True) + epsilon)
    weighted = grad * gains[0:1, :]
    inner = jnp.sum(weighted * stream, axis=1, keepdims=True)
    through = inv * weighted - stream * (inv * inv * inv * inner / D)
    by_feature(rows_two, (grad_mid_own[...] + through).astype(BF))
    back = narrow_swap(net, rows_two, grad_rows)
    step(back)
    gain_one = jnp.sum(grad * stream * inv, axis=0, keepdims=True)
    both = jnp.concatenate([gain_one, gain_two_part[0:1, :], jnp.zeros((6, D), F32)], axis=0)
    for j in range(8):
        parts[j, :, :320] = both[:, j * 320 : (j + 1) * 320]
        parts[j, :, 320:] = jnp.zeros((8, 64), F32)
    me = at.n
    copies = [net.send(parts.at[p[1]], narrow_parts.at[me], p) for p in at.narrow_peers()]
    narrow_parts[me] = parts[me]
    step(wide_qkv, wide_d, wide_out)
    for copy in copies:
        copy.wait_recv()
    sum_parts = narrow_parts[0]
    for k in range(1, 8):
        sum_parts += narrow_parts[k]
    wide_parts[0] = sum_parts
    copies = [
        net.send(wide_parts.at[0], wide_parts.at[k + 1], p) for k, p in enumerate(everyone)
    ]
    step(wide_qkv, wide_d, wide_out)
    for copy in copies:
        copy.wait_recv()
    sum_parts = wide_parts[0]
    for k in range(1, 16):
        sum_parts += wide_parts[k]
    gain_sums[...] = sum_parts
    finish(wide_d, wide_out, wide_qkv, rows_one_of, back)
    net.run([])


def by_feature(dst, rows):
    for j in range(8):
        dst[j] = rows[:, j * 320 : (j + 1) * 320]


def wide_sum_scratch(columns):
    return [
        pltpu.VMEM((4, 2, ROWS, columns), BF),
        pltpu.VMEM((3, 2, ROWS, columns), BF),
        pltpu.VMEM((ROWS, columns), BF),
    ]


def vmem():
    return pl.BlockSpec(memory_space=pltpu.VMEM)


def hbm():
    return pl.BlockSpec(memory_space=pl.ANY)


def exchange(name, number, body, ins, outs, scratch=(), sends=160, keeps=16):
    def kernel(*refs):
        a, b = len(ins), len(ins) + len(outs)
        net = Net(Place(), *refs[-3:])
        body(net, refs[:a], refs[a:b], refs[b:-3])

    return pl.pallas_call(
        kernel,
        out_shape=[jax.ShapeDtypeStruct(shape, dtype) for shape, dtype, _ in outs],
        in_specs=[spec for _, spec in ins],
        out_specs=[spec for _, _, spec in outs],
        scratch_shapes=[
            *scratch,
            pltpu.SemaphoreType.DMA((sends,)),
            pltpu.SemaphoreType.DMA((sends,)),
            pltpu.SemaphoreType.DMA((keeps,)),
        ],
        compiler_params=pltpu.CompilerParams(
            collective_id=number, has_side_effects=True, vmem_limit_bytes=58 * 2**20
        ),
        name=name,
    )(*[array for array, _ in ins])


def documents(doc_lengths, places):
    ends_at = jnp.cumsum(doc_lengths)
    passed = places[:, None] >= ends_at[None, :]
    segment = jnp.sum(passed.astype(jnp.int32), axis=1)
    begins = jnp.sum(jnp.where(passed, doc_lengths[None, :], 0), axis=1)
    return (segment, places - begins)


def scaled_freqs():
    half_width = HEAD // 2
    freqs = rope_base ** (-2.0 * jnp.arange(half_width, dtype=jnp.float32) / HEAD)
    wavelen = 2.0 * math.pi / freqs
    smooth = (long_wave / wavelen - 1.0) / 3.0
    blended = (1.0 - smooth) * freqs / rope_factor + smooth * freqs
    return jnp.where(
        wavelen < short_wave, freqs, jnp.where(wavelen > long_wave, freqs / rope_factor, blended)
    )


def rope_tables(position):
    freqs = scaled_freqs()
    angles = freqs[:, None] * position.astype(jnp.float32)[None, :]
    return (jnp.cos(angles), jnp.sin(angles))


def packed(block):
    return jnp.concatenate([block[: TOK // 2], block[TOK // 2 :]], axis=1)


def body(
    layer_input,
    gain_attn,
    w_query,
    w_key,
    w_value,
    w_out,
    gain_mlp,
    w_gate,
    w_up,
    w_down,
    doc_lengths,
    cotangent,
):
    me_w = lax.axis_index("wide")
    shard_a = jnp.concatenate(
        [w_query, w_key, w_value, jnp.zeros((ROWS, 32), BF), w_out.T, jnp.zeros((ROWS, 64), BF)],
        axis=1,
    )
    shard_gu = jnp.concatenate([w_gate, w_up], axis=1)
    gains_own = jnp.zeros((8, 384), F32).at[0, :320].set(gain_attn).at[1, :320].set(gain_mlp)
    places = me_w * TOK + jnp.arange(TOK, dtype=jnp.int32)
    position = documents(doc_lengths, places)[1]
    cosine, sine = rope_tables(position)
    low = jnp.maximum(places - jnp.minimum(position, WINDOW - 1), 0) - (me_w - 2) * TOK
    low = jnp.broadcast_to(low.reshape(4, 1, 1, TILE), (4, 1, 4, TILE)).reshape(4, 1, 4 * TILE)

    def held(*shape, dtype=BF):
        return (shape, dtype, vmem())

    def far(*shape, dtype=BF):
        return (shape, dtype, hbm())

    def room(*shape, dtype=BF):
        return pltpu.VMEM(shape, dtype)

    def local(*arrays):
        return [(a, vmem()) for a in arrays]

    def remote(*arrays):
        return [(a, hbm()) for a in arrays]

    slots = room(7, OWN, D)
    (
        normed,
        queries,
        kv,
        lse,
        attended,
        w_a,
        x_rows,
        mid,
        normed_mid,
        inverse,
        gains,
        cot_pieces,
        full_gu,
        full_d,
    ) = exchange(
        "attention",
        1,
        attention,
        remote(packed(layer_input), packed(cotangent), gains_own, shard_a, shard_gu, w_down.T)
        + local(cosine, sine, low),
        [
            held(TOK, D),
            held(4, TILE, 4 * TILE),
            held(3 * TOK, 256),
            held(4, 1, 4 * TILE, dtype=F32),
            held(TOK, 320),
            held(D, PANEL),
            held(OWN, D, dtype=F32),
            held(OWN, D, dtype=F32),
            held(OWN, D),
            held(OWN, 128, dtype=F32),
            held(8, D, dtype=F32),
            far(8, TOK // 2, 640),
            far(D, 2 * PANEL),
            far(D, PANEL),
        ],
        [
            room(8, TOK // 2, 640),
            room(8, 8, 384, dtype=F32),
            room(TOK, D),
            room(512, TOK, dtype=F32),
            room(TOK, D),
            slots,
            room(OWN, D, dtype=F32),
            room(TILE, 3 * TOK),
        ],
    )
    grad_mid, grad_mid_own, down_part, grad_gu_sum, grad_d_part, gain_two_part = exchange(
        "mlp",
        2,
        mlp,
        local(normed_mid) + remote(full_d, full_gu, cot_pieces) + local(mid, inverse, gains),
        [
            held(TOK, D),
            held(OWN, D, dtype=F32),
            held(TOK, D),
            held(ROWS, 2 * PANEL, dtype=F32),
            far(D, PANEL),
            held(8, D, dtype=F32),
        ],
        [
            room(D, 2 * PANEL),
            room(D, PANEL),
            room(TOK, D),
            room(8, TOK // 2, 640),
            room(TOK, D),
            room(TOK, 2 * PANEL, dtype=F32),
            room(TOK, PANEL, dtype=F32),
            room(TOK, PANEL),
            room(TOK, 2 * PANEL),
            room(TOK, D),
            slots,
            room(OWN, D, dtype=F32),
            *wide_sum_scratch(2 * PANEL),
            room(OWN, D),
        ],
    )
    output_rows, grad_rows, gain_sums, grad_out, grad_qkv, grad_d = exchange(
        "attention_back",
        3,
        attention_back,
        local(grad_mid, grad_mid_own, attended, queries, kv, lse, low, w_a, normed)
        + local(cosine, sine, down_part)
        + remote(grad_d_part)
        + local(mid, x_rows, gains, gain_two_part),
        [
            far(8, OWN, 320),
            far(8, OWN, 320),
            held(8, 384, dtype=F32),
            held(ROWS, 384, dtype=F32),
            held(ROWS, 512, dtype=F32),
            held(ROWS, PANEL, dtype=F32),
        ],
        [
            room(D, PANEL),
            room(4, TILE, 4 * TILE),
            room(TILE, 3 * TOK),
            room(3 * TOK, 256, dtype=F32),
            room(320, TOK, dtype=F32),
            room(TOK, D),
            slots,
            slots,
            room(OWN, D, dtype=F32),
            room(OWN, D, dtype=F32),
            room(2 * TOK, 256),
            room(2, TOK, 256),
            room(TOK, 320, dtype=F32),
            room(D, 384),
            room(D, 512),
            room(8, OWN, 320),
            room(8, OWN, 320),
            room(8, 8, 384, dtype=F32),
            room(8, 8, 384, dtype=F32),
            room(16, 8, 384, dtype=F32),
            *wide_sum_scratch(PANEL),
            *wide_sum_scratch(384),
            *wide_sum_scratch(512),
            room(TOK, 512),
        ],
    )
    return (
        output_rows.reshape(TOK, 320),
        grad_rows.reshape(TOK, 320).astype(F32),
        gain_sums[0, :320],
        grad_qkv[:, :320],
        grad_qkv[:, 320:400],
        grad_qkv[:, 400:480],
        grad_out[:, :320].T,
        gain_sums[1, :320],
        grad_gu_sum[:, :PANEL],
        grad_gu_sum[:, PANEL:],
        grad_d.T,
    )


def solution(mesh):
    rows, columns = P("wide", "narrow"), P("narrow", "wide")
    return jax.shard_map(
        body,
        mesh=mesh,
        in_specs=(
            rows,
            P("narrow"),
            rows,
            rows,
            rows,
            columns,
            P("narrow"),
            rows,
            rows,
            columns,
            P(),
            rows,
        ),
        out_specs=(
            rows,
            rows,
            P("narrow"),
            rows,
            rows,
            rows,
            columns,
            P("narrow"),
            rows,
            rows,
            columns,
        ),
        check_vma=False,
    )
```

time: 518 us -> 361 us (0.70); the launches traced: 511 us -> 361 us
  matrix products: 87.7 us -> 0 us
  local copies, waits for them, and re-layouts: 56.8 us -> 17.2 us
  other arithmetic: 32.9 us -> 5.68 us
  Pallas kernels: 331 us -> 337 us
    dot_general x21 -> x0, matrix products: 87.7 us -> none  [the longest x5 22.7 us: dot(): return jnp.dot(a, b, preferred_element_type=F32)]
    unnamed x116 -> x19, local copies, waits for them, and re-layouts: 22.6 us -> 4.55 us
    another operation x7 -> x1, other arithmetic: 10.4 us -> 0.91 us
    reduce_sum x6 -> x0, other arithmetic: 6.49 us -> none  [the longest x2 2.76 us: norm_back(): return (through, jnp.sum(upstream * stream * inverse_rms, axis=0))]
    pallas_call x2 -> x0, local copies, waits for them, and re-layouts: 6.1 us -> none  [exchange(): pl.pallas_call(kernel, out_shape=[jax.ShapeDtypeStruct(shape, dtype) for...]
    pallas_call x9 -> x3, Pallas kernels: 331 us -> 337 us  [exchange(): pl.pallas_call(kernel, out_shape=[jax.ShapeDtypeStruct(shape, dtype) for...]
    transpose x3 -> x1, local copies, waits for them, and re-layouts: 7.05 us -> 1.71 us  [body(): grad_out[:, :320]]
where the time goes in v3:
time: 361 us
  Pallas kernels  337 us (93%)
  local copies, waits for them, and re-layouts  17.2 us (5%)
  other arithmetic  5.68 us (2%)
    pallas_call x3, Pallas kernels, exchange(): pl.pallas_call(kernel, out_shape=[jax.ShapeDtypeStruct(shape, dtype) for...  337 us

profile of v3, /device:TPU:1, one launch (start us, length us, event | category | flops | bytes accessed | tf_op | source)
XLA Modules:
  0.0 360.8 jit_solution(9307511043001552641)
XLA Ops:
  0.6 0.0 copy-start.2
  0.7 0.0 copy-start.3
  0.7 0.0 copy-start.4
  0.7 0.9 reduce-window.8
  1.6 0.7 reshape.169
  2.3 0.7 reshape.170
  3.0 0.7 select_reduce_fusion
  3.7 0.6 broadcast_in_dim.35
  4.4 0.2 scatter.9.refs_2_
  4.5 0.0 copy-start.5
  4.6 1.0 multiply_sine_fusion
  5.6 1.9 concatenate.18.refs_3_
  7.5 1.0 fusion.7
  8.5 0.2 copy.35
  8.7 0.2 copy.36
  8.8 0.0 copy-done.2
  8.9 0.2 copy.37
  9.1 0.2 copy.38
  9.2 1.0 pad_maximum_fusion.1
  10.3 0.0 copy-done.3
  10.3 0.0 copy-done.4
  10.3 0.9 pad_maximum_fusion.refs_4_
  11.1 0.0 copy-done.5
  11.1 130.0 %attention.1 = (bf16[512,2560]{1,0:T(8,128)(2,1)}, bf16[4,128,512]{2,1,0:T(8,128)(2,1)}, bf16[1536,256]{1,0:T(8,128)(2,1)}, f32[4,1,512]{2,1,0:T(1,128)}, bf16[5...) custom-call(bf16[256,640]{1,0:T(8,128)(2,1)} %get-tuple-element.121., ...), custom_call_target="tpu_custom_call" | custom-call | tf_op jit(solution)/shard_map/attention/pallas_call | solution.py:707
  141.2 98.8 %mlp.1 = (bf16[512,2560]{1,0:T(8,128)(2,1)}, f32[64,2560]{1,0:T(8,128)}, bf16[512,2560]{1,0:T(8,128)(2,1)}, f32[160,1792]{1,0:T(8,128)}, bf16[2560,896]{1,0:T(8,128)(2,1)}, /*index=5*/f32[8,2560]{1,0:T(8,128)}) custom-call(bf16[64,2560]{1,0:T(8,128)(2,1)} %get-tuple-element.61.refs_0_, bf16[2560,896]{1,0:T(8,128)(2,1)} %get-tuple-element.62.refs_1_, ...), custom_call_target="tpu_custom_call" | custom-call | tf_op jit(solution)/shard_map/mlp/pallas_call | solution.py:707
  240.0 108.3 %attention_back.1 = (bf16[8,64,320]{2,1,0:T(8,128)(2,1)}, bf16[8,64,320]{2,1,0:T(8,128)(2,1)}, f32[8,384]{1,0:T(8,128)}, f32[160,384]{1,0:T(8,128)}, f32[160,512]{1,0:T(8,128)}, /*index=5*/f32[160,896]{1,0:T(8,128)}) custom-call(bf16[512,2560]{1,0:T(8,128)(2,1)} %get-tuple-element.68.refs_0_, f32[64,2560]{1,0:T(8,128)} %get-tuple-element.69.refs_1_, ...), custom_call_target="tpu_custom_call" | custom-call | tf_op jit(solution)/shard_map/attention_back/pallas_call | solution.py:707
  348.3 0.0 copy-start
  348.3 2.0 copy.33
  350.3 1.4 slice_reduce_fusion
  351.7 1.8 fusion.5
  353.4 1.7 slice.76
  355.1 0.0 copy-start.1
  355.1 1.7 slice_bitcast_fusion
  356.8 1.0 bitcast_convert_fusion
  357.8 1.1 copy.34
  358.9 0.0 copy-done
  358.9 1.1 fusion.4
  360.0 0.0 copy-done.1
  360.0 0.8 copy.41
  (8 shorter events, 0.1 us)
Async XLA Ops:
  0.6 8.2 %copy-start.2 = (bf16[512,320]{0,1:T(8,128)(2,1)S(1)}, bf16[512,320]{0,1:T(8,128)(2,1)}, u32[]{:S(2)}) copy-start(bf16[512,320]{0,1:T(8,128)(2,1)} %param.27) | copy-start | bytes 983044
  0.7 9.6 %copy-start.3 = (bf16[160,896]{1,0:T(8,128)(2,1)S(1)}, bf16[160,896]{1,0:T(8,128)(2,1)}, u32[]{:S(2)}) copy-start(bf16[160,896]{1,0:T(8,128)(2,1)} %param.24) | copy-start | bytes 860164
  0.7 9.6 %copy-start.4 = (bf16[160,896]{1,0:T(8,128)(2,1)S(1)}, bf16[160,896]{1,0:T(8,128)(2,1)}, u32[]{:S(2)}) copy-start(bf16[160,896]{1,0:T(8,128)(2,1)} %param.23) | copy-start | bytes 860164
  4.5 6.6 %copy-start.5 = (f32[8,384]{1,0:T(8,128)}, f32[8,384]{1,0:T(8,128)S(1)}, u32[]{:S(2)}) copy-start(f32[8,384]{1,0:T(8,128)S(1)} %scatter.9.refs_2_) | copy-start | bytes 36868
  348.3 10.6 %copy-start = (f32[160,1792]{1,0:T(8,128)S(1)}, f32[160,1792]{1,0:T(8,128)}, u32[]{:S(2)}) copy-start(f32[160,1792]{1,0:T(8,128)} %get-tuple-element.85) | copy-start | bytes 3440644
  355.1 4.9 %copy-start.1 = (f32[160,896]{1,0:T(8,128)S(1)}, f32[160,896]{1,0:T(8,128)}, u32[]{:S(2)}) copy-start(f32[160,896]{1,0:T(8,128)} %get-tuple-element.86) | copy-start | bytes 1720324

commit v4 on v3

v4 whole, which is shorter than its diff:
```python
import functools
import math

import jax
import jax.numpy as jnp
import numpy as np
from jax import lax
from jax.experimental import pallas as pl
from jax.experimental.pallas import tpu as pltpu
from jax.sharding import PartitionSpec as P

D = 2560
HEADS = 32
KV_HEADS = 8
HEAD = 80
WINDOW = 1024
TOK = 512
OWN = 64
ROWS = 160
PANEL = 896
TILE = 128
REACH = WINDOW + TILE

epsilon = 1e-05
rope_base = 1000000.0
rope_factor = 8.0
long_wave = 8192.0
short_wave = 2048.0
masked = -1e30

MESH = pl.DeviceIdType.MESH
BF = jnp.bfloat16
F32 = jnp.float32


class Place:
    def __init__(self):
        self.w = lax.axis_index("wide")
        self.n = lax.axis_index("narrow")
        self.z, self.h, self.c = self.w // 4, (self.w // 2) % 2, self.w % 2
        self.x, self.l = self.n // 2, self.n % 2

    def wide(self, dz, dh, dc):
        return ((self.z + dz) % 4) * 4 + ((self.h + dh) % 2) * 2 + (self.c + dc) % 2

    def narrow(self, dx, dl):
        return ((self.x + dx) % 4) * 2 + (self.l + dl) % 2

    def narrow_peers(self):
        return [(self.w, self.narrow(k // 2, k % 2)) for k in (2, 6, 1, 3, 7, 4, 5)]

    def wide_peers(self):
        return [(self.wide(*d), self.n) for d in ((0, 1, 0), (1, 0, 0), (3, 0, 0), (2, 0, 0), (0, 0, 1))]


class Net:
    def __init__(self, place, send_sems, recv_sems, local_sems):
        self.at = place
        self.sems = (send_sems, recv_sems, local_sems)
        self.sent, self.kept, self.open, self.done = [], [], [], 0

    def barrier(self, givers, takers):
        bar = pltpu.get_barrier_semaphore()
        for device in givers:
            pl.semaphore_signal(bar, inc=1, device_id=device, device_id_type=MESH)
        pl.semaphore_wait(bar, takers)

    def send(self, src, dst, device):
        i = len(self.sent)
        copy = pltpu.make_async_remote_copy(
            src_ref=src,
            dst_ref=dst,
            send_sem=self.sems[0].at[i],
            recv_sem=self.sems[1].at[i],
            device_id=device,
            device_id_type=MESH,
        )
        copy.start()
        self.sent.append(copy)
        return copy

    def keep(self, src, dst):
        copy = pltpu.make_async_copy(src, dst, self.sems[2].at[len(self.kept)])
        copy.start()
        self.kept.append(copy)
        self.open.append(copy)
        return copy

    def settle(self, *copies):
        for copy in copies:
            copy.wait()
            self.open = [c for c in self.open if c is not copy]

    def release(self, count):
        for copy in self.sent[self.done : count]:
            copy.wait_send()
        self.done = count

    def run(self, tasks):
        tasks = list(tasks)
        while tasks:
            left = []
            for task in tasks:
                try:
                    next(task)
                    left.append(task)
                except StopIteration:
                    pass
            tasks = left
        for copy in self.sent[self.done :]:
            copy.wait_send()
        for copy in self.open:
            copy.wait()


def block_of(ref, index, rows):
    return ref.at[pl.ds(pl.multiple_of(index * rows, 16), rows)]


def narrow_gather(net, src, dst, cut, stacked=False):
    at = net.at
    me, near = at.n, at.narrow(0, 1)
    rows = src.shape[0]

    def block(n):
        return dst.at[n] if stacked else block_of(dst, n, rows)

    kept = net.keep(src, block(me))
    late = net.send(src.at[cut:], block(me).at[cut:], (at.w, near))
    turns = [(d, net.send(src, block(me), (at.w, at.narrow(d, 0)))) for d in (1, 3, 2)]
    early = net.send(src.at[:cut], block(me).at[:cut], (at.w, near))
    yield
    late.wait_recv()
    rest = [
        net.send(block(near).at[cut:], block(near).at[cut:], (at.w, at.narrow(d, 0)))
        for d in (1, 3, 2)
    ]
    yield
    for d, copy in turns:
        copy.wait_recv()
        part = block(at.narrow(-d, 0)).at[:cut]
        rest.append(net.send(part, part, (at.w, near)))
    yield
    early.wait_recv()
    for copy in rest:
        copy.wait_recv()
    net.settle(kept)


def narrow_share(net, src, dst):
    me = net.at.n
    copies = [net.send(src, dst.at[me], peer) for peer in net.at.narrow_peers()]
    kept = net.keep(src, dst.at[me])
    yield
    yield
    for copy in copies:
        copy.wait_recv()
    net.settle(kept)


def narrow_swap(net, src, dst):
    me = net.at.n
    copies = [net.send(src.at[peer[1]], dst.at[me], peer) for peer in net.at.narrow_peers()]
    kept = net.keep(src.at[me], dst.at[me])
    yield
    for copy in copies:
        copy.wait_recv()
    net.settle(kept)


def add_rows(rows, step, dst, terms):
    @pl.loop(0, rows // step)
    def _(i):
        part = pl.ds(pl.multiple_of(i * step, step), step)
        total = terms[0][part, :].astype(F32)
        for term in terms[1:]:
            total += term[part, :].astype(F32)
        dst[part, :] = total.astype(dst.dtype)


def narrow_sum(net, src, slots, out, cut, held=None):
    at = net.at
    me, near = at.n, at.narrow(0, 1)
    rows = out.shape[0]

    def block(n):
        return block_of(src, n, rows)

    def term_of(n):
        return block_of(src if held is None else held, n, rows)

    over = {
        d: net.send(block(at.narrow(d, 1)).at[:cut], slots.at[d - 1, :cut], (at.w, near))
        for d in (1, 3, 2)
    }
    across = {
        d: net.send(block(at.narrow(d, 1)).at[cut:], slots.at[d - 1, cut:], (at.w, at.narrow(d, 0)))
        for d in (1, 3, 2)
    }
    late = [
        net.send(block(at.narrow(d, 0)).at[cut:], slots.at[2 + d, cut:], (at.w, at.narrow(d, 0)))
        for d in (1, 3, 2)
    ]
    final = [net.send(block(near).at[:cut], slots.at[6, :cut], (at.w, near))]
    yield
    early = []
    for d in (1, 3, 2):
        over[d].wait_recv()
        term = slots.at[d - 1, :cut]
        add_rows(cut, 16, term, [term, term_of(at.narrow(d, 0)).at[:cut]])
        early.append(net.send(term, slots.at[2 + d, :cut], (at.w, at.narrow(d, 0))))
    yield
    for d in (1, 3, 2):
        across[d].wait_recv()
    term = slots.at[0, cut:]
    add_rows(rows - cut, 16, term, [term_of(near).at[cut:], *(slots.at[k, cut:] for k in range(3))])
    final.append(net.send(term, slots.at[6, cut:], (at.w, near)))
    yield
    for copy in late + early + final:
        copy.wait_recv()
    add_rows(rows, 16, out, [term_of(me), *(slots.at[k] for k in range(3, 7))])


def wide_gather(net, src, dst):
    at = net.at
    half = ROWS // 2
    me, far = at.w, at.wide(0, 1, 0)
    up, down = (at.wide(1, 0, 0), at.n), (at.wide(3, 0, 0), at.n)
    other = (at.wide(0, 0, 1), at.n)

    def block(w):
        return block_of(dst, w, ROWS)

    kept = net.keep(src, block(me))
    turns = [[net.send(src, block(me), up), net.send(src, block(me), down)]]
    over = [net.send(src, block(me), other)]
    further = []

    def relay(e):
        for d, part, ahead, copy in (
            (3, slice(0, half), up, turns[e][0]),
            (1, slice(half, ROWS), down, turns[e][1]),
        ):
            copy.wait_recv()
            shard = block(at.wide(d, e, 0))
            further.append((e, part, net.send(shard.at[part], shard.at[part], ahead)))
            over.append(net.send(shard, shard, other))

    yield
    from_far = net.send(src, block(me), (far, at.n))
    yield
    relay(0)
    yield
    from_far.wait_recv()
    turns.append([net.send(block(far), block(far), up), net.send(block(far), block(far), down)])
    over.append(net.send(block(far), block(far), other))
    yield
    relay(1)
    yield
    for e, part, copy in further:
        copy.wait_recv()
        shard = block(at.wide(2, e, 0)).at[part]
        over.append(net.send(shard, shard, other))
    yield
    for copy in over:
        copy.wait_recv()
    net.settle(kept)


def wide_sum(net, src, core, turned, last, outs, held=None):
    at = net.at
    half = ROWS // 2
    up, down = (at.wide(1, 0, 0), at.n), (at.wide(3, 0, 0), at.n)
    other = (at.wide(0, 0, 1), at.n)
    order = [(d, e) for d in (2, 1, 3, 0) for e in (1, 0)]

    def block(w):
        return block_of(src, w, ROWS)

    over = {(d, e): net.send(block(at.wide(d, e, 1)), core.at[d, e], other) for d, e in order}
    yield
    further = []
    for d, e in order:
        over[d, e].wait_recv()
        part = core.at[d, e]
        add_rows(ROWS, 32, part, [part, block(at.wide(d, e, 0)) if held is None else held.at[d, e]])
        if d == 2:
            further.append(
                (
                    e,
                    net.send(part.at[:half], turned.at[2, e, :half], up),
                    net.send(part.at[half:], turned.at[2, e, half:], down),
                )
            )
    yield
    turns = []
    for e, first, second in further:
        first.wait_recv()
        part = core.at[1, e]
        add_rows(half, 16, part.at[:half], [part.at[:half], turned.at[2, e, :half]])
        turns.append((e, net.send(part, turned.at[0, e], up)))
        second.wait_recv()
        part = core.at[3, e]
        add_rows(half, 16, part.at[half:], [part.at[half:], turned.at[2, e, half:]])
        turns.append((e, net.send(part, turned.at[1, e], down)))
        yield
    for e, copy in turns:
        if e:
            copy.wait_recv()
    part = core.at[0, 1]
    add_rows(ROWS, 32, part, [part, turned.at[0, 1], turned.at[1, 1]])
    final = net.send(part, last, (at.wide(0, 1, 0), at.n))
    yield
    for e, copy in turns:
        if not e:
            copy.wait_recv()
    final.wait_recv()

    @pl.loop(0, ROWS // 32)
    def _(i):
        part = pl.ds(pl.multiple_of(i * 32, 32), 32)
        total = core[0, 0, part, :].astype(F32) + last[part, :].astype(F32)
        for d in range(2):
            total += turned[d, 0, part, :].astype(F32)
        for out, first, columns in outs:
            out[part, :] = total[:, first : first + columns]


def step(*tasks):
    for task in tasks:
        next(task, None)


def finish(*tasks):
    tasks = list(tasks)
    while tasks:
        tasks = [task for task in tasks if next(task, "end") != "end"]


def pieces_of(width, size, body):
    whole = width // size

    @pl.loop(0, whole)
    def _(i):
        body(pl.ds(pl.multiple_of(i * size, size), size))

    if width % size:
        body(pl.ds(whole * size, width % size))


def dot(a, b):
    return jnp.dot(a, b, preferred_element_type=F32)


def dot_t(a, b):
    return lax.dot_general(a, b, (((1,), (1,)), ((), ())), preferred_element_type=F32)


def t_dot(a, b):
    return lax.dot_general(a, b, (((0,), (0,)), ((), ())), preferred_element_type=F32)


def scores(keys, queries, low, first):
    raw = dot(keys, queries) * (1.0 / math.sqrt(HEAD))
    key = first + lax.broadcasted_iota(jnp.int32, raw.shape, 0)
    query = first + WINDOW + lax.broadcasted_iota(jnp.int32, raw.shape, 1) % TILE
    return jnp.where((key >= low) & (key <= query), raw, masked)


def by_feature(dst, rows):
    for j in range(8):
        dst[j] = rows[:, j * 320 : (j + 1) * 320]


def every(size, body):
    @pl.loop(0, D // size)
    def _(i):
        body(pl.ds(pl.multiple_of(i * size, size), size))


def attention(net, ins, outs, scratch):
    x_own, cot_own, w_query, w_key, w_value, w_out, w_gate, w_up, gain_one, gain_two, freqs, lengths = ins
    normed_far, w_qkv_far, w_out_far, cot, w_gu = outs[:5]
    queries, kv, lse, low, tables, attended, x_rows, mid, normed_mid, inverse, gains = outs[5:]
    (
        shard_qkv,
        shard_out,
        shard_gu,
        gains_own,
        gain_pieces,
        w_qkv,
        w_o,
        x_t,
        x,
        normed,
        qkv,
        src,
        slots,
        total,
        values_t,
    ) = scratch
    at = net.at
    later = [((at.w + k) % 16, at.n) for k in (1, 2)]
    earlier = [((at.w + 16 - k) % 16, at.n) for k in (1, 2)]
    shard_qkv[:, :320] = w_query[...]
    shard_qkv[:, 320:] = jnp.concatenate(
        [w_key[...], w_value[...], jnp.zeros((ROWS, 32), BF)], axis=1
    )
    gains_own[...] = jnp.zeros(gains_own.shape, F32)
    gains_own[0:1, :320] = gain_one[...].reshape(1, 320)
    gains_own[1:2, :320] = gain_two[...].reshape(1, 320)
    net.barrier(at.narrow_peers() + at.wide_peers() + earlier, 14)
    panel = wide_gather(net, shard_qkv, w_qkv)
    step(panel, panel)
    stream = narrow_gather(net, x_own, x_t, 160)
    sizes = narrow_share(net, gains_own, gain_pieces)
    step(stream, sizes)
    shard_out[...] = jnp.concatenate([w_out[...], jnp.zeros((ROWS, 64), BF)], axis=1)
    shard_gu[:, :PANEL] = w_gate[...]
    shard_gu[:, PANEL:] = w_up[...]

    place = at.w * TOK + lax.broadcasted_iota(jnp.int32, (1, TOK), 1)
    begins, end = jnp.zeros((1, TOK), jnp.int32), 0
    for k in range(8):
        end = end + lengths[k]
        begins = jnp.where(place >= end, end, begins)
    position = place - begins
    angles = freqs[:, 0:1] * position.astype(F32)
    cos, sin = jnp.cos(angles), jnp.sin(angles)
    tables[0], tables[1] = cos, sin
    first_key = jnp.maximum(begins, jnp.maximum(place - (WINDOW - 1), 0)) - (at.w - 2) * TOK
    for tile in range(4):
        one = first_key[:, tile * TILE : (tile + 1) * TILE]
        low[tile] = jnp.concatenate([one] * 4, axis=1)

    step(stream, panel, panel, panel)
    w_outs = wide_gather(net, shard_out, w_o)
    gate_up = wide_gather(net, shard_gu, w_gu)
    step(w_outs, w_outs, gate_up, stream, panel)
    finish(stream, sizes, panel)
    step(gate_up)
    for j in range(8):
        gains[:, pl.ds(j * 320, 320)] = gain_pieces[j, :, :320]
    every(256, lambda rows: turned_over(x, x_t, rows))

    @pl.loop(0, TOK // 16)
    def _(i):
        rows = pl.ds(pl.multiple_of(i * 16, 16), 16)
        part = x[rows, :].astype(F32)
        inv = lax.rsqrt(jnp.mean(part * part, axis=1, keepdims=True) + epsilon)
        normed[rows, :] = (part * inv * gains[0:1, :]).astype(BF)

    for h in range(2):
        x_rows[pl.ds(h * 32, 32), :] = x[own_rows(at, h), :].astype(F32)
    for k in range(2):
        part = pl.ds(k * 256, 256)
        qkv[part, :] = dot(normed[...], w_qkv[:, part]).T
    zeros = jnp.zeros((48, TOK), F32)

    def turned(at_row):
        a, b = qkv[pl.ds(at_row, 40), :], qkv[pl.ds(at_row + 40, 40), :]
        return jnp.concatenate([a * cos - b * sin, b * cos + a * sin, zeros], axis=0)

    mine = pl.ds(2 * TOK, TOK)
    kv[mine, :128] = turned(320).T.astype(BF)
    kv[mine, 128:] = jnp.concatenate([qkv[pl.ds(400, 80), :], zeros], axis=0).T.astype(BF)
    arriving = [
        net.send(kv.at[mine], kv.at[pl.ds((2 - k) * TOK, TOK)], later[k - 1]) for k in (1, 2)
    ]
    cots = narrow_gather(net, cot_own, cot, 160)
    step(cots)
    net.keep(normed, normed_far)
    net.keep(w_qkv, w_qkv_far)
    for head in range(4):
        one = turned(head * HEAD).astype(BF)
        for tile in range(4):
            queries[tile, :, pl.ds(head * TILE, TILE)] = one[:, tile * TILE : (tile + 1) * TILE]
    step(w_outs, w_outs)
    for copy in arriving:
        copy.wait_recv()
    step(w_outs)
    values_t[...] = kv[:, 128:].T

    def one_tile(i):
        first = pl.multiple_of(i * TILE, TILE)
        seen = pl.ds(first, REACH)
        s = scores(kv[seen, :128], queries[i], low[i], first)
        largest = jnp.max(s, axis=0, keepdims=True)
        powers = jnp.exp(s - largest)
        totals = jnp.sum(powers, axis=0, keepdims=True)
        weights = (powers / totals).astype(BF)
        lse[i] = largest + jnp.log(totals)
        mixed = dot(values_t[:, seen], weights)
        attended[pl.ds(first, TILE), :] = (
            jnp.concatenate([mixed[:HEAD, h * TILE : (h + 1) * TILE] for h in range(4)], axis=0)
            .T.astype(BF)
        )

    def out_part(h):
        tokens = pl.ds(h * 256, 256)

        def columns(rows):
            src[tokens, rows] = dot_t(attended[tokens, :], w_o[rows, :320]).astype(BF)

        every(256, columns)
        return narrow_sum(
            net, src.at[tokens], slots.at[h], total.at[pl.ds(h * 32, 32)], 16
        )

    def norm_part(h):
        rows = pl.ds(h * 32, 32)
        stream = x_rows[rows, :] + total[rows, :]
        mid[rows, :] = stream
        inv = lax.rsqrt(jnp.mean(stream * stream, axis=1, keepdims=True) + epsilon)
        inverse[rows, :] = jnp.broadcast_to(inv, (32, 128))
        normed_mid[rows, :] = (stream * inv * gains[1:2, :]).astype(BF)

    step(gate_up)
    pl.loop(0, 2)(one_tile)
    finish(w_outs)
    net.keep(w_o, w_out_far)
    early = out_part(0)
    step(early, gate_up, cots)
    pl.loop(2, 4)(one_tile)
    step(early)
    late = out_part(1)
    step(late, early, gate_up, late, cots)
    finish(early)
    norm_part(0)
    step(late, gate_up)
    finish(late)
    norm_part(1)
    finish(cots, gate_up)
    net.run([])


def own_rows(at, h):
    return pl.ds(pl.multiple_of(h * 256 + at.n * 32, 32), 32)


def turned_over(dst, src, rows):
    dst[:, rows] = src[rows, :].T


def mlp(net, ins, outs, scratch):
    normed_own, w_down, gu_far, cot_far, mid, inverse, gains = ins
    grad_mid_far, grad_mid, down_far, grad_gate, du_far, gain_part = outs
    shard_d, w_gu, w_d, normed, cot_t, cot, gu, grad_hidden, hidden, grad_pre, src = scratch[:11]
    down_part, slots, total, core, turned, last, low, grad_mid_full = scratch[11:]
    at = net.at
    shard_d[...] = w_down[...]
    net.barrier(at.narrow_peers() + at.wide_peers(), 12)
    tokens = [pl.ds(0, 256), pl.ds(256, 256)]
    own = [pl.ds(0, 32), pl.ds(32, 32)]
    gathers = [narrow_gather(net, normed_own.at[own[h]], normed.at[tokens[h]], 16) for h in (0, 1)]
    panel = wide_gather(net, shard_d, w_d)
    step(panel, gathers[0], panel)
    cots, weights = net.keep(cot_far, cot_t), net.keep(gu_far, w_gu)
    step(gathers[0], gathers[1])
    net.settle(cots)
    every(256, lambda rows: turned_over(cot, cot_t, rows))
    step(panel, gathers[1], panel, gathers[0], panel)
    net.settle(weights)
    finish(gathers[0])

    def gate_up(h):
        def part(columns):
            gu[tokens[h], columns] = dot(normed[tokens[h], :], w_gu[:, columns])

        pieces_of(2 * PANEL, 256, part)

    def back_down(h):
        def part(columns):
            grad_hidden[tokens[h], columns] = dot(cot[tokens[h], :], w_d[:, columns])

        pieces_of(PANEL, 256, part)

    def back_hidden(h):
        @pl.loop(h * 16, h * 16 + 16)
        def _(i):
            rows = pl.ds(pl.multiple_of(i * 16, 16), 16)
            gate, up, grad = gu[rows, :PANEL], gu[rows, PANEL:], grad_hidden[rows, :]
            sigmoid = jax.nn.sigmoid(gate)
            active = gate * sigmoid
            hidden[rows, :] = (active * up).astype(BF)
            grad_pre[rows, :PANEL] = (
                grad * up * sigmoid * (1.0 + gate * (1.0 - sigmoid))
            ).astype(BF)
            grad_pre[rows, PANEL:] = (grad * active).astype(BF)

    def back_normed(h):
        def part(rows):
            src[tokens[h], rows] = dot_t(grad_pre[tokens[h], :], w_gu[rows, :]).astype(BF)

        every(256, part)
        return narrow_sum(net, src.at[tokens[h]], slots.at[h], total.at[own[h]], 16)

    def back_norm(h):
        inv, scale = inverse[own[h], :1], gains[1:2, :]
        grad, stream = total[own[h], :], mid[own[h], :]
        weighted = grad * scale
        inner = jnp.sum(weighted * stream, axis=1, keepdims=True)
        through = inv * weighted - stream * (inv * inv * inv * inner / D)
        mine = cot[own_rows(at, h), :].astype(F32) + through
        grad_mid[own[h], :] = mine
        low[own[h], :] = mine.astype(BF)
        return narrow_gather(net, low.at[own[h]], grad_mid_full.at[tokens[h]], 16)

    gate_up(0)
    step(gathers[1], panel)
    finish(panel)
    gathered = len(net.sent)
    back_down(0)
    back_hidden(0)
    sums = [back_normed(0)]
    step(sums[0])
    finish(gathers[1])
    gate_up(1)
    step(sums[0])
    back_down(1)
    back_hidden(1)
    sums.append(back_normed(1))
    step(sums[1], sums[0])

    def grad_gate_rows(rows):
        w_gu[rows, :PANEL] = t_dot(normed[:, rows], grad_pre[:, :PANEL]).astype(BF)

    every(256, grad_gate_rows)
    wide = wide_sum(net, w_gu.at[:, pl.ds(0, PANEL)], core, turned, last, [(grad_gate, 0, PANEL)])
    step(wide, sums[1])
    finish(sums[0])
    back = [back_norm(0)]
    step(back[0], sums[1])

    def grad_up_rows(rows):
        w_gu[rows, PANEL:] = t_dot(normed[:, rows], grad_pre[:, PANEL:]).astype(BF)

    every(256, grad_up_rows)
    net.keep(w_gu.at[:, pl.ds(PANEL, PANEL)], du_far.at[:, pl.ds(PANEL, PANEL)])
    finish(sums[1])
    back.append(back_norm(1))
    step(back[0], back[1], wide)

    def forward_down(rows):
        down_part[:, rows] = dot_t(hidden[...], w_d[rows, :]).astype(BF)

    every(256, forward_down)
    net.keep(down_part, down_far)
    step(back[1], back[0], wide)
    net.release(gathered)

    def grad_d_rows(rows):
        w_d[rows, :] = dot(cot_t[rows, :], hidden[...]).astype(BF)

    every(256, grad_d_rows)
    net.keep(w_d, du_far.at[:, pl.ds(0, PANEL)])
    finish(back[0])
    step(back[1], wide)
    grad, stream = total[...], mid[...]
    gain_part[...] = jnp.broadcast_to(
        jnp.sum(grad * stream * inverse[:, :1], axis=0, keepdims=True), gain_part.shape
    )
    finish(back[1])
    net.keep(grad_mid_full, grad_mid_far)
    finish(wide)
    net.run([])


def attention_back(net, ins, outs, scratch):
    grad_mid_far, normed_far, w_qkv_far, w_out_far, down_far, du_far = ins[:6]
    grad_mid_own, attended, queries, kv, lse, low, tables, mid, x_rows, gains, gain_two_part = ins[6:]
    back_one, back_two, wide_parts, grad_out, grad_query, grad_key, grad_value, grad_d, grad_up = outs
    grad_mid, normed, w_qkv, w_o, down_part, held_du = scratch[:6]
    upstream, keys_t, grad_kv, grad_q, slots_one, slots_two, total_one, total_two = scratch[6:14]
    later_kv, turned_back, ga, rows_one, rows_two, parts, narrow_parts, grads_ref = scratch[14:22]
    sum_du, sum_out, sum_qkv = scratch[22:25], scratch[25:28], scratch[28:31]
    at = net.at
    tokens = [pl.ds(0, 256), pl.ds(256, 256)]
    own = [pl.ds(0, 32), pl.ds(32, 32)]
    loads = [net.keep(a, b) for a, b in zip(ins[:5], (grad_mid, normed, w_qkv, w_o, down_part))]
    held_loads = [
        net.keep(block_of(du_far, at.wide(d, e, 0), ROWS), held_du.at[d, e])
        for d in range(4)
        for e in range(2)
    ]
    everyone = [((at.w + k) % 16, at.n) for k in range(1, 16)]
    net.barrier(at.narrow_peers() + everyone, 22)
    wide_du = wide_sum(
        net, du_far, *sum_du, [(grad_d, 0, PANEL), (grad_up, PANEL, PANEL)], held_du
    )
    downs = [
        narrow_sum(
            net, down_far.at[tokens[h]], slots_one.at[h], total_one.at[own[h]], 16, down_part.at[tokens[h]]
        )
        for h in (0, 1)
    ]
    step(wide_du, *downs)
    net.settle(loads[0], loads[3])
    for first, columns in ((0, 256), (256, 64)):
        ga[:, pl.ds(first, columns)] = dot(grad_mid[...], w_o[:, pl.ds(first, columns)])
    grads_t = ga[...].T
    zeros = jnp.zeros((48, TOK), F32)
    for head in range(4):
        one = jnp.concatenate([grads_t[head * HEAD : (head + 1) * HEAD], zeros], axis=0).astype(BF)
        for tile in range(4):
            upstream[tile, :, pl.ds(head * TILE, TILE)] = one[:, tile * TILE : (tile + 1) * TILE]
    keys_t[...] = kv[:, :128].T
    net.settle(loads[4], *held_loads)
    step(wide_du, *downs)
    fill = jnp.zeros((256, 64), F32)

    def grad_out_rows(rows):
        w_o[rows, :] = jnp.concatenate(
            [t_dot(grad_mid[:, rows], attended[...]), fill], axis=1
        ).astype(BF)

    every(256, grad_out_rows)
    wide_out = wide_sum(net, w_o, *sum_out, [(grad_out, 0, 320)])
    step(wide_out)
    grad_kv[...] = jnp.zeros(grad_kv.shape, F32)
    factor = 1.0 / math.sqrt(HEAD)

    def one_tile(i):
        first = pl.multiple_of(i * TILE, TILE)
        seen = pl.ds(first, REACH)
        s = scores(kv[seen, :128], queries[i], low[i], first)
        weights = jnp.exp(s - lse[i])
        grad_weights = dot(kv[seen, 128:], upstream[i])
        inner = jnp.sum(weights * grad_weights, axis=0, keepdims=True)
        grad_scores = (weights * (grad_weights - inner)).astype(BF)
        grad_kv[seen, 128:] += dot_t(weights.astype(BF), upstream[i])
        grad_kv[seen, :128] += dot_t(grad_scores, queries[i]) * factor
        back = dot(keys_t[:, seen], grad_scores) * factor
        for head in range(4):
            grad_q[pl.ds(head * HEAD, HEAD), pl.ds(first, TILE)] = back[
                :HEAD, head * TILE : (head + 1) * TILE
            ]

    pl.loop(0, 2)(one_tile)
    step(*downs, wide_du)
    pl.loop(2, 4)(one_tile)
    later_kv[...] = grad_kv[pl.ds(0, 2 * TOK), :].astype(BF)
    arriving = [
        net.send(
            later_kv.at[pl.ds((2 - k) * TOK, TOK)],
            turned_back.at[2 - k],
            ((at.w + 16 - k) % 16, at.n),
        )
        for k in (1, 2)
    ]
    cos, sin = tables[0], tables[1]

    def unturned(part):
        a, b = part[:40], part[40:80]
        return [a * cos + b * sin, b * cos - a * sin]

    rotated = []
    for head in range(4):
        rotated += unturned(grad_q[pl.ds(head * HEAD, HEAD), :])
    step(wide_du, wide_out)
    finish(*downs)
    by_feature(rows_one, (mid[...] + total_one[...]).astype(BF))
    output_rows = narrow_swap(net, rows_one, back_one)
    step(output_rows)
    for copy in arriving:
        copy.wait_recv()
    whole = (
        grad_kv[pl.ds(2 * TOK, TOK), :]
        + turned_back[0].astype(F32)
        + turned_back[1].astype(F32)
    )
    rotated += unturned(whole[:, :128].T)
    rotated += [whole[:, 128:].T[:HEAD], jnp.zeros((32, TOK), F32)]
    grads_ref[...] = jnp.concatenate(rotated, axis=0).T.astype(BF)
    net.settle(loads[2])

    def back_normed(h):
        def part(rows):
            down_part[tokens[h], rows] = dot_t(grads_ref[tokens[h], :], w_qkv[rows, :]).astype(BF)

        every(256, part)
        return narrow_sum(net, down_part.at[tokens[h]], slots_two.at[h], total_two.at[own[h]], 16)

    sums = [back_normed(0)]
    step(sums[0])
    sums.append(back_normed(1))
    step(sums[1])
    net.settle(loads[1])

    def grad_qkv_rows(rows):
        w_qkv[rows, :] = t_dot(normed[:, rows], grads_ref[...]).astype(BF)

    step(sums[0])
    every(256, grad_qkv_rows)
    wide_qkv = wide_sum(
        net, w_qkv, *sum_qkv, [(grad_query, 0, 320), (grad_key, 320, 80), (grad_value, 400, 80)]
    )
    step(wide_qkv, sums[1], sums[0], wide_out, wide_qkv, sums[1], wide_du)
    finish(sums[0])
    finish(sums[1])
    stream, grad = x_rows[...], total_two[...]
    inv = lax.rsqrt(jnp.mean(stream * stream, axis=1, keepdims=True) + epsilon)
    weighted = grad * gains[0:1, :]
    inner = jnp.sum(weighted * stream, axis=1, keepdims=True)
    through = inv * weighted - stream * (inv * inv * inv * inner / D)
    by_feature(rows_two, (grad_mid_own[...] + through).astype(BF))
    back = narrow_swap(net, rows_two, back_two)
    step(back)
    gain_one = jnp.sum(grad * stream * inv, axis=0, keepdims=True)
    both = jnp.concatenate([gain_one, gain_two_part[0:1, :], jnp.zeros((6, D), F32)], axis=0)
    for j in range(8):
        parts[j, :, :320] = both[:, j * 320 : (j + 1) * 320]
        parts[j, :, 320:] = jnp.zeros((8, 64), F32)
    me = at.n
    copies = [net.send(parts.at[p[1]], narrow_parts.at[me], p) for p in at.narrow_peers()]
    narrow_parts[me] = parts[me]
    step(wide_out, wide_qkv, wide_du)
    for copy in copies:
        copy.wait_recv()
    sum_parts = narrow_parts[0]
    for k in range(1, 8):
        sum_parts += narrow_parts[k]
    wide_parts[0] = sum_parts
    copies = [
        net.send(wide_parts.at[0], wide_parts.at[k + 1], p) for k, p in enumerate(everyone)
    ]
    step(wide_out, wide_qkv, wide_du)
    finish(wide_out, wide_qkv, wide_du)
    for copy in copies:
        copy.wait_recv()
    finish(back, output_rows)
    net.run([])


def closing(*refs):
    ins, outs = refs[:10], refs[10:]
    for rows, out in ((ins[0], outs[0]), (ins[1], outs[1])):
        halves = [rows[:, pl.ds(h * 32, 32), :].reshape(256, 320) for h in (0, 1)]
        out[...] = jnp.concatenate(halves, axis=0).astype(F32).T.astype(out.dtype)
    total = ins[2][0]
    for k in range(1, 16):
        total += ins[2][k]
    outs[2][...] = total[0:1, :320].reshape(320)
    outs[3][...] = total[1:2, :320].reshape(320)
    for source, out in zip(ins[3:], outs[4:]):
        out[...] = source[...]


def wide_sum_scratch(columns):
    return [
        pltpu.VMEM((4, 2, ROWS, columns), BF),
        pltpu.VMEM((3, 2, ROWS, columns), BF),
        pltpu.VMEM((ROWS, columns), BF),
    ]


def vmem():
    return pl.BlockSpec(memory_space=pltpu.VMEM)


def hbm():
    return pl.BlockSpec(memory_space=pl.ANY)


def exchange(name, number, body, ins, outs, scratch=(), sends=200, keeps=24):
    def kernel(*refs):
        a, b = len(ins), len(ins) + len(outs)
        net = Net(Place(), *refs[-3:])
        body(net, refs[:a], refs[a:b], refs[b:-3])

    return pl.pallas_call(
        kernel,
        out_shape=[jax.ShapeDtypeStruct(shape, dtype) for shape, dtype, _ in outs],
        in_specs=[spec for _, spec in ins],
        out_specs=[spec for _, _, spec in outs],
        scratch_shapes=[
            *scratch,
            pltpu.SemaphoreType.DMA((sends,)),
            pltpu.SemaphoreType.DMA((sends,)),
            pltpu.SemaphoreType.DMA((keeps,)),
        ],
        compiler_params=pltpu.CompilerParams(
            collective_id=number, has_side_effects=True, vmem_limit_bytes=60 * 2**20
        ),
        name=name,
    )(*[array for array, _ in ins])


def scaled_freqs():
    freqs = (rope_base ** (-2.0 * np.arange(HEAD // 2) / HEAD)).astype(np.float32)
    wavelen = (2.0 * math.pi / freqs).astype(np.float32)
    smooth = (long_wave / wavelen - 1.0) / 3.0
    blended = (1.0 - smooth) * freqs / rope_factor + smooth * freqs
    return np.where(
        wavelen < short_wave, freqs, np.where(wavelen > long_wave, freqs / rope_factor, blended)
    ).astype(np.float32)


def body(
    layer_input,
    gain_attn,
    w_query,
    w_key,
    w_value,
    w_out,
    gain_mlp,
    w_gate,
    w_up,
    w_down,
    doc_lengths,
    cotangent,
):
    def held(*shape, dtype=BF):
        return (shape, dtype, vmem())

    def far(*shape, dtype=BF):
        return (shape, dtype, hbm())

    def room(*shape, dtype=BF):
        return pltpu.VMEM(shape, dtype)

    def local(*arrays):
        return [(a, vmem()) for a in arrays]

    def remote(*arrays):
        return [(a, hbm()) for a in arrays]

    freqs = jnp.asarray(np.repeat(scaled_freqs()[:, None], 128, axis=1))
    slots = room(2, 7, OWN // 2, D)
    own = room(OWN, D, dtype=F32)
    normed, w_qkv, w_o, cot, w_gu, queries, kv, lse, low, tables, attended, x_rows, mid, normed_mid, inverse, gains = exchange(
        "attention",
        1,
        attention,
        remote(layer_input.T, cotangent.T)
        + local(w_query, w_key, w_value, w_out.T, w_gate, w_up, gain_attn, gain_mlp, freqs)
        + [(doc_lengths, pl.BlockSpec(memory_space=pltpu.SMEM))],
        [
            far(TOK, D),
            far(D, 512),
            far(D, 384),
            far(D, TOK),
            far(D, 2 * PANEL),
            held(4, TILE, 4 * TILE),
            held(3 * TOK, 256),
            held(4, 1, 4 * TILE, dtype=F32),
            held(4, 1, 4 * TILE, dtype=jnp.int32),
            held(2, 40, TOK, dtype=F32),
            held(TOK, 320),
            held(OWN, D, dtype=F32),
            held(OWN, D, dtype=F32),
            held(OWN, D),
            held(OWN, 128, dtype=F32),
            held(8, D, dtype=F32),
        ],
        [
            room(ROWS, 512),
            room(ROWS, 384),
            room(ROWS, 2 * PANEL),
            room(8, 384, dtype=F32),
            room(8, 8, 384, dtype=F32),
            room(D, 512),
            room(D, 384),
            room(D, TOK),
            room(TOK, D),
            room(TOK, D),
            room(512, TOK, dtype=F32),
            room(TOK, D),
            slots,
            own,
            room(TILE, 3 * TOK),
        ],
    )
    grad_mid, grad_mid_own, down_part, grad_gate, grad_du, gain_two_part = exchange(
        "mlp",
        2,
        mlp,
        local(normed_mid, w_down.T) + remote(w_gu, cot) + local(mid, inverse, gains),
        [
            far(TOK, D),
            held(OWN, D, dtype=F32),
            far(TOK, D),
            held(ROWS, PANEL, dtype=F32),
            far(D, 2 * PANEL),
            held(8, D, dtype=F32),
        ],
        [
            room(ROWS, PANEL),
            room(D, 2 * PANEL),
            room(D, PANEL),
            room(TOK, D),
            room(D, TOK),
            room(TOK, D),
            room(TOK, 2 * PANEL, dtype=F32),
            room(TOK, PANEL, dtype=F32),
            room(TOK, PANEL),
            room(TOK, 2 * PANEL),
            room(TOK, D),
            room(TOK, D),
            slots,
            own,
            *wide_sum_scratch(PANEL),
            room(OWN, D),
            room(TOK, D),
        ],
    )
    output_rows, grad_rows, gain_parts, grad_out, grad_query, grad_key, grad_value, grad_d, grad_up = exchange(
        "attention_back",
        3,
        attention_back,
        remote(grad_mid, normed, w_qkv, w_o, down_part, grad_du)
        + local(grad_mid_own, attended, queries, kv, lse, low, tables, mid, x_rows, gains, gain_two_part),
        [
            held(8, OWN, 320),
            held(8, OWN, 320),
            held(16, 8, 384, dtype=F32),
            held(ROWS, 320, dtype=F32),
            held(ROWS, 320, dtype=F32),
            held(ROWS, 80, dtype=F32),
            held(ROWS, 80, dtype=F32),
            held(ROWS, PANEL, dtype=F32),
            held(ROWS, PANEL, dtype=F32),
        ],
        [
            room(TOK, D),
            room(TOK, D),
            room(D, 512),
            room(D, 384),
            room(TOK, D),
            room(4, 2, ROWS, 2 * PANEL),
            room(4, TILE, 4 * TILE),
            room(TILE, 3 * TOK),
            room(3 * TOK, 256, dtype=F32),
            room(320, TOK, dtype=F32),
            slots,
            slots,
            own,
            own,
            room(2 * TOK, 256),
            room(2, TOK, 256),
            room(TOK, 320, dtype=F32),
            room(8, OWN, 320),
            room(8, OWN, 320),
            room(8, 8, 384, dtype=F32),
            room(8, 8, 384, dtype=F32),
            room(TOK, 512),
            *wide_sum_scratch(2 * PANEL),
            *wide_sum_scratch(384),
            *wide_sum_scratch(512),
        ],
    )
    results = [
        ((320, TOK), BF),
        ((320, TOK), F32),
        ((320,), F32),
        ((320,), F32),
        ((ROWS, 320), F32),
        ((ROWS, 80), F32),
        ((ROWS, 80), F32),
        ((ROWS, 320), F32),
        ((ROWS, PANEL), F32),
        ((ROWS, PANEL), F32),
        ((ROWS, PANEL), F32),
    ]
    out = pl.pallas_call(
        closing,
        out_shape=[jax.ShapeDtypeStruct(shape, dtype) for shape, dtype in results],
        in_specs=[vmem()] * 10,
        out_specs=[vmem()] * 11,
        name="closing",
    )(output_rows, grad_rows, gain_parts, grad_query, grad_key, grad_value, grad_out, grad_gate, grad_up, grad_d)
    return (
        out[0].T,
        out[1].T,
        out[2],
        out[4],
        out[5],
        out[6],
        out[7].T,
        out[3],
        out[8],
        out[9],
        out[10].T,
    )


def solution(mesh):
    rows, columns = P("wide", "narrow"), P("narrow", "wide")
    return jax.shard_map(
        body,
        mesh=mesh,
        in_specs=(
            rows,
            P("narrow"),
            rows,
            rows,
            rows,
            columns,
            P("narrow"),
            rows,
            rows,
            columns,
            P(),
            rows,
        ),
        out_specs=(
            rows,
            rows,
            P("narrow"),
            rows,
            rows,
            rows,
            columns,
            P("narrow"),
            rows,
            rows,
            columns,
        ),
        check_vma=False,
    )
```

time: 361 us -> 323 us (0.89)
  local copies, waits for them, and re-layouts: 17.2 us -> 0 us
  Pallas kernels: 337 us -> 321 us
  other arithmetic: 5.68 us -> 0 us
    pallas_call x3, Pallas kernels: 337 us -> 317 us  [exchange(): pl.pallas_call(kernel, out_shape=[jax.ShapeDtypeStruct(shape, dtype) for...]
    slice x6 -> x0, local copies, waits for them, and re-layouts: 6.91 us -> none  [the longest x1 1.76 us: body(): grad_qkv[:, 400:480]]
    unnamed x19 -> x0, local copies, waits for them, and re-layouts: 4.55 us -> none
    pallas_call x0 -> x1, Pallas kernels: none -> 3.9 us  [body(): pl.pallas_call(closing, out_shape=[jax.ShapeDtypeStruct(shape, dtype) for...]
where the time goes in v4:
time: 323 us; the launch traced here: 322 us
  Pallas kernels  321 us (99%)
    pallas_call x3, Pallas kernels, exchange(): pl.pallas_call(kernel, out_shape=[jax.ShapeDtypeStruct(shape, dtype) for...  317 us

profile of v4, /device:TPU:1, one launch (start us, length us, event | category | flops | bytes accessed | tf_op | source)
XLA Modules:
  0.0 321.6 jit_solution(14424844984959222729)
XLA Ops:
  0.6 108.6 %attention.1 = (bf16[512,2560]{1,0:T(8,128)(2,1)}, bf16[2560,512]{1,0:T(8,128)(2,1)}, bf16[2560,384]{1,0:T(8,128)(2,1)}, bf16[2560,512]{1,0:T(8,128)(2,1)}, bf16...) custom-call(bf16[320,512]{1,0:T(8,128)(2,1)} %bitcast.8, ...), custom_call_target="tpu_custom_call" | custom-call | tf_op jit(solution)/shard_map/attention/pallas_call | solution.py:871
  109.3 102.7 %mlp.1 = (bf16[512,2560]{1,0:T(8,128)(2,1)}, f32[64,2560]{1,0:T(8,128)}, bf16[512,2560]{1,0:T(8,128)(2,1)}, f32[160,896]{1,0:T(8,128)}, bf16[2560,1792]{1,0:T(8,128)(2,1)}, /*index=5*/f32[8,2560]{1,0:T(8,128)}) custom-call(bf16[64,2560]{1,0:T(8,128)(2,1)} %get-tuple-element.53.refs_0_, bf16[160,896]{1,0:T(8,128)(2,1)} %bitcast.10, ...), custom_call_target="tpu_custom_call" | custom-call | tf_op jit(solution)/shard_map/mlp/pallas_call | solution.py:871
  212.0 105.8 %attention_back.1 = (bf16[8,64,320]{2,1,0:T(8,128)(2,1)}, bf16[8,64,320]{2,1,0:T(8,128)(2,1)}, f32[16,8,384]{2,1,0:T(8,128)}, f32[160,320]{1,0:T(8,128)}, f32[16...) custom-call(bf16[512,2560]{1,0:T(8,128)(2,1)} %get-tuple-element.59.refs_0, ...), custom_call_target="tpu_custom_call" | custom-call | tf_op jit(solution)/shard_map/attention_back/pallas_call | solution.py:871
  317.7 3.9 %closing.1 = (bf16[320,512]{1,0:T(8,128)(2,1)}, f32[320,512]{1,0:T(8,128)}, f32[320]{0:T(512)}, f32[320]{0:T(512)}, f32[160,320]{1,0:T(8,128)}, /*index=5*/f32[1...) custom-call(bf16[8,64,320]{2,1,0:T(8,128)(2,1)} %get-tuple-element.7, ...), custom_call_target="tpu_custom_call" | custom-call | tf_op jit(solution)/shard_map/closing/pallas_call | solution.py:1065

commit v5 on v4

--- a/solution.py
+++ b/solution.py
@@ -20,6 +20,7 @@
 PANEL = 896
 TILE = 128
 REACH = WINDOW + TILE
+CUT = 1024
 
 epsilon = 1e-05
 rope_base = 1000000.0
@@ -63,6 +64,7 @@
         bar = pltpu.get_barrier_semaphore()
         for device in givers:
             pl.semaphore_signal(bar, inc=1, device_id=device, device_id_type=MESH)
+        self.settle(*self.loads)
         pl.semaphore_wait(bar, takers)
 
     def send(self, src, dst, device):
@@ -109,40 +111,55 @@
             tasks = left
         for copy in self.sent[self.done :]:
             copy.wait_send()
-        for copy in self.open:
-            copy.wait()
+        self.settle(*self.open)
 
 
 def block_of(ref, index, rows):
     return ref.at[pl.ds(pl.multiple_of(index * rows, 16), rows)]
 
 
-def narrow_gather(net, src, dst, cut, stacked=False):
+def narrow_gather(net, src, dst, cut):
     at = net.at
     me, near = at.n, at.narrow(0, 1)
-    rows = src.shape[0]
+    right, left, beside = (at.w, at.narrow(1, 0)), (at.w, at.narrow(3, 0)), (at.w, near)
+    rows, columns = src.shape
+    upper, lower = pl.ds(0, rows // 2), pl.ds(rows // 2, rows // 2)
+    early, late = pl.ds(0, cut), pl.ds(cut, columns - cut)
 
     def block(n):
-        return dst.at[n] if stacked else block_of(dst, n, rows)
+        return block_of(dst, n, rows)
+
+    def on(part, device):
+        return net.send(part, part, device)
 
     kept = net.keep(src, block(me))
-    late = net.send(src.at[cut:], block(me).at[cut:], (at.w, near))
-    turns = [(d, net.send(src, block(me), (at.w, at.narrow(d, 0)))) for d in (1, 3, 2)]
-    early = net.send(src.at[:cut], block(me).at[:cut], (at.w, near))
-    yield
-    late.wait_recv()
-    rest = [
-        net.send(block(near).at[cut:], block(near).at[cut:], (at.w, at.narrow(d, 0)))
-        for d in (1, 3, 2)
-    ]
-    yield
-    for d, copy in turns:
-        copy.wait_recv()
-        part = block(at.narrow(-d, 0)).at[:cut]
-        rest.append(net.send(part, part, (at.w, near)))
-    yield
-    early.wait_recv()
-    for copy in rest:
+    first = net.send(src.at[:, late], block(me).at[:, late], beside)
+    to_right, to_left = net.send(src, block(me), right), net.send(src, block(me), left)
+    over = [net.send(src.at[:, early], block(me).at[:, early], beside)]
+    yield
+    first.wait_recv()
+    part = block(near).at[:, late]
+    near_right, near_left = on(part, right), on(part, left)
+    yield
+    to_right.wait_recv()
+    part = block(at.narrow(3, 0))
+    from_left = on(part.at[upper], right)
+    over.append(on(part.at[:, early], beside))
+    to_left.wait_recv()
+    part = block(at.narrow(1, 0))
+    from_right = on(part.at[lower], left)
+    over.append(on(part.at[:, early], beside))
+    yield
+    near_right.wait_recv()
+    over.append(on(block(at.narrow(3, 1)).at[upper, late], right))
+    near_left.wait_recv()
+    over.append(on(block(at.narrow(1, 1)).at[lower, late], left))
+    yield
+    from_left.wait_recv()
+    from_right.wait_recv()
+    over.append(on(block(at.narrow(2, 0)).at[:, early], beside))
+    yield
+    for copy in over:
         copy.wait_recv()
     net.settle(kept)
 
@@ -181,44 +198,75 @@
 def narrow_sum(net, src, slots, out, cut, held=None):
     at = net.at
     me, near = at.n, at.narrow(0, 1)
-    rows = out.shape[0]
+    right, left, beside = (at.w, at.narrow(1, 0)), (at.w, at.narrow(3, 0)), (at.w, near)
+    rows, columns = out.shape
+    upper, lower = pl.ds(0, rows // 2), pl.ds(rows // 2, rows // 2)
+    early, late = pl.ds(0, cut), pl.ds(cut, columns - cut)
 
     def block(n):
         return block_of(src, n, rows)
 
-    def term_of(n):
-        return block_of(src if held is None else held, n, rows)
-
+    def term(n, *part):
+        return block_of(src if held is None else held, n, rows)[part].astype(F32)
+
+    def put(slot, value, *part):
+        slots[slot, *part] = value.astype(BF)
+
+    def at_slot(slot, *part):
+        return slots[slot, *part].astype(F32)
+
+    everything = slice(None)
     over = {
-        d: net.send(block(at.narrow(d, 1)).at[:cut], slots.at[d - 1, :cut], (at.w, near))
-        for d in (1, 3, 2)
+        d: net.send(block(at.narrow(d, 1)).at[:, early], slots.at[k, :, early], beside)
+        for d, k in ((2, 2), (1, 0), (3, 1))
     }
-    across = {
-        d: net.send(block(at.narrow(d, 1)).at[cut:], slots.at[d - 1, cut:], (at.w, at.narrow(d, 0)))
-        for d in (1, 3, 2)
-    }
-    late = [
-        net.send(block(at.narrow(d, 0)).at[cut:], slots.at[2 + d, cut:], (at.w, at.narrow(d, 0)))
-        for d in (1, 3, 2)
-    ]
-    final = [net.send(block(near).at[:cut], slots.at[6, :cut], (at.w, near))]
-    yield
-    early = []
-    for d in (1, 3, 2):
+    far = block(at.narrow(2, 1))
+    pass_right = net.send(far.at[upper, late], slots.at[3, upper, late], right)
+    pass_left = net.send(far.at[lower, late], slots.at[3, lower, late], left)
+    final = [net.send(block(near).at[:, early], slots.at[7, :, early], beside)]
+    yield
+    over[2].wait_recv()
+    n = at.narrow(2, 0)
+    put(2, at_slot(2, everything, early) + term(n, everything, early), everything, early)
+    put(2, term(n, everything, late), everything, late)
+    far_right = net.send(slots.at[2, upper], slots.at[4, upper], right)
+    far_left = net.send(slots.at[2, lower], slots.at[4, lower], left)
+    yield
+    pass_right.wait_recv()
+    n = at.narrow(1, 1)
+    put(10, term(n, upper, late) + at_slot(3, upper, late), upper, late)
+    put(10, term(n, lower, late), lower, late)
+    near_right = net.send(slots.at[10, :, late], slots.at[8, :, late], right)
+    pass_left.wait_recv()
+    n = at.narrow(3, 1)
+    put(11, term(n, lower, late) + at_slot(3, lower, late), lower, late)
+    put(11, term(n, upper, late), upper, late)
+    near_left = net.send(slots.at[11, :, late], slots.at[9, :, late], left)
+    yield
+    for d, slot, copy, half, whole in (
+        (1, 0, far_right, upper, lower),
+        (3, 1, far_left, lower, upper),
+    ):
         over[d].wait_recv()
-        term = slots.at[d - 1, :cut]
-        add_rows(cut, 16, term, [term, term_of(at.narrow(d, 0)).at[:cut]])
-        early.append(net.send(term, slots.at[2 + d, :cut], (at.w, at.narrow(d, 0))))
-    yield
-    for d in (1, 3, 2):
-        across[d].wait_recv()
-    term = slots.at[0, cut:]
-    add_rows(rows - cut, 16, term, [term_of(near).at[cut:], *(slots.at[k, cut:] for k in range(3))])
-    final.append(net.send(term, slots.at[6, cut:], (at.w, near)))
-    yield
-    for copy in late + early + final:
         copy.wait_recv()
-    add_rows(rows, 16, out, [term_of(me), *(slots.at[k] for k in range(3, 7))])
+        n = at.narrow(d, 0)
+        put(slot, at_slot(slot, half, early) + term(n, half, early) + at_slot(4, half, early), half, early)
+        put(slot, at_slot(slot, whole, early) + term(n, whole, early), whole, early)
+        put(slot, term(n, half, late) + at_slot(4, half, late), half, late)
+        put(slot, term(n, whole, late), whole, late)
+        final.append(
+            net.send(slots.at[slot], slots.at[5 + slot], right if d == 1 else left)
+        )
+    yield
+    near_right.wait_recv()
+    near_left.wait_recv()
+    value = term(near, everything, late) + at_slot(8, everything, late) + at_slot(9, everything, late)
+    put(8, value, everything, late)
+    final.append(net.send(slots.at[8, :, late], slots.at[7, :, late], beside))
+    yield
+    for copy in final:
+        copy.wait_recv()
+    out[...] = term(me, everything, everything) + at_slot(5) + at_slot(6) + at_slot(7)
 
 
 def wide_gather(net, src, dst):
@@ -367,21 +415,32 @@
     return jnp.where((key >= low) & (key <= query), raw, masked)
 
 
+def gain_terms(dst, grad, normed, gains, k):
+    def part(columns):
+        total = jnp.sum(
+            grad[:, columns].astype(F32) * normed[:, columns].astype(F32), axis=0, keepdims=True
+        )
+        dst[:, columns] = jnp.broadcast_to(total / gains[k : k + 1, columns], (8, 256))
+
+    every(256, part)
+
+
 def by_feature(dst, rows):
     for j in range(8):
         dst[j] = rows[:, j * 320 : (j + 1) * 320]
 
 
-def every(size, body):
-    @pl.loop(0, D // size)
+def every(size, body, begin=0, end=D):
+    @pl.loop(begin // size, end // size)
     def _(i):
         body(pl.ds(pl.multiple_of(i * size, size), size))
 
 
 def attention(net, ins, outs, scratch):
-    x_own, cot_own, w_query, w_key, w_value, w_out, w_gate, w_up, gain_one, gain_two, freqs, lengths = ins
-    normed_far, w_qkv_far, w_out_far, cot, w_gu = outs[:5]
-    queries, kv, lse, low, tables, attended, x_rows, mid, normed_mid, inverse, gains = outs[5:]
+    x_own, cot_own, w_query, w_key, w_value, w_out, w_gate, w_up, w_down = ins[:9]
+    gain_one, gain_two, freqs, lengths = ins[9:]
+    normed_far, w_qkv_far, w_out_far, cot, w_gu, w_d, normed_two = outs[:7]
+    queries, kv, lse, low, tables, attended, x_rows, mid, inverse, gains = outs[7:]
     (
         shard_qkv,
         shard_out,
@@ -398,10 +457,12 @@
         slots,
         total,
         values_t,
+        normed_mid,
     ) = scratch
     at = net.at
     later = [((at.w + k) % 16, at.n) for k in (1, 2)]
     earlier = [((at.w + 16 - k) % 16, at.n) for k in (1, 2)]
+    net.barrier(at.narrow_peers() + at.wide_peers() + earlier, 14)
     shard_qkv[:, :320] = w_query[...]
     shard_qkv[:, 320:] = jnp.concatenate(
         [w_key[...], w_value[...], jnp.zeros((ROWS, 32), BF)], axis=1
@@ -409,10 +470,9 @@
     gains_own[...] = jnp.zeros(gains_own.shape, F32)
     gains_own[0:1, :320] = gain_one[...].reshape(1, 320)
     gains_own[1:2, :320] = gain_two[...].reshape(1, 320)
-    net.barrier(at.narrow_peers() + at.wide_peers() + earlier, 14)
     panel = wide_gather(net, shard_qkv, w_qkv)
     step(panel, panel)
-    stream = narrow_gather(net, x_own, x_t, 160)
+    stream = narrow_gather(net, x_own, x_t, 256)
     sizes = narrow_share(net, gains_own, gain_pieces)
     step(stream, sizes)
     shard_out[...] = jnp.concatenate([w_out[...], jnp.zeros((ROWS, 64), BF)], axis=1)
@@ -433,12 +493,13 @@
         one = first_key[:, tile * TILE : (tile + 1) * TILE]
         low[tile] = jnp.concatenate([one] * 4, axis=1)
 
-    step(stream, panel, panel, panel)
+    step(panel, stream, panel, stream, panel)
     w_outs = wide_gather(net, shard_out, w_o)
     gate_up = wide_gather(net, shard_gu, w_gu)
-    step(w_outs, w_outs, gate_up, stream, panel)
-    finish(stream, sizes, panel)
-    step(gate_up)
+    step(w_outs, w_outs, gate_up, panel, stream, stream, gate_up, w_outs, w_outs)
+    finish(panel, sizes)
+    step(w_outs)
+    finish(stream)
     for j in range(8):
         gains[:, pl.ds(j * 320, 320)] = gain_pieces[j, :, :320]
     every(256, lambda rows: turned_over(x, x_t, rows))
@@ -467,18 +528,16 @@
     arriving = [
         net.send(kv.at[mine], kv.at[pl.ds((2 - k) * TOK, TOK)], later[k - 1]) for k in (1, 2)
     ]
-    cots = narrow_gather(net, cot_own, cot, 160)
-    step(cots)
-    net.keep(normed, normed_far)
-    net.keep(w_qkv, w_qkv_far)
+    cots = narrow_gather(net, cot_own, cot, 256)
+    down = wide_gather(net, w_down, w_d)
+    step(cots, down)
     for head in range(4):
         one = turned(head * HEAD).astype(BF)
         for tile in range(4):
             queries[tile, :, pl.ds(head * TILE, TILE)] = one[:, tile * TILE : (tile + 1) * TILE]
-    step(w_outs, w_outs)
+    step(w_outs, gate_up)
     for copy in arriving:
         copy.wait_recv()
-    step(w_outs)
     values_t[...] = kv[:, 128:].T
 
     def one_tile(i):
@@ -502,10 +561,8 @@
         def columns(rows):
             src[tokens, rows] = dot_t(attended[tokens, :], w_o[rows, :320]).astype(BF)
 
-        every(256, columns)
-        return narrow_sum(
-            net, src.at[tokens], slots.at[h], total.at[pl.ds(h * 32, 32)], 16
-        )
+        every(512, columns)
+        return narrow_sum(net, src.at[tokens], slots.at[h], total.at[pl.ds(h * 32, 32)], CUT)
 
     def norm_part(h):
         rows = pl.ds(h * 32, 32)
@@ -514,23 +571,32 @@
         inv = lax.rsqrt(jnp.mean(stream * stream, axis=1, keepdims=True) + epsilon)
         inverse[rows, :] = jnp.broadcast_to(inv, (32, 128))
         normed_mid[rows, :] = (stream * inv * gains[1:2, :]).astype(BF)
-
-    step(gate_up)
+        return narrow_gather(
+            net, normed_mid.at[rows], normed_two.at[pl.ds(h * 256, 256)], CUT
+        )
+
     pl.loop(0, 2)(one_tile)
     finish(w_outs)
-    net.keep(w_o, w_out_far)
     early = out_part(0)
     step(early, gate_up, cots)
     pl.loop(2, 4)(one_tile)
-    step(early)
+    step(early, early)
     late = out_part(1)
-    step(late, early, gate_up, late, cots)
+    step(early, late, early, down, cots, late)
+    net.keep(w_o, w_out_far)
+    net.keep(normed, normed_far)
+    step(late)
+    net.keep(w_qkv, w_qkv_far)
     finish(early)
-    norm_part(0)
-    step(late, gate_up)
+    ahead = norm_part(0)
+    step(ahead, late, gate_up, ahead, late, down, ahead)
+    step(cots, ahead, gate_up, ahead)
     finish(late)
-    norm_part(1)
-    finish(cots, gate_up)
+    behind = norm_part(1)
+    step(behind, down, cots, behind, down, behind)
+    finish(ahead)
+    step(behind, down, behind)
+    finish(behind, gate_up, cots, down)
     net.run([])
 
 
@@ -543,26 +609,16 @@
 
 
 def mlp(net, ins, outs, scratch):
-    normed_own, w_down, gu_far, cot_far, mid, inverse, gains = ins
+    normed_far, d_far, gu_far, cot_far, mid, inverse, gains = ins
     grad_mid_far, grad_mid, down_far, grad_gate, du_far, gain_part = outs
-    shard_d, w_gu, w_d, normed, cot_t, cot, gu, grad_hidden, hidden, grad_pre, src = scratch[:11]
-    down_part, slots, total, core, turned, last, low, grad_mid_full = scratch[11:]
+    w_gu, w_d, normed, cot_t, cot, gu, grad_hidden, hidden, grad_pre, src = scratch[:10]
+    down_part, slots, total, core, turned, last, low, grad_mid_full = scratch[10:]
     at = net.at
-    shard_d[...] = w_down[...]
+    sources, rooms = (normed_far, gu_far, cot_far, d_far), (normed, w_gu, cot_t, w_d)
+    loads = [net.keep(a, b) for a, b in zip(sources, rooms)]
     net.barrier(at.narrow_peers() + at.wide_peers(), 12)
     tokens = [pl.ds(0, 256), pl.ds(256, 256)]
     own = [pl.ds(0, 32), pl.ds(32, 32)]
-    gathers = [narrow_gather(net, normed_own.at[own[h]], normed.at[tokens[h]], 16) for h in (0, 1)]
-    panel = wide_gather(net, shard_d, w_d)
-    step(panel, gathers[0], panel)
-    cots, weights = net.keep(cot_far, cot_t), net.keep(gu_far, w_gu)
-    step(gathers[0], gathers[1])
-    net.settle(cots)
-    every(256, lambda rows: turned_over(cot, cot_t, rows))
-    step(panel, gathers[1], panel, gathers[0], panel)
-    net.settle(weights)
-    finish(gathers[0])
-
     def gate_up(h):
         def part(columns):
             gu[tokens[h], columns] = dot(normed[tokens[h], :], w_gu[:, columns])
@@ -593,7 +649,7 @@
             src[tokens[h], rows] = dot_t(grad_pre[tokens[h], :], w_gu[rows, :]).astype(BF)
 
         every(256, part)
-        return narrow_sum(net, src.at[tokens[h]], slots.at[h], total.at[own[h]], 16)
+        return narrow_sum(net, src.at[tokens[h]], slots.at[h], total.at[own[h]], CUT)
 
     def back_norm(h):
         inv, scale = inverse[own[h], :1], gains[1:2, :]
@@ -604,62 +660,67 @@
         mine = cot[own_rows(at, h), :].astype(F32) + through
         grad_mid[own[h], :] = mine
         low[own[h], :] = mine.astype(BF)
-        return narrow_gather(net, low.at[own[h]], grad_mid_full.at[tokens[h]], 16)
-
+        return narrow_gather(net, low.at[own[h]], grad_mid_full.at[tokens[h]], CUT)
+
+    net.settle(*loads[:2])
     gate_up(0)
-    step(gathers[1], panel)
-    finish(panel)
-    gathered = len(net.sent)
+    net.settle(*loads[2:])
+    every(256, lambda rows: turned_over(cot, cot_t, rows))
     back_down(0)
     back_hidden(0)
     sums = [back_normed(0)]
     step(sums[0])
-    finish(gathers[1])
     gate_up(1)
     step(sums[0])
     back_down(1)
+    step(sums[0])
     back_hidden(1)
+    step(sums[0])
     sums.append(back_normed(1))
-    step(sums[1], sums[0])
+    step(sums[0], sums[1])
 
     def grad_gate_rows(rows):
         w_gu[rows, :PANEL] = t_dot(normed[:, rows], grad_pre[:, :PANEL]).astype(BF)
 
-    every(256, grad_gate_rows)
-    wide = wide_sum(net, w_gu.at[:, pl.ds(0, PANEL)], core, turned, last, [(grad_gate, 0, PANEL)])
-    step(wide, sums[1])
+    every(256, grad_gate_rows, 0, 1280)
+    step(sums[1])
     finish(sums[0])
     back = [back_norm(0)]
     step(back[0], sums[1])
+    every(256, grad_gate_rows, 1280, D)
+    wide = wide_sum(net, w_gu.at[:, pl.ds(0, PANEL)], core, turned, last, [(grad_gate, 0, PANEL)])
+    step(back[0], sums[1], wide, back[0])
 
     def grad_up_rows(rows):
         w_gu[rows, PANEL:] = t_dot(normed[:, rows], grad_pre[:, PANEL:]).astype(BF)
 
-    every(256, grad_up_rows)
-    net.keep(w_gu.at[:, pl.ds(PANEL, PANEL)], du_far.at[:, pl.ds(PANEL, PANEL)])
+    every(256, grad_up_rows, 0, 1280)
+    step(sums[1], back[0], wide)
+    every(256, grad_up_rows, 1280, D)
     finish(sums[1])
     back.append(back_norm(1))
-    step(back[0], back[1], wide)
+    step(back[1], back[0])
+    net.keep(w_gu.at[:, pl.ds(PANEL, PANEL)], du_far.at[:, pl.ds(PANEL, PANEL)])
 
     def forward_down(rows):
         down_part[:, rows] = dot_t(hidden[...], w_d[rows, :]).astype(BF)
 
-    every(256, forward_down)
+    every(256, forward_down, 0, 1280)
+    step(back[1], wide)
+    every(256, forward_down, 1280, D)
     net.keep(down_part, down_far)
-    step(back[1], back[0], wide)
-    net.release(gathered)
+    step(back[1], wide)
 
     def grad_d_rows(rows):
         w_d[rows, :] = dot(cot_t[rows, :], hidden[...]).astype(BF)
 
-    every(256, grad_d_rows)
+    every(256, grad_d_rows, 0, 1280)
+    step(back[1], wide, back[1])
+    every(256, grad_d_rows, 1280, D)
     net.keep(w_d, du_far.at[:, pl.ds(0, PANEL)])
     finish(back[0])
-    step(back[1], wide)
-    grad, stream = total[...], mid[...]
-    gain_part[...] = jnp.broadcast_to(
-        jnp.sum(grad * stream * inverse[:, :1], axis=0, keepdims=True), gain_part.shape
-    )
+    step(wide)
+    gain_terms(gain_part, src, normed, gains, 1)
     finish(back[1])
     net.keep(grad_mid_full, grad_mid_far)
     finish(wide)
@@ -673,7 +734,7 @@
     grad_mid, normed, w_qkv, w_o, down_part, held_du = scratch[:6]
     upstream, keys_t, grad_kv, grad_q, slots_one, slots_two, total_one, total_two = scratch[6:14]
     later_kv, turned_back, ga, rows_one, rows_two, parts, narrow_parts, grads_ref = scratch[14:22]
-    sum_du, sum_out, sum_qkv = scratch[22:25], scratch[25:28], scratch[28:31]
+    sum_du, sum_out, sum_qkv, gain_one_part = scratch[22:25], scratch[25:28], scratch[28:31], scratch[31]
     at = net.at
     tokens = [pl.ds(0, 256), pl.ds(256, 256)]
     own = [pl.ds(0, 32), pl.ds(32, 32)]
@@ -690,7 +751,7 @@
     )
     downs = [
         narrow_sum(
-            net, down_far.at[tokens[h]], slots_one.at[h], total_one.at[own[h]], 16, down_part.at[tokens[h]]
+            net, down_far.at[tokens[h]], slots_one.at[h], total_one.at[own[h]], CUT, down_part.at[tokens[h]]
         )
         for h in (0, 1)
     ]
@@ -706,15 +767,15 @@
             upstream[tile, :, pl.ds(head * TILE, TILE)] = one[:, tile * TILE : (tile + 1) * TILE]
     keys_t[...] = kv[:, :128].T
     net.settle(loads[4], *held_loads)
-    step(wide_du, *downs)
-    fill = jnp.zeros((256, 64), F32)
+    step(downs[0], wide_du, downs[1], *downs)
+    fill = jnp.zeros((512, 64), F32)
 
     def grad_out_rows(rows):
         w_o[rows, :] = jnp.concatenate(
             [t_dot(grad_mid[:, rows], attended[...]), fill], axis=1
         ).astype(BF)
 
-    every(256, grad_out_rows)
+    every(512, grad_out_rows)
     wide_out = wide_sum(net, w_o, *sum_out, [(grad_out, 0, 320)])
     step(wide_out)
     grad_kv[...] = jnp.zeros(grad_kv.shape, F32)
@@ -737,7 +798,7 @@
             ]
 
     pl.loop(0, 2)(one_tile)
-    step(*downs, wide_du)
+    step(*downs, wide_du, *downs, wide_out)
     pl.loop(2, 4)(one_tile)
     later_kv[...] = grad_kv[pl.ds(0, 2 * TOK), :].astype(BF)
     arriving = [
@@ -757,7 +818,7 @@
     rotated = []
     for head in range(4):
         rotated += unturned(grad_q[pl.ds(head * HEAD, HEAD), :])
-    step(wide_du, wide_out)
+    step(wide_du)
     finish(*downs)
     by_feature(rows_one, (mid[...] + total_one[...]).astype(BF))
     output_rows = narrow_swap(net, rows_one, back_one)
@@ -779,42 +840,35 @@
             down_part[tokens[h], rows] = dot_t(grads_ref[tokens[h], :], w_qkv[rows, :]).astype(BF)
 
         every(256, part)
-        return narrow_sum(net, down_part.at[tokens[h]], slots_two.at[h], total_two.at[own[h]], 16)
+        return narrow_sum(net, down_part.at[tokens[h]], slots_two.at[h], total_two.at[own[h]], CUT)
 
     sums = [back_normed(0)]
-    step(sums[0])
+    step(sums[0], wide_out)
     sums.append(back_normed(1))
-    step(sums[1])
+    step(sums[0], sums[1], sums[0])
     net.settle(loads[1])
 
     def grad_qkv_rows(rows):
         w_qkv[rows, :] = t_dot(normed[:, rows], grads_ref[...]).astype(BF)
 
-    step(sums[0])
-    every(256, grad_qkv_rows)
+    every(512, grad_qkv_rows)
     wide_qkv = wide_sum(
         net, w_qkv, *sum_qkv, [(grad_query, 0, 320), (grad_key, 320, 80), (grad_value, 400, 80)]
     )
-    step(wide_qkv, sums[1], sums[0], wide_out, wide_qkv, sums[1], wide_du)
-    finish(sums[0])
-    finish(sums[1])
-    stream, grad = x_rows[...], total_two[...]
-    inv = lax.rsqrt(jnp.mean(stream * stream, axis=1, keepdims=True) + epsilon)
-    weighted = grad * gains[0:1, :]
-    inner = jnp.sum(weighted * stream, axis=1, keepdims=True)
-    through = inv * weighted - stream * (inv * inv * inv * inner / D)
-    by_feature(rows_two, (grad_mid_own[...] + through).astype(BF))
-    back = narrow_swap(net, rows_two, back_two)
-    step(back)
-    gain_one = jnp.sum(grad * stream * inv, axis=0, keepdims=True)
-    both = jnp.concatenate([gain_one, gain_two_part[0:1, :], jnp.zeros((6, D), F32)], axis=0)
+    step(wide_qkv, sums[1], sums[0])
+    gain_terms(gain_one_part, down_part, normed, gains, 0)
+    both = jnp.concatenate(
+        [gain_one_part[0:1, :], gain_two_part[0:1, :], jnp.zeros((6, D), F32)], axis=0
+    )
     for j in range(8):
         parts[j, :, :320] = both[:, j * 320 : (j + 1) * 320]
         parts[j, :, 320:] = jnp.zeros((8, 64), F32)
     me = at.n
     copies = [net.send(parts.at[p[1]], narrow_parts.at[me], p) for p in at.narrow_peers()]
     narrow_parts[me] = parts[me]
-    step(wide_out, wide_qkv, wide_du)
+    step(sums[1], sums[0], wide_qkv, wide_out, sums[1], wide_du, wide_qkv)
+    finish(sums[0])
+    step(sums[1])
     for copy in copies:
         copy.wait_recv()
     sum_parts = narrow_parts[0]
@@ -824,8 +878,17 @@
     copies = [
         net.send(wide_parts.at[0], wide_parts.at[k + 1], p) for k, p in enumerate(everyone)
     ]
-    step(wide_out, wide_qkv, wide_du)
-    finish(wide_out, wide_qkv, wide_du)
+    step(wide_out, wide_qkv)
+    finish(sums[1])
+    stream, grad = x_rows[...], total_two[...]
+    inv = lax.rsqrt(jnp.mean(stream * stream, axis=1, keepdims=True) + epsilon)
+    weighted = grad * gains[0:1, :]
+    inner = jnp.sum(weighted * stream, axis=1, keepdims=True)
+    through = inv * weighted - stream * (inv * inv * inv * inner / D)
+    by_feature(rows_two, (grad_mid_own[...] + through).astype(BF))
+    back = narrow_swap(net, rows_two, back_two)
+    step(back, wide_out, wide_qkv, wide_du)
+    finish(wide_out, wide_du, wide_qkv)
     for copy in copies:
         copy.wait_recv()
     finish(back, output_rows)
@@ -862,22 +925,42 @@
     return pl.BlockSpec(memory_space=pl.ANY)
 
 
-def exchange(name, number, body, ins, outs, scratch=(), sends=200, keeps=24):
+def exchange(name, number, body, ins, outs, scratch=()):
+    def room_for(where, shape, dtype):
+        return [pltpu.VMEM(shape, dtype)] if where == "vmem" else []
+
+    in_rooms = [room_for(where, a.shape, a.dtype) for a, where in ins]
+    out_rooms = [room_for(where, shape, dtype) for shape, dtype, where in outs]
+    rooms = [r for part in (*in_rooms, *out_rooms) for r in part]
+
     def kernel(*refs):
         a, b = len(ins), len(ins) + len(outs)
+        c = b + len(rooms)
+        spare = iter(refs[b:c])
         net = Net(Place(), *refs[-3:])
-        body(net, refs[:a], refs[a:b], refs[b:-3])
+        in_refs = [next(spare) if room else ref for ref, room in zip(refs[:a], in_rooms)]
+        out_refs = [next(spare) if room else ref for ref, room in zip(refs[a:b], out_rooms)]
+        net.loads = [net.keep(far, near) for far, near in zip(refs[:a], in_refs) if far is not near]
+        body(net, in_refs, out_refs, refs[c:-3])
+        for far, near in zip(refs[a:b], out_refs):
+            if far is not near:
+                net.keep(near, far)
+        net.settle(*net.open)
+
+    def spec(where):
+        return pl.BlockSpec(memory_space=pltpu.SMEM) if where == "smem" else hbm()
 
     return pl.pallas_call(
         kernel,
         out_shape=[jax.ShapeDtypeStruct(shape, dtype) for shape, dtype, _ in outs],
-        in_specs=[spec for _, spec in ins],
-        out_specs=[spec for _, _, spec in outs],
+        in_specs=[spec(where) for _, where in ins],
+        out_specs=[hbm() for _ in outs],
         scratch_shapes=[
+            *rooms,
             *scratch,
-            pltpu.SemaphoreType.DMA((sends,)),
-            pltpu.SemaphoreType.DMA((sends,)),
-            pltpu.SemaphoreType.DMA((keeps,)),
+            pltpu.SemaphoreType.DMA((200,)),
+            pltpu.SemaphoreType.DMA((200,)),
+            pltpu.SemaphoreType.DMA((56,)),
         ],
         compiler_params=pltpu.CompilerParams(
             collective_id=number, has_side_effects=True, vmem_limit_bytes=60 * 2**20
@@ -911,36 +994,56 @@
     cotangent,
 ):
     def held(*shape, dtype=BF):
-        return (shape, dtype, vmem())
+        return (shape, dtype, "vmem")
 
     def far(*shape, dtype=BF):
-        return (shape, dtype, hbm())
+        return (shape, dtype, "hbm")
 
     def room(*shape, dtype=BF):
         return pltpu.VMEM(shape, dtype)
 
     def local(*arrays):
-        return [(a, vmem()) for a in arrays]
+        return [(a, "vmem") for a in arrays]
 
     def remote(*arrays):
-        return [(a, hbm()) for a in arrays]
+        return [(a, "hbm") for a in arrays]
 
     freqs = jnp.asarray(np.repeat(scaled_freqs()[:, None], 128, axis=1))
-    slots = room(2, 7, OWN // 2, D)
+    slots = room(2, 12, OWN // 2, D)
     own = room(OWN, D, dtype=F32)
-    normed, w_qkv, w_o, cot, w_gu, queries, kv, lse, low, tables, attended, x_rows, mid, normed_mid, inverse, gains = exchange(
+    (
+        normed,
+        w_qkv,
+        w_o,
+        cot,
+        w_gu,
+        w_d,
+        normed_two,
+        queries,
+        kv,
+        lse,
+        low,
+        tables,
+        attended,
+        x_rows,
+        mid,
+        inverse,
+        gains,
+    ) = exchange(
         "attention",
         1,
         attention,
         remote(layer_input.T, cotangent.T)
-        + local(w_query, w_key, w_value, w_out.T, w_gate, w_up, gain_attn, gain_mlp, freqs)
-        + [(doc_lengths, pl.BlockSpec(memory_space=pltpu.SMEM))],
+        + local(w_query, w_key, w_value, w_out.T, w_gate, w_up, w_down.T, gain_attn, gain_mlp, freqs)
+        + [(doc_lengths, "smem")],
         [
             far(TOK, D),
             far(D, 512),
             far(D, 384),
             far(D, TOK),
             far(D, 2 * PANEL),
+            far(D, PANEL),
+            far(TOK, D),
             held(4, TILE, 4 * TILE),
             held(3 * TOK, 256),
             held(4, 1, 4 * TILE, dtype=F32),
@@ -949,7 +1052,6 @@
             held(TOK, 320),
             held(OWN, D, dtype=F32),
             held(OWN, D, dtype=F32),
-            held(OWN, D),
             held(OWN, 128, dtype=F32),
             held(8, D, dtype=F32),
         ],
@@ -969,13 +1071,14 @@
             slots,
             own,
             room(TILE, 3 * TOK),
+            room(OWN, D),
         ],
     )
     grad_mid, grad_mid_own, down_part, grad_gate, grad_du, gain_two_part = exchange(
         "mlp",
         2,
         mlp,
-        local(normed_mid, w_down.T) + remote(w_gu, cot) + local(mid, inverse, gains),
+        remote(normed_two, w_d, w_gu, cot) + local(mid, inverse, gains),
         [
             far(TOK, D),
             held(OWN, D, dtype=F32),
@@ -985,7 +1088,6 @@
             held(8, D, dtype=F32),
         ],
         [
-            room(ROWS, PANEL),
             room(D, 2 * PANEL),
             room(D, PANEL),
             room(TOK, D),
@@ -1047,6 +1149,7 @@
             *wide_sum_scratch(2 * PANEL),
             *wide_sum_scratch(384),
             *wide_sum_scratch(512),
+            room(8, D, dtype=F32),
         ],
     )
     results = [

time: 323 us -> 300 us (0.929)
  Pallas kernels: 321 us -> 297 us
    pallas_call x3, Pallas kernels: 317 us -> 293 us  [exchange(): pl.pallas_call(kernel, out_shape=[jax.ShapeDtypeStruct(shape, dtype) for...]
where the time goes in v5:
time: 300 us; the launch traced here: 297 us
  Pallas kernels  297 us (99%)
    pallas_call x3, Pallas kernels, exchange(): pl.pallas_call(kernel, out_shape=[jax.ShapeDtypeStruct(shape, dtype) for...  293 us

profile of v5, /device:TPU:1, one launch (start us, length us, event | category | flops | bytes accessed | tf_op | source)
XLA Modules:
  0.0 297.3 jit_solution(7136132405360131746)
XLA Ops:
  0.6 124.4 %attention.1 = (bf16[512,2560]{1,0:T(8,128)(2,1)}, bf16[2560,512]{1,0:T(8,128)(2,1)}, bf16[2560,384]{1,0:T(8,128)(2,1)}, bf16[2560,512]{1,0:T(8,128)(2,1)}, bf16...) custom-call(bf16[320,512]{1,0:T(8,128)(2,1)} %bitcast.8, ...), custom_call_target="tpu_custom_call" | custom-call | tf_op jit(solution)/shard_map/attention/pallas_call | solution.py:953
  125.1 74.3 %mlp.1 = (bf16[512,2560]{1,0:T(8,128)(2,1)}, f32[64,2560]{1,0:T(8,128)}, bf16[512,2560]{1,0:T(8,128)(2,1)}, f32[160,896]{1,0:T(8,128)}, bf16[2560,1792]{1,0:T(8,128)(2,1)}, /*index=5*/f32[8,2560]{1,0:T(8,128)}) custom-call(bf16[512,2560]{1,0:T(8,128)(2,1)} %get-tuple-element.54.refs_0_, bf16[2560,896]{1,0:T(8,128)(2,1)} %get-tuple-element.55.refs_1_, ...), custom_call_target="tpu_custom_call" | custom-call | tf_op jit(solution)/shard_map/mlp/pallas_call | solution.py:953
  199.4 94.0 %attention_back.1 = (bf16[8,64,320]{2,1,0:T(8,128)(2,1)}, bf16[8,64,320]{2,1,0:T(8,128)(2,1)}, f32[16,8,384]{2,1,0:T(8,128)}, f32[160,320]{1,0:T(8,128)}, f32[16...) custom-call(bf16[512,2560]{1,0:T(8,128)(2,1)} %get-tuple-element.61.refs_0, ...), custom_call_target="tpu_custom_call" | custom-call | tf_op jit(solution)/shard_map/attention_back/pallas_call | solution.py:953
  293.4 3.9 %closing.1 = (bf16[320,512]{1,0:T(8,128)(2,1)}, f32[320,512]{1,0:T(8,128)}, f32[320]{0:T(512)}, f32[320]{0:T(512)}, f32[160,320]{1,0:T(8,128)}, /*index=5*/f32[1...) custom-call(bf16[8,64,320]{2,1,0:T(8,128)(2,1)} %get-tuple-element.7, ...), custom_call_target="tpu_custom_call" | custom-call | tf_op jit(solution)/shard_map/closing/pallas_call | solution.py:1168

commit v6 on v5

--- a/solution.py
+++ b/solution.py
@@ -20,7 +20,7 @@
 PANEL = 896
 TILE = 128
 REACH = WINDOW + TILE
-CUT = 1024
+CUT = 768
 
 epsilon = 1e-05
 rope_base = 1000000.0
@@ -439,12 +439,11 @@
 def attention(net, ins, outs, scratch):
     x_own, cot_own, w_query, w_key, w_value, w_out, w_gate, w_up, w_down = ins[:9]
     gain_one, gain_two, freqs, lengths = ins[9:]
-    normed_far, w_qkv_far, w_out_far, cot, w_gu, w_d, normed_two = outs[:7]
-    queries, kv, lse, low, tables, attended, x_rows, mid, inverse, gains = outs[7:]
+    normed_far, w_qkv_far, w_out_far, cot, w_g, w_u, w_d, normed_two = outs[:8]
+    queries, kv, lse, low, tables, attended, x_rows, mid, inverse, gains = outs[8:]
     (
         shard_qkv,
         shard_out,
-        shard_gu,
         gains_own,
         gain_pieces,
         w_qkv,
@@ -472,12 +471,13 @@
     gains_own[1:2, :320] = gain_two[...].reshape(1, 320)
     panel = wide_gather(net, shard_qkv, w_qkv)
     step(panel, panel)
-    stream = narrow_gather(net, x_own, x_t, 256)
+    lanes = [pl.ds(0, 256), pl.ds(256, 256)]
+    streams = [
+        narrow_gather(net, x_own.at[:, half], x_t.at[:, half], 128) for half in lanes
+    ]
     sizes = narrow_share(net, gains_own, gain_pieces)
-    step(stream, sizes)
+    step(streams[0], sizes)
     shard_out[...] = jnp.concatenate([w_out[...], jnp.zeros((ROWS, 64), BF)], axis=1)
-    shard_gu[:, :PANEL] = w_gate[...]
-    shard_gu[:, PANEL:] = w_up[...]
 
     place = at.w * TOK + lax.broadcasted_iota(jnp.int32, (1, TOK), 1)
     begins, end = jnp.zeros((1, TOK), jnp.int32), 0
@@ -493,29 +493,37 @@
         one = first_key[:, tile * TILE : (tile + 1) * TILE]
         low[tile] = jnp.concatenate([one] * 4, axis=1)
 
-    step(panel, stream, panel, stream, panel)
+    step(streams[0], streams[1], panel, panel, streams[0], streams[1], panel)
     w_outs = wide_gather(net, shard_out, w_o)
-    gate_up = wide_gather(net, shard_gu, w_gu)
-    step(w_outs, w_outs, gate_up, panel, stream, stream, gate_up, w_outs, w_outs)
+    gate, up = wide_gather(net, w_gate, w_g), wide_gather(net, w_up, w_u)
+    step(w_outs, w_outs, gate, streams[0], streams[1], streams[0], panel, streams[1])
+    step(streams[1], gate, w_outs, w_outs, up)
     finish(panel, sizes)
     step(w_outs)
-    finish(stream)
+    finish(streams[0])
     for j in range(8):
         gains[:, pl.ds(j * 320, 320)] = gain_pieces[j, :, :320]
-    every(256, lambda rows: turned_over(x, x_t, rows))
-
-    @pl.loop(0, TOK // 16)
-    def _(i):
-        rows = pl.ds(pl.multiple_of(i * 16, 16), 16)
-        part = x[rows, :].astype(F32)
-        inv = lax.rsqrt(jnp.mean(part * part, axis=1, keepdims=True) + epsilon)
-        normed[rows, :] = (part * inv * gains[0:1, :]).astype(BF)
-
+
+    def norm_in(h):
+        every(256, lambda rows: turned_over(x.at[pl.ds(h * 256, 256)], x_t.at[:, lanes[h]], rows))
+
+        @pl.loop(h * 16, h * 16 + 16)
+        def _(i):
+            rows = pl.ds(pl.multiple_of(i * 16, 16), 16)
+            part = x[rows, :].astype(F32)
+            inv = lax.rsqrt(jnp.mean(part * part, axis=1, keepdims=True) + epsilon)
+            normed[rows, :] = (part * inv * gains[0:1, :]).astype(BF)
+
+    norm_in(0)
+    finish(streams[1])
+    cots = narrow_gather(net, cot_own, cot, 256)
+    down = wide_gather(net, w_down, w_d)
+    step(cots, gate, down)
+    norm_in(1)
     for h in range(2):
         x_rows[pl.ds(h * 32, 32), :] = x[own_rows(at, h), :].astype(F32)
-    for k in range(2):
-        part = pl.ds(k * 256, 256)
-        qkv[part, :] = dot(normed[...], w_qkv[:, part]).T
+    part = pl.ds(256, 256)
+    qkv[part, :] = dot(normed[...], w_qkv[:, part]).T
     zeros = jnp.zeros((48, TOK), F32)
 
     def turned(at_row):
@@ -528,14 +536,14 @@
     arriving = [
         net.send(kv.at[mine], kv.at[pl.ds((2 - k) * TOK, TOK)], later[k - 1]) for k in (1, 2)
     ]
-    cots = narrow_gather(net, cot_own, cot, 256)
-    down = wide_gather(net, w_down, w_d)
-    step(cots, down)
+    step(up, cots, down)
+    part = pl.ds(0, 256)
+    qkv[part, :] = dot(normed[...], w_qkv[:, part]).T
     for head in range(4):
         one = turned(head * HEAD).astype(BF)
         for tile in range(4):
             queries[tile, :, pl.ds(head * TILE, TILE)] = one[:, tile * TILE : (tile + 1) * TILE]
-    step(w_outs, gate_up)
+    step(w_outs, gate, up)
     for copy in arriving:
         copy.wait_recv()
     values_t[...] = kv[:, 128:].T
@@ -578,25 +586,25 @@
     pl.loop(0, 2)(one_tile)
     finish(w_outs)
     early = out_part(0)
-    step(early, gate_up, cots)
+    step(early, cots, gate, up, cots)
     pl.loop(2, 4)(one_tile)
     step(early, early)
     late = out_part(1)
-    step(early, late, early, down, cots, late)
+    step(early, late, early, down, late)
     net.keep(w_o, w_out_far)
     net.keep(normed, normed_far)
     step(late)
     net.keep(w_qkv, w_qkv_far)
     finish(early)
     ahead = norm_part(0)
-    step(ahead, late, gate_up, ahead, late, down, ahead)
-    step(cots, ahead, gate_up, ahead)
+    step(ahead, late, up, gate, ahead, late, down, ahead)
+    step(cots, ahead, up, ahead, down)
     finish(late)
     behind = norm_part(1)
-    step(behind, down, cots, behind, down, behind)
+    step(behind, down, behind, behind, down)
     finish(ahead)
-    step(behind, down, behind)
-    finish(behind, gate_up, cots, down)
+    step(behind, behind)
+    finish(behind, gate, up, cots, down)
     net.run([])
 
 
@@ -609,12 +617,13 @@
 
 
 def mlp(net, ins, outs, scratch):
-    normed_far, d_far, gu_far, cot_far, mid, inverse, gains = ins
+    normed_far, d_far, g_far, u_far, cot_far, mid, inverse, gains = ins
     grad_mid_far, grad_mid, down_far, grad_gate, du_far, gain_part = outs
     w_gu, w_d, normed, cot_t, cot, gu, grad_hidden, hidden, grad_pre, src = scratch[:10]
-    down_part, slots, total, core, turned, last, low, grad_mid_full = scratch[10:]
+    down_part, slots, total, core, turned, last, low = scratch[10:17]
     at = net.at
-    sources, rooms = (normed_far, gu_far, cot_far, d_far), (normed, w_gu, cot_t, w_d)
+    sources = (normed_far, g_far, u_far, cot_far, d_far)
+    rooms = (normed, w_gu.at[:, pl.ds(0, PANEL)], w_gu.at[:, pl.ds(PANEL, PANEL)], cot_t, w_d)
     loads = [net.keep(a, b) for a, b in zip(sources, rooms)]
     net.barrier(at.narrow_peers() + at.wide_peers(), 12)
     tokens = [pl.ds(0, 256), pl.ds(256, 256)]
@@ -660,11 +669,11 @@
         mine = cot[own_rows(at, h), :].astype(F32) + through
         grad_mid[own[h], :] = mine
         low[own[h], :] = mine.astype(BF)
-        return narrow_gather(net, low.at[own[h]], grad_mid_full.at[tokens[h]], CUT)
-
-    net.settle(*loads[:2])
+        return narrow_gather(net, low.at[own[h]], grad_mid_far.at[tokens[h]], CUT)
+
+    net.settle(*loads[:3])
     gate_up(0)
-    net.settle(*loads[2:])
+    net.settle(*loads[3:])
     every(256, lambda rows: turned_over(cot, cot_t, rows))
     back_down(0)
     back_hidden(0)
@@ -722,7 +731,6 @@
     step(wide)
     gain_terms(gain_part, src, normed, gains, 1)
     finish(back[1])
-    net.keep(grad_mid_full, grad_mid_far)
     finish(wide)
     net.run([])
 
@@ -845,7 +853,7 @@
     sums = [back_normed(0)]
     step(sums[0], wide_out)
     sums.append(back_normed(1))
-    step(sums[0], sums[1], sums[0])
+    step(sums[0], sums[1], sums[0], wide_du)
     net.settle(loads[1])
 
     def grad_qkv_rows(rows):
@@ -866,9 +874,9 @@
     me = at.n
     copies = [net.send(parts.at[p[1]], narrow_parts.at[me], p) for p in at.narrow_peers()]
     narrow_parts[me] = parts[me]
-    step(sums[1], sums[0], wide_qkv, wide_out, sums[1], wide_du, wide_qkv)
+    step(sums[1], sums[0], wide_qkv, sums[1], wide_out, wide_qkv)
     finish(sums[0])
-    step(sums[1])
+    step(sums[1], wide_qkv)
     for copy in copies:
         copy.wait_recv()
     sum_parts = narrow_parts[0]
@@ -878,7 +886,7 @@
     copies = [
         net.send(wide_parts.at[0], wide_parts.at[k + 1], p) for k, p in enumerate(everyone)
     ]
-    step(wide_out, wide_qkv)
+    step(wide_out, wide_qkv, wide_du)
     finish(sums[1])
     stream, grad = x_rows[...], total_two[...]
     inv = lax.rsqrt(jnp.mean(stream * stream, axis=1, keepdims=True) + epsilon)
@@ -1016,7 +1024,8 @@
         w_qkv,
         w_o,
         cot,
-        w_gu,
+        w_g,
+        w_u,
         w_d,
         normed_two,
         queries,
@@ -1041,7 +1050,8 @@
             far(D, 512),
             far(D, 384),
             far(D, TOK),
-            far(D, 2 * PANEL),
+            far(D, PANEL),
+            far(D, PANEL),
             far(D, PANEL),
             far(TOK, D),
             held(4, TILE, 4 * TILE),
@@ -1058,7 +1068,6 @@
         [
             room(ROWS, 512),
             room(ROWS, 384),
-            room(ROWS, 2 * PANEL),
             room(8, 384, dtype=F32),
             room(8, 8, 384, dtype=F32),
             room(D, 512),
@@ -1078,7 +1087,7 @@
         "mlp",
         2,
         mlp,
-        remote(normed_two, w_d, w_gu, cot) + local(mid, inverse, gains),
+        remote(normed_two, w_d, w_g, w_u, cot) + local(mid, inverse, gains),
         [
             far(TOK, D),
             held(OWN, D, dtype=F32),
@@ -1103,7 +1112,6 @@
             own,
             *wide_sum_scratch(PANEL),
             room(OWN, D),
-            room(TOK, D),
         ],
     )
     output_rows, grad_rows, gain_parts, grad_out, grad_query, grad_key, grad_value, grad_d, grad_up = exchange(

time: 300 us -> 291 us (0.970)
  Pallas kernels: 297 us -> 287 us
    pallas_call x3, Pallas kernels: 293 us -> 284 us  [exchange(): pl.pallas_call(kernel, out_shape=[jax.ShapeDtypeStruct(shape, dtype) for...]
where the time goes in v6:
time: 291 us; the launch traced here: 288 us
  Pallas kernels  287 us (99%)
    pallas_call x3, Pallas kernels, exchange(): pl.pallas_call(kernel, out_shape=[jax.ShapeDtypeStruct(shape, dtype) for...  284 us

profile of v6, /device:TPU:1, one launch (start us, length us, event | category | flops | bytes accessed | tf_op | source)
XLA Modules:
  0.0 288.1 jit_solution(5971002190517462328)
XLA Ops:
  0.6 119.2 %attention.1 = (bf16[512,2560]{1,0:T(8,128)(2,1)}, bf16[2560,512]{1,0:T(8,128)(2,1)}, bf16[2560,384]{1,0:T(8,128)(2,1)}, bf16[2560,512]{1,0:T(8,128)(2,1)}, bf16...) custom-call(bf16[320,512]{1,0:T(8,128)(2,1)} %bitcast.8, ...), custom_call_target="tpu_custom_call" | custom-call | tf_op jit(solution)/shard_map/attention/pallas_call | solution.py:961
  119.8 71.7 %mlp.1 = (bf16[512,2560]{1,0:T(8,128)(2,1)}, f32[64,2560]{1,0:T(8,128)}, bf16[512,2560]{1,0:T(8,128)(2,1)}, f32[160,896]{1,0:T(8,128)}, bf16[2560,1792]{1,0:T(8,128)(2,1)}, /*index=5*/f32[8,2560]{1,0:T(8,128)}) custom-call(bf16[512,2560]{1,0:T(8,128)(2,1)} %get-tuple-element.55.refs_0_, bf16[2560,896]{1,0:T(8,128)(2,1)} %get-tuple-element.56.refs_1_, ...), custom_call_target="tpu_custom_call" | custom-call | tf_op jit(solution)/shard_map/mlp/pallas_call | solution.py:961
  191.5 92.7 %attention_back.1 = (bf16[8,64,320]{2,1,0:T(8,128)(2,1)}, bf16[8,64,320]{2,1,0:T(8,128)(2,1)}, f32[16,8,384]{2,1,0:T(8,128)}, f32[160,320]{1,0:T(8,128)}, f32[16...) custom-call(bf16[512,2560]{1,0:T(8,128)(2,1)} %get-tuple-element.63.refs_0, ...), custom_call_target="tpu_custom_call" | custom-call | tf_op jit(solution)/shard_map/attention_back/pallas_call | solution.py:961
  284.2 3.9 %closing.1 = (bf16[320,512]{1,0:T(8,128)(2,1)}, f32[320,512]{1,0:T(8,128)}, f32[320]{0:T(512)}, f32[320]{0:T(512)}, f32[160,320]{1,0:T(8,128)}, /*index=5*/f32[1...) custom-call(bf16[8,64,320]{2,1,0:T(8,128)(2,1)} %get-tuple-element.7, ...), custom_call_target="tpu_custom_call" | custom-call | tf_op jit(solution)/shard_map/closing/pallas_call | solution.py:1176

commit v7 on v6

--- a/solution.py
+++ b/solution.py
@@ -516,7 +516,7 @@
 
     norm_in(0)
     finish(streams[1])
-    cots = narrow_gather(net, cot_own, cot, 256)
+    cots = narrow_gather(net, cot_own, cot, 128)
     down = wide_gather(net, w_down, w_d)
     step(cots, gate, down)
     norm_in(1)

time: 291 us -> 291 us (level)
  no operation moved by 1% of the time
where the time goes in v7:
time: 291 us; the launch traced here: 289 us
  Pallas kernels  288 us (99%)
    pallas_call x3, Pallas kernels, exchange(): pl.pallas_call(kernel, out_shape=[jax.ShapeDtypeStruct(shape, dtype) for...  284 us

profile of v7, /device:TPU:1, one launch (start us, length us, event | category | flops | bytes accessed | tf_op | source)
XLA Modules:
  0.0 288.9 jit_solution(3160450203283746590)
XLA Ops:
  0.6 119.2 %attention.1 = (bf16[512,2560]{1,0:T(8,128)(2,1)}, bf16[2560,512]{1,0:T(8,128)(2,1)}, bf16[2560,384]{1,0:T(8,128)(2,1)}, bf16[2560,512]{1,0:T(8,128)(2,1)}, bf16...) custom-call(bf16[320,512]{1,0:T(8,128)(2,1)} %bitcast.8, ...), custom_call_target="tpu_custom_call" | custom-call | tf_op jit(solution)/shard_map/attention/pallas_call | solution.py:961
  119.8 71.5 %mlp.1 = (bf16[512,2560]{1,0:T(8,128)(2,1)}, f32[64,2560]{1,0:T(8,128)}, bf16[512,2560]{1,0:T(8,128)(2,1)}, f32[160,896]{1,0:T(8,128)}, bf16[2560,1792]{1,0:T(8,128)(2,1)}, /*index=5*/f32[8,2560]{1,0:T(8,128)}) custom-call(bf16[512,2560]{1,0:T(8,128)(2,1)} %get-tuple-element.55.refs_0_, bf16[2560,896]{1,0:T(8,128)(2,1)} %get-tuple-element.56.refs_1_, ...), custom_call_target="tpu_custom_call" | custom-call | tf_op jit(solution)/shard_map/mlp/pallas_call | solution.py:961
  191.3 93.6 %attention_back.1 = (bf16[8,64,320]{2,1,0:T(8,128)(2,1)}, bf16[8,64,320]{2,1,0:T(8,128)(2,1)}, f32[16,8,384]{2,1,0:T(8,128)}, f32[160,320]{1,0:T(8,128)}, f32[16...) custom-call(bf16[512,2560]{1,0:T(8,128)(2,1)} %get-tuple-element.63.refs_0, ...), custom_call_target="tpu_custom_call" | custom-call | tf_op jit(solution)/shard_map/attention_back/pallas_call | solution.py:961
  285.0 3.9 %closing.1 = (bf16[320,512]{1,0:T(8,128)(2,1)}, f32[320,512]{1,0:T(8,128)}, f32[320]{0:T(512)}, f32[320]{0:T(512)}, f32[160,320]{1,0:T(8,128)}, /*index=5*/f32[1...) custom-call(bf16[8,64,320]{2,1,0:T(8,128)(2,1)} %get-tuple-element.7, ...), custom_call_target="tpu_custom_call" | custom-call | tf_op jit(solution)/shard_map/closing/pallas_call | solution.py:1176
